TPU v7x, 256 devices: a whole 4x4x8 slice. The times are simulated.
256 devices in a mesh: wave: 4 (over x), row: 8 (over z_lo, core), col: 8 (over z_hi, y).
Axes of the slice: x: 4, y: 4, z: 8 (z_hi: 2, z_lo: 4; z = z_hi * 4 + z_lo), core: 2. Of those that a mesh axis runs over, the one named last changes fastest.
Arguments:
- wavefield: float32 [2, 32, 512, 1024], P(None, 'wave', 'row', 'col'), may hold values from -6 to 6
- wavelength: float32 [32], P('wave'), may hold values from 0.45 to 0.65
- weight: float32 [32], P('wave'), may hold values from 0.25 to 1
- spectrum: float32 [2, 512, 1024], P(None, 'col', 'row'), may hold values from -5 to 5
- measured: float32 [512, 1024], P('row', 'col'), may hold values from -6 to 6
Outputs:
- field_grad: float32 [2, 32, 512, 1024], P(None, 'wave', 'row', 'col')
- residual: float32 [512, 1024], P('row', 'col')
All inputs are finite; a program needn't handle non-finite values.
Results may differ from a plain program's by a relative error of at most 0.00018.
Values sent between devices are 32-bit elements; how exact they have to be, the bound alone decides.
No kernel may reach another device: no remote copies, remote signals or barrier semaphores. Data moves between devices by JAX's collectives and lax.ppermute only.
A program may use at most 64 MiB of HBM per device.

v0:
```python
import jax
import jax.numpy as jnp
from jax import lax
from jax.sharding import PartitionSpec as P

WAVES = 32
HALO = 64


HIGHEST = lax.Precision.HIGHEST
TWO_PI = 6.283185307179586


def extended_2(cells, sides, width):
    for axis, dim in sides:
        count = lax.axis_size(axis)
        ends = count - 1
        head = lax.slice_in_dim(cells, 0, width, axis=dim)
        tail = lax.slice_in_dim(cells, cells.shape[dim] - width, cells.shape[dim], axis=dim)
        cells = jnp.concatenate(
            [
                lax.ppermute(tail, axis, [(i, (i + 1) % count) for i in range(ends)]),
                cells,
                lax.ppermute(head, axis, [((i + 1) % count, i) for i in range(ends)]),
            ],
            axis=dim,
        )
    return cells


def tap_values(offset, wave_len):
    spread_d = jnp.arange(-HALO, HALO + 1).astype(jnp.float32)
    profile = jnp.exp(-2.0 * (spread_d / HALO) ** 2)
    norm_scale = 1.0 / jnp.sqrt(jnp.sum(profile))
    amplitude = jnp.exp(-((offset / HALO) ** 2)) * norm_scale
    phase = offset * offset / (2.0 * wave_len * HALO)
    inside = jnp.abs(offset) <= HALO
    return (
        jnp.where(inside, amplitude * jnp.cos(phase), 0.0),
        jnp.where(inside, amplitude * jnp.sin(phase), 0.0),
    )


def band_tables(length, wave_len, conj_sign):
    row_index = jnp.arange(length + 2 * HALO)[:, None]
    col_index = jnp.arange(length)[None, :]
    offset = (row_index - col_index - HALO).astype(jnp.float32)
    real_part, imag_part = tap_values(offset[None], wave_len[:, None, None])
    return (real_part, conj_sign * imag_part)


def column_table(length, wave_len, conj_sign):
    real_part, imag_part = band_tables(length, wave_len, conj_sign)
    top_half = jnp.concatenate([real_part, imag_part], axis=2)
    low_half = jnp.concatenate([-imag_part, real_part], axis=2)
    return jnp.concatenate([top_half, low_half], axis=1)


def row_table(length, wave_len, conj_sign):
    real_part, imag_part = band_tables(length, wave_len, conj_sign)
    return jnp.concatenate([real_part, imag_part], axis=2)


def column_pass(extended, table):
    stacked = jnp.concatenate([extended[0], extended[1]], axis=-1)
    return jnp.einsum(
        "ltE,lEX->ltX", stacked, table, precision=HIGHEST, preferred_element_type=jnp.float32
    )


def row_pass(widened, table, rows_tile, cols_tile):
    mixture = jnp.einsum(
        "lEt,lEX->ltX", table, widened, precision=HIGHEST, preferred_element_type=jnp.float32
    )
    top_half = mixture[:, :rows_tile]
    low_half = mixture[:, rows_tile:]
    real_out = top_half[..., :cols_tile] - low_half[..., cols_tile:]
    imag_out = top_half[..., cols_tile:] + low_half[..., :cols_tile]
    return jnp.stack([real_out, imag_out])


def propagate(field_pair, col_tab, row_tab):
    rows_tile = field_pair.shape[2]
    cols_tile = field_pair.shape[3]
    extended = extended_2(field_pair, (("row", 2), ("col", 3)), HALO)
    widened = column_pass(extended, col_tab)
    return row_pass(widened, row_tab, rows_tile, cols_tile)


def phase_table(left_ids, right_ids, modulus):
    product = left_ids[:, None] * right_ids[None, :] % modulus
    angles = TWO_PI * product.astype(jnp.float32) / modulus
    return (jnp.cos(angles), jnp.sin(angles))


def complex_left(cos_part, sin_part, operand, half_width):
    height = cos_part.shape[0]
    mixture = jnp.dot(
        jnp.concatenate([cos_part, sin_part], axis=0),
        operand,
        precision=HIGHEST,
        preferred_element_type=jnp.float32,
    )
    top_half = mixture[:height]
    low_half = mixture[height:]
    real_out = top_half[:, :half_width] - low_half[:, half_width:]
    imag_out = top_half[:, half_width:] + low_half[:, :half_width]
    return jnp.concatenate([real_out, imag_out], axis=1)


def filter_product(freq_rows, spec_re, spec_im, half_width):
    freq_re = freq_rows[:, :half_width]
    freq_im = freq_rows[:, half_width:]
    return jnp.concatenate(
        [freq_re * spec_re - freq_im * spec_im, freq_re * spec_im + freq_im * spec_re], axis=1
    )


def blur(image_in, spectrum_pair, conj_sign, forward_dft, inverse_dft):
    row_count = lax.axis_size("row")
    col_count = lax.axis_size("col")
    wave_count = lax.axis_size("wave")
    share = lax.axis_index("wave")
    groups = wave_count * col_count
    place = share * col_count + lax.axis_index("col")
    tile_rows = image_in.shape[0] * wave_count
    row_slab = lax.all_to_all(image_in, "col", split_axis=0, concat_axis=1, tiled=True)
    slab_rows = row_slab.shape[0]
    full_cols = row_slab.shape[1]
    spectra = jnp.dot(row_slab, forward_dft, precision=HIGHEST, preferred_element_type=jnp.float32)
    halves = (
        lax.all_to_all(spectra[:, :full_cols], "row", split_axis=1, concat_axis=0, tiled=True),
        lax.all_to_all(spectra[:, full_cols:], "row", split_axis=1, concat_axis=0, tiled=True),
    )
    half_width = halves[0].shape[1]
    full_rows = tile_rows * row_count
    group_rows = row_count * slab_rows
    local_rows = jnp.arange(group_rows)
    source = local_rows // slab_rows * tile_rows + place * slab_rows + local_rows % slab_rows
    freq_count = full_rows // groups
    band = full_rows // col_count

    def order(ids):
        owner = ids // freq_count
        return owner % col_count * band + owner // col_count * freq_count + ids % freq_count

    spec_re = lax.dynamic_slice_in_dim(spectrum_pair[0], share * freq_count, freq_count, 0)
    spec_im = conj_sign * lax.dynamic_slice_in_dim(
        spectrum_pair[1], share * freq_count, freq_count, 0
    )
    freq_input = jnp.concatenate(halves, axis=1)
    frequencies = order(jnp.arange(freq_count * lax.axis_size(("wave", "col"))))
    cos_part, sin_part = phase_table(frequencies, source, full_rows)
    freq_rows = lax.psum_scatter(
        complex_left(cos_part, -sin_part, freq_input, half_width),
        ("wave", "col"),
        scatter_dimension=0,
        tiled=True,
    )
    filtered = filter_product(freq_rows, spec_re, spec_im, half_width)
    portion = lax.all_gather(filtered, ("wave", "col"), axis=0, tiled=True)
    frequencies = order(jnp.arange(portion.shape[0]))
    cos_part, sin_part = phase_table(source, frequencies, full_rows)
    restored = complex_left(cos_part / full_rows, sin_part / full_rows, portion, half_width)
    restored_re = restored[:, :half_width]
    restored_im = restored[:, half_width:]
    rows_back = (
        lax.all_to_all(restored_re, "row", split_axis=0, concat_axis=1, tiled=True),
        lax.all_to_all(restored_im, "row", split_axis=0, concat_axis=1, tiled=True),
    )
    spatial = jnp.dot(
        jnp.concatenate(rows_back, axis=1),
        inverse_dft,
        precision=HIGHEST,
        preferred_element_type=jnp.float32,
    )
    return lax.all_to_all(spatial, "col", split_axis=1, concat_axis=0, tiled=True)


def shards(wavefield, wavelength, weight, spectrum, measured):
    rows_tile = wavefield.shape[2]
    cols_tile = wavefield.shape[3]
    forward_field = propagate(
        wavefield, column_table(cols_tile, wavelength, 1.0), row_table(rows_tile, wavelength, 1.0)
    )
    partial_intensity = (
        jnp.sum(
            weight[:, None, None]
            * (forward_field[0] * forward_field[0] + forward_field[1] * forward_field[1]),
            axis=0,
        )
        / WAVES
    )
    full_cols = cols_tile * lax.axis_size("col")
    frequencies = jnp.arange(full_cols)
    col_cos, col_sin = phase_table(frequencies, frequencies, full_cols)
    forward_dft = jnp.concatenate([col_cos, -col_sin], axis=1)
    inverse_dft = jnp.concatenate([col_cos, -col_sin], axis=0) / full_cols
    spectrum_pair = (spectrum[0], spectrum[1])
    share_rows = rows_tile // lax.axis_size("wave")
    intensity = lax.psum_scatter(partial_intensity, "wave", scatter_dimension=0, tiled=True)
    blurred = blur(intensity, spectrum_pair, 1.0, forward_dft, inverse_dft)
    measured_share = lax.dynamic_slice_in_dim(
        measured, lax.axis_index("wave") * share_rows, share_rows, 0
    )
    residual_share = blurred - measured_share
    pulled_share = blur(residual_share, spectrum_pair, -1.0, forward_dft, inverse_dft)
    residual, pulled = (
        lax.all_gather(residual_share, "wave", axis=0, tiled=True),
        lax.all_gather(pulled_share, "wave", axis=0, tiled=True),
    )
    source = 2.0 * weight[None, :, None, None] * pulled[None, None] * forward_field
    field_grad = propagate(
        source, column_table(cols_tile, wavelength, -1.0), row_table(rows_tile, wavelength, -1.0)
    )
    return (field_grad, residual)


def solution(mesh):
    placed = (
        P(None, "wave", "row", "col"),
        P("wave"),
        P("wave"),
        P(None, "col", "row"),
        P("row", "col"),
    )
    return jax.shard_map(
        shards,
        mesh=mesh,
        in_specs=placed,
        out_specs=(P(None, "wave", "row", "col"), P("row", "col")),
        check_vma=False,
    )
```

profile of v0, /device:TPU:193, one launch (start us, length us, event | category | flops | bytes accessed | tf_op | source)
XLA Modules:
  0.0 1043.1 jit_solution(14002006963505910494)
XLA Ops:
  44.3 25.7 %collective-permute-done.3 = f32[2,8,192,64]{2,3,1,0:T(8,128)} collective-permute-done((f32[2,8,192,64]{2,3,1,0:T(8,128)}, f32[2,8,192,64]{2,3,1,0:T(8,128)}, u32[]{:S(2)}, u32[]{:S(2)}) %collective-permute-start.3) | collective-permute-done | bytes 786464 | tf_op jit(solution)/shard_map/ppermute | solution.py:24
  72.9 9.0 collective-permute-done.2
  96.1 17.7 %sine_negate_fusion = (f32[1024,1024]{1,0:T(8,128)}, f32[1024,1024]{1,0:T(8,128)}) fusion(), kind=kLoop, calls=%fused_computation.26 | loop fusion | flops 15728640 | bytes 8388608 | tf_op jit(solution)/shard_map/neg | solution.py:197
  115.8 9.6 all-to-all-start
  136.5 9.1 all-to-all-start.2
  159.8 182.1 %reduce-scatter.10.cloned.1.call-done = f32[16,256]{1,0:T(8,128)} async-done(((f32[512,256]{1,0:T(8,128)}), f32[16,256]{1,0:T(8,128)}) %reduce-scatter.10.cloned.1.call-update) | async-done | bytes 16400 | tf_op jit(solution)/shard_map/reduce_scatter | solution.py:154
  342.6 97.5 %all_gather.12 = f32[512,256]{1,0:T(8,128)S(1)} all-gather(f32[16,256]{1,0:T(8,128)S(1)} %pad_maximum_fusion.21), channel_id=1, replica_groups=mesh['wave'=4,'row'=8,'col'=8] {'wave','col'}, dimensions={0}, use_global_device_ids=true | all-gather | bytes 540672 | tf_op jit(solution)/shard_map/all_gather | solution.py:161
  440.5 47.4 %all_to_all.228 = f32[8,2,128]{2,1,0:T(2,128)S(1)} all-to-all(f32[8,2,128]{2,1,0:T(2,128)S(1)} %bitcast.118), channel_id=1, replica_groups=mesh['wave'=4,'row'=8,'col'=8] {'row'}, dimensions={0} | all-to-all | bytes 16384 | tf_op jit(solution)/shard_map/all_to_all | solution.py:169
  487.9 8.0 all_to_all.229
  503.7 22.4 %all_to_all.230 = f32[2,8,128]{2,0,1:T(2,128)S(1)} all-to-all(f32[2,8,128]{2,0,1:T(2,128)S(1)} %fusion.29), channel_id=1, replica_groups=mesh['wave'=4,'row'=8,'col'=8] {'col'}, dimensions={1} | all-to-all | bytes 16384 | tf_op jit(solution)/shard_map/all_to_all | solution.py:177
  526.8 11.5 %all_to_all.231 = f32[8,2,128]{2,1,0:T(2,128)S(1)} all-to-all(f32[8,2,128]{2,1,0:T(2,128)S(1)} %bitcast.105), channel_id=1, replica_groups=mesh['wave'=4,'row'=8,'col'=8] {'col'}, dimensions={0} | all-to-all | bytes 16384 | tf_op jit(solution)/shard_map/all_to_all | solution.py:127
  542.3 10.0 all_to_all.232
  552.3 8.0 all_to_all.233
  562.4 181.0 %reduce-scatter.12.cloned.1.call-done = f32[16,256]{1,0:T(8,128)} async-done(((f32[512,256]{1,0:T(8,128)}), f32[16,256]{1,0:T(8,128)}) %reduce-scatter.12.cloned.1.call-update) | async-done | bytes 16400 | tf_op jit(solution)/shard_map/reduce_scatter | solution.py:154
  744.1 97.8 %all_gather.13 = f32[512,256]{1,0:T(8,128)S(1)} all-gather(f32[16,256]{1,0:T(8,128)S(1)} %pad_maximum_fusion.22), channel_id=1, replica_groups=mesh['wave'=4,'row'=8,'col'=8] {'wave','col'}, dimensions={0}, use_global_device_ids=true | all-gather | bytes 540672 | tf_op jit(solution)/shard_map/all_gather | solution.py:161
  842.3 47.1 %all_to_all.234 = f32[8,2,128]{2,1,0:T(2,128)S(1)} all-to-all(f32[8,2,128]{2,1,0:T(2,128)S(1)} %bitcast.119), channel_id=1, replica_groups=mesh['wave'=4,'row'=8,'col'=8] {'row'}, dimensions={0} | all-to-all | bytes 16384 | tf_op jit(solution)/shard_map/all_to_all | solution.py:169
  889.5 8.0 all_to_all.235
  897.4 8.3 fusion.30
  905.7 19.2 %all-to-all-start.11 = ((f32[2,8,128]{2,0,1:T(2,128)}), f32[2,8,128]{2,0,1:T(2,128)S(1)}, u32[]{:S(2)}, u32[]{:S(2)}) async-start(f32[2,8,128]{2,0,1:T(2,128)} %fusion.30), calls=%async_computation.12 | async-start | bytes 16384 | tf_op jit(solution)/shard_map/all_to_all | solution.py:177
  929.1 9.0 all_gather.14
  958.4 7.8 collective-permute-start.7
  969.7 9.2 all_gather.15
  978.9 30.7 %collective-permute-done.7 = f32[2,8,192,64]{2,3,1,0:T(8,128)} collective-permute-done((f32[2,8,192,64]{2,3,1,0:T(8,128)}, f32[2,8,192,64]{2,3,1,0:T(8,128)}, u32[]{:S(2)}, u32[]{:S(2)}) %collective-permute-start.7) | collective-permute-done | bytes 786464 | tf_op jit(solution)/shard_map/ppermute | solution.py:24
  1011.4 10.5 %collective-permute-done.6 = f32[2,8,192,64]{2,3,1,0:T(8,128)} collective-permute-done((f32[2,8,192,64]{2,3,1,0:T(8,128)}, f32[2,8,192,64]{2,3,1,0:T(8,128)}, u32[]{:S(2)}, u32[]{:S(2)}) %collective-permute-start.6) | collective-permute-done | bytes 786464 | tf_op jit(solution)/shard_map/ppermute | solution.py:22
  (112 shorter events, 141.6 us)
Async XLA Ops:
  7.2 108.6 %reduce-scatter.8.cloned.1.call-start = ((), (), s32[]{:S(2)}) async-start(), calls=%async_computation.15 | async-start | bytes 40960 | tf_op jit(solution)/shard_map/reduce_scatter | solution.py:201
  7.2 9.6 collective-permute-start
  10.4 10.7 %collective-permute-start.1 = (f32[2,8,64,128]{3,2,1,0:T(8,128)}, f32[2,8,64,128]{3,2,1,0:T(8,128)S(1)}, u32[]{:S(2)}, u32[]{:S(2)}) collective-permute-start(f32[2,8,64,128]{3,2,1,0:T(8,128)} %param.5), channel_id=1, source_target_pairs={{8,0},{16,8},{24,16},{32,24},{40,32},{48,40},{56,48},{9,1},{17,9},... | collective-permute-start | bytes 1572872 | tf_op jit(solution)/shard_map/ppermute | solution.py:24
  25.9 44.1 %collective-permute-start.3 = (f32[2,8,192,64]{2,3,1,0:T(8,128)}, f32[2,8,192,64]{2,3,1,0:T(8,128)}, u32[]{:S(2)}, u32[]{:S(2)}) collective-permute-start(f32[2,8,192,64]{2,3,1,0:T(8,128)} %copy.39), channel_id=1, source_target_pairs={{1,0},{2,1},{3,2},{4,3},{5,4},{6,5},{7,6},{9,8},{10,9},{11,10},{12... | collective-permute-start | bytes 2359304 | tf_op jit(solution)/shard_map/ppermute | solution.py:24
  33.1 48.9 %collective-permute-start.2 = (f32[2,8,192,64]{2,3,1,0:T(8,128)}, f32[2,8,192,64]{2,3,1,0:T(8,128)}, u32[]{:S(2)}, u32[]{:S(2)}) collective-permute-start(f32[2,8,192,64]{2,3,1,0:T(8,128)} %copy.38), channel_id=1, source_target_pairs={{0,1},{1,2},{2,3},{3,4},{4,5},{5,6},{6,7},{8,9},{9,10},{10,11},{11... | collective-permute-start | bytes 2359304 | tf_op jit(solution)/shard_map/ppermute | solution.py:22
  88.0 1.5 copy-start.8
  88.1 1.8 copy-start.9
  93.2 2.2 copy-start.11
  115.8 13.7 %all-to-all-start = ((f32[8,2,128]{2,1,0:T(2,128)}), f32[8,2,128]{2,1,0:T(2,128)S(1)}, u32[]{:S(2)}, u32[]{:S(2)}) async-start(f32[8,2,128]{2,1,0:T(2,128)} %bitcast.120), calls=%async_computation.1 | async-start | bytes 16384 | tf_op jit(solution)/shard_map/all_to_all | solution.py:127
  135.9 23.9 %copy-start.10 = (f32[2,64,128]{2,1,0:T(8,128)S(1)}, f32[2,64,128]{2,1,0:T(8,128)}, u32[]{:S(2)}) copy-start(f32[2,64,128]{2,1,0:T(8,128)} %param.8) | copy-start | bytes 196612
  136.5 12.0 %all-to-all-start.2 = ((f32[2,8,128]{2,0,1:T(2,128)}), f32[2,8,128]{2,0,1:T(2,128)S(1)}, u32[]{:S(2)}, u32[]{:S(2)}) async-start(f32[2,8,128]{2,0,1:T(2,128)} %get-tuple-element.40), calls=%async_computation.3 | async-start | bytes 16384 | tf_op jit(solution)/shard_map/all_to_all | solution.py:133
  148.5 8.9 all-to-all-start.1
  154.5 187.4 %reduce-scatter.10.cloned.1.call-start = ((), (), s32[]{:S(2)}) async-start(), calls=%async_computation.16 | async-start | bytes 540672 | tf_op jit(solution)/shard_map/reduce_scatter | solution.py:154
  159.5 583.9 %reduce-scatter.12.cloned.1.call-start = ((), (), s32[]{:S(2)}) async-start(), calls=%async_computation.17 | async-start | bytes 540672 | tf_op jit(solution)/shard_map/reduce_scatter | solution.py:154
  495.9 42.4 %copy-start = (f32[1024,1024]{1,0:T(8,128)S(1)}, f32[1024,1024]{1,0:T(8,128)}, u32[]{:S(2)}) copy-start(f32[1024,1024]{1,0:T(8,128)} %get-tuple-element.49) | copy-start | bytes 12582916
  495.9 42.4 %copy-start.1 = (f32[1024,1024]{1,0:T(8,128)S(1)}, f32[1024,1024]{1,0:T(8,128)}, u32[]{:S(2)}) copy-start(f32[1024,1024]{1,0:T(8,128)} %get-tuple-element.50) | copy-start | bytes 12582916
  905.7 23.3 %all-to-all-start.11 = ((f32[2,8,128]{2,0,1:T(2,128)}), f32[2,8,128]{2,0,1:T(2,128)S(1)}, u32[]{:S(2)}, u32[]{:S(2)}) async-start(f32[2,8,128]{2,0,1:T(2,128)} %fusion.30), calls=%async_computation.12 | async-start | bytes 16384 | tf_op jit(solution)/shard_map/all_to_all | solution.py:177
  938.2 13.7 %collective-permute-start.5 = (f32[2,8,64,128]{3,2,1,0:T(8,128)S(1)}, f32[2,8,64,128]{3,2,1,0:T(8,128)S(1)}, u32[]{:S(2)}, u32[]{:S(2)}) collective-permute-start(f32[2,8,64,128]{3,2,1,0:T(8,128)S(1)} %maximum_multiply_fusion.7), channel_id=1, source_target_pairs={{8,0},{16,8},{24,16},{32,24},{40,32},{48,40},{56,48},{9,1},{17,9},... | collective-permute-start | bytes 1572872 | tf_op jit(solution)/shard_map/ppermute | solution.py:24
  944.6 8.2 collective-permute-start.4
  958.4 51.2 %collective-permute-start.7 = (f32[2,8,192,64]{2,3,1,0:T(8,128)}, f32[2,8,192,64]{2,3,1,0:T(8,128)}, u32[]{:S(2)}, u32[]{:S(2)}) collective-permute-start(f32[2,8,192,64]{2,3,1,0:T(8,128)} %copy.53), channel_id=1, source_target_pairs={{1,0},{2,1},{3,2},{4,3},{5,4},{6,5},{7,6},{9,8},{10,9},{11,10},{12... | collective-permute-start | bytes 2359304 | tf_op jit(solution)/shard_map/ppermute | solution.py:24
  967.8 54.1 %collective-permute-start.6 = (f32[2,8,192,64]{2,3,1,0:T(8,128)}, f32[2,8,192,64]{2,3,1,0:T(8,128)}, u32[]{:S(2)}, u32[]{:S(2)}) collective-permute-start(f32[2,8,192,64]{2,3,1,0:T(8,128)} %copy.52), channel_id=1, source_target_pairs={{0,1},{1,2},{2,3},{3,4},{4,5},{5,6},{6,7},{8,9},{9,10},{10,11},{11... | collective-permute-start | bytes 2359304 | tf_op jit(solution)/shard_map/ppermute | solution.py:22
  1027.6 1.5 copy-start.5
  1027.6 1.8 copy-start.7
  1029.4 3.3 copy-start.2
  (3 other events, 3.2 us)
Sparse Core Ops, SparseCore 0:
  96.2 19.5 reduce-scatter.7
  159.7 182.1 reduce-scatter.9
  562.6 180.8 reduce-scatter.11
where the time goes:
time: 1050 us; the launch traced here: 1040 us
  waiting for transfers between devices  467 us (44%)
  blocking collectives  376 us (36%)
  starting transfers between devices  74.7 us (7%)
  matrix products  40 us (4%)
  other arithmetic  39.1 us (4%)
  local copies, waits for them, and re-layouts  31.8 us (3%)
  between operations  15.1 us (1%)
    reduce_scatter x2, waiting for transfers between devices, blur(): lax.psum_scatter(complex_left(cos_part, -sin_part, freq_input, half_width...  363 us
    all_gather x2, blocking collectives, blur(): portion = lax.all_gather(filtered, ('wave', 'col'), axis=0, tiled=True)  195 us
    all_to_all x2, blocking collectives, blur(): lax.all_to_all(restored_im, 'row', split_axis=0, concat_axis=1, tiled=True)  94.6 us
    ppermute x4, waiting for transfers between devices, extended_2(): lax.ppermute(head, axis, [((i + 1) % count, i) for i in range(ends)])  64.8 us
    ppermute x4, waiting for transfers between devices, extended_2(): lax.ppermute(tail, axis, [(i, (i + 1) % count) for i in range(ends)])  22.8 us
    all_to_all x1, blocking collectives, blur(): lax.all_to_all(spatial, 'col', split_axis=1, concat_axis=0, tiled=True)  22.4 us
    ppermute x4, starting transfers between devices, extended_2(): lax.ppermute(head, axis, [((i + 1) % count, i) for i in range(ends)])  21.6 us
  transfers between devices with their start and end apart: 15, of which 15 were waited for; matrix products, arithmetic and copies ran while one was open for 4% of the time, Pallas kernels for 0%

commit v1 on v0

v1 whole, which is shorter than its diff:
```python
import functools

import jax
import jax.numpy as jnp
import ml_dtypes
import numpy as np
from jax import lax
from jax.experimental import pallas as pl
from jax.experimental.pallas import tpu as pltpu
from jax.sharding import PartitionSpec as P

WAVES = 32
HALO = 64
TR = 64
TC = 128
NR = 512
NC = 1024
NW = 4
NROW = 8
NCOL = 8
LW = WAVES // NW
QC = TC // NW
KB = NR // (NCOL * NW)
F32 = jnp.float32
BF16 = jnp.bfloat16
VMEM_LIMIT = 48 * 1024 * 1024


def halves_of(table):
    high = table.astype(ml_dtypes.bfloat16)
    low = (table - high.astype(np.float64)).astype(ml_dtypes.bfloat16)
    return high, low


@functools.lru_cache(None)
def row_dft_table():
    group, block, inner = np.meshgrid(np.arange(4), np.arange(NROW), np.arange(16), indexing="ij")
    rows = (TR * block + 16 * group + inner).reshape(-1)
    angle = 2 * np.pi * (np.arange(NR)[:, None] * rows[None, :] % NR) / NR
    return halves_of(np.concatenate([np.cos(angle), -np.sin(angle)], axis=1))


@functools.lru_cache(None)
def col_dft_table():
    freq = np.arange(NC).reshape(NROW, 1, TC)
    angle = 2 * np.pi * (np.arange(NC)[None, :, None] * freq % NC) / NC
    return halves_of(np.concatenate([np.cos(angle), np.sin(angle)], axis=2))


@functools.lru_cache(None)
def col_inverse_table():
    angle = 2 * np.pi * (np.arange(NC)[:, None] * np.arange(NC)[None, :] % NC) / NC
    angle = angle.reshape(NC, 16, 1, 64)
    table = np.concatenate([np.cos(angle), np.sin(angle)], axis=2)
    return halves_of(table.reshape(NC, 2 * NC))


@functools.lru_cache(None)
def row_inverse_table():
    rows = (TR * np.arange(NROW)[:, None] - HALO + np.arange(TR + 2 * HALO)[None, :]) % NR
    angle = 2 * np.pi * (rows[:, :, None] * np.arange(NR)[None, None, :] % NR) / NR
    return halves_of(np.concatenate([np.cos(angle), np.sin(angle)], axis=1))


def split(values):
    high = values.astype(BF16)
    return high, (values - high.astype(F32)).astype(BF16)


def mm(left, right):
    return jnp.dot(left, right, preferred_element_type=F32)


def mm3(left, right):
    return mm(left[0], right[0]) + (mm(left[1], right[0]) + mm(left[0], right[1]))


def lane_ids(rows, lanes=128):
    return lax.broadcasted_iota(jnp.int32, (rows, lanes), 1)


def swapped(values):
    return pltpu.roll(values, 64, 1)


def column_taps(base):
    wide = jnp.broadcast_to(base, (128, 256))
    own = pltpu.roll(wide, 0, 1, stride=1, stride_axis=0)[:, :128]
    left = pltpu.roll(wide[:64], 256 - 64, 1, stride=1, stride_axis=0)[:, :128]
    right = pltpu.roll(wide[:64], 128, 1, stride=1, stride_axis=0)[:, :128]
    return jnp.concatenate([own, left, right], axis=0)


def row_taps(base):
    wide = jnp.broadcast_to(base, (64, 256))
    return pltpu.roll(wide, 64, 1, stride=1, stride_axis=0)[:, :192]


def column_pass(parts_re, parts_im, base_re, base_im):
    rows = parts_re[0].shape[0]
    field = jnp.concatenate(
        [jnp.concatenate(parts_re, axis=1), jnp.concatenate(parts_im, axis=1)], axis=0
    )
    table = jnp.concatenate([column_taps(base_re), column_taps(base_im)], axis=1)
    mix = mm3(split(field), split(table))
    return (
        mix[:rows, :128] - mix[rows:, 128:],
        mix[:rows, 128:] + mix[rows:, :128],
    )


def row_pass(stacked, base_re, base_im):
    table = jnp.concatenate([row_taps(base_re), row_taps(base_im)], axis=0)
    mix = mm3(split(table), split(stacked))
    return mix[:64, :128] - mix[64:, 128:], mix[:64, 128:] + mix[64:, :128]


def edges(re_part, im_part):
    lane = lane_ids(64)
    return (
        jnp.where(lane < 64, re_part, swapped(im_part)),
        jnp.where(lane < 64, swapped(re_part), im_part),
    )


def halo_parts(from_left, from_right):
    lane = lane_ids(from_left.shape[0])
    return (
        jnp.where(lane < 64, from_left, swapped(from_right)),
        jnp.where(lane < 64, swapped(from_left), from_right),
    )


def quarter(block, which):
    lane = lane_ids(16)
    out = jnp.zeros((16, 128), F32)
    for group in range(4):
        amount = lax.rem(32 * group - 32 * which + 128, 128)
        moved = pltpu.roll(block[16 * group : 16 * group + 16], amount, 1)
        out = jnp.where(lane // 32 == group, moved, out)
    return out


def pack_kernel(place_ref, field_ref, measured_ref, left_ref, right_ref, share_ref):
    for wave in range(LW):
        left, right = edges(field_ref[0, wave], field_ref[1, wave])
        left_ref[wave] = left
        right_ref[wave] = right
    share_ref[...] = jnp.broadcast_to(
        quarter(measured_ref[...], place_ref[0])[None], share_ref.shape
    )


def columns_kernel(field_ref, left_ref, right_ref, base_re_ref, base_im_ref, out_ref):
    halo_re, halo_im = halo_parts(left_ref[0], right_ref[0])
    re_out, im_out = column_pass(
        (field_ref[0, 0], halo_re), (field_ref[1, 0], halo_im), base_re_ref[0], base_im_ref[0]
    )
    out_ref[0, 0] = re_out
    out_ref[1, 0] = im_out


def rows_kernel(
    weight_ref, up_ref, own_ref, down_ref, base_re_ref, base_im_ref,
    out_ref, left_ref, right_ref, share_ref, total_ref,
):
    wave = pl.program_id(0)
    stacked = jnp.concatenate(
        [
            jnp.concatenate([ref[0, 0], ref[1, 0]], axis=1)
            for ref in (up_ref, own_ref, down_ref)
        ],
        axis=0,
    )
    re_out, im_out = row_pass(stacked, base_re_ref[0], base_im_ref[0])
    out_ref[0, 0] = re_out
    out_ref[1, 0] = im_out
    left, right = edges(re_out, im_out)
    left_ref[0] = left
    right_ref[0] = right
    term = weight_ref[wave] * (re_out * re_out + im_out * im_out)

    @pl.when(wave == 0)
    def _():
        total_ref[...] = term

    @pl.when(wave > 0)
    def _():
        total_ref[...] += term

    @pl.when(wave == LW - 1)
    def _():
        block = total_ref[...] * (1.0 / WAVES)
        for target in range(NW):
            piece = quarter(block, target)
            share_ref[pl.ds(target * NROW, NROW)] = jnp.broadcast_to(
                piece[None], (NROW, 16, 128)
            )


def row_dft_kernel(image_ref, measured_ref, high_ref, low_ref, out_ref):
    summed = image_ref[0:NROW] + image_ref[NROW : 2 * NROW]
    summed = summed + image_ref[2 * NROW : 3 * NROW]
    summed = (summed + image_ref[3 * NROW : 4 * NROW]).reshape(128, 128)
    known = measured_ref[...].reshape(128, 128)
    lane = lane_ids(128) // 32
    top = []
    low = []
    for group in range(4):
        first = pltpu.roll(summed, (128 - 32 * group) % 128, 1)
        third = pltpu.roll(known, (192 - 32 * group) % 128, 1)
        both = jnp.where(lane == 0, first, jnp.where(lane == 2, third, 0.0))
        top.append(both)
        low.append(pltpu.roll(both, 32, 1))
    operand = split(jnp.concatenate(top + low, axis=0))
    out_ref[...] = mm3((high_ref[...], low_ref[...]), operand).reshape(out_ref.shape)


def filter_kernel(place_ref, rows_ref, high_ref, low_ref, spec_re_ref, spec_im_ref, out_ref):
    lane = lane_ids(16) // 32
    channels = []
    for channel in range(4):
        pieces = []
        for col in range(NCOL):
            piece = jnp.zeros((16, 128), F32)
            for wave in range(NW):
                moved = pltpu.roll(rows_ref[col * NW + wave], (32 * (wave - channel)) % 128, 1)
                piece = jnp.where(lane == wave, moved, piece)
            pieces.append(piece)
        channels.append(jnp.concatenate(pieces, axis=1))
    operand = split(jnp.concatenate(channels, axis=0))
    mix = mm3(operand, (high_ref[0], low_ref[0]))
    image_re = mix[0:16, :128] + mix[16:32, 128:]
    image_im = mix[16:32, :128] - mix[0:16, 128:]
    known_re = mix[32:48, :128] + mix[48:64, 128:]
    known_im = mix[48:64, :128] - mix[32:48, 128:]
    spec_re, spec_im = spec_re_ref[...], spec_im_ref[...]
    blur_re = image_re * spec_re - image_im * spec_im
    blur_im = image_re * spec_im + image_im * spec_re
    rest_re = blur_re - known_re
    rest_im = blur_im - known_im
    pull_re = rest_re * spec_re + rest_im * spec_im
    pull_im = rest_im * spec_re - rest_re * spec_im
    scale = 1.0 / (NR * NC)
    both = jnp.concatenate([blur_re - pull_im, blur_im + pull_re], axis=0) * scale
    out_ref[...] = jnp.broadcast_to(both[None], out_ref.shape)


def col_inverse_kernel(rows_ref, high_ref, low_ref, out_ref):
    step = pl.program_id(0)
    operand = split(jnp.concatenate([rows_ref[block] for block in range(NROW)], axis=1))
    mix = mm3(operand, (high_ref[...], low_ref[...]))
    lane = lane_ids(16)
    for half in range(2):
        part = mix[:, 128 * half : 128 * half + 128]
        other = swapped(part[16:])
        piece = part[:16] + jnp.where(lane < 64, -other, other)
        if half == 0:
            targets = (step * NW + 1, lax.rem(step + 7, 8) * NW + 3)
        else:
            targets = (lax.rem(step + 1, 8) * NW, step * NW + 2)
        for target in targets:
            out_ref[target] = piece


def row_inverse_kernel(place_ref, rows_ref, high_ref, low_ref, out_ref):
    operand = split(rows_ref[...].reshape(NR, 128))
    mix = mm3((high_ref[0], low_ref[0]), operand)
    cos_part, sin_part = mix[:192], mix[192:]
    pulled = sin_part + swapped(cos_part)
    blurred = cos_part[64:128] - swapped(sin_part[64:128])
    low = lane_ids(96) < 64
    packed = jnp.where(low, pulled[:96], swapped(pulled[96:]))
    packed_blur = jnp.where(low[:32], blurred[:32], swapped(blurred[32:]))
    both = jnp.concatenate([packed, packed_blur], axis=0)
    out_ref[...] = jnp.broadcast_to(both[None], out_ref.shape)


def gradient_kernel(
    weight_ref, own_ref, left_ref, right_ref, up_ref, up_halo_ref, down_ref, down_halo_ref,
    images_ref, measured_ref, base_re_ref, base_im_ref, out_ref, residual_ref,
):
    wave = pl.program_id(0)
    low = lane_ids(96) < 64

    def joined(first, second):
        one, two = images_ref[first], images_ref[second]
        return (
            jnp.concatenate(
                [
                    jnp.where(low, one[:96], swapped(two[:96])),
                    jnp.where(low, swapped(one[:96]), two[:96]),
                ],
                axis=0,
            ),
            jnp.concatenate(
                [
                    jnp.where(low[:32], one[96:], swapped(two[96:])),
                    jnp.where(low[:32], swapped(one[96:]), two[96:]),
                ],
                axis=0,
            ),
        )

    centre, blurred = joined(1, 2)
    border, unused = joined(0, 3)

    @pl.when(wave == 0)
    def _():
        residual_ref[...] = blurred - measured_ref[...]

    factor = 2.0 * weight_ref[wave]
    centre = centre * factor
    border = border * factor
    halos = [
        halo_parts(up_halo_ref[0, 0], up_halo_ref[1, 0]),
        halo_parts(left_ref[0], right_ref[0]),
        halo_parts(down_halo_ref[0, 0], down_halo_ref[1, 0]),
    ]
    parts = []
    for part, sign in ((0, 1.0), (1, -1.0)):
        own = jnp.concatenate([up_ref[part, 0], own_ref[part, 0], down_ref[part, 0]], axis=0)
        halo = jnp.concatenate([pair[part] for pair in halos], axis=0)
        parts.append((sign * (own * centre), sign * (halo * border)))
    re_mid, im_mid = column_pass(parts[0], parts[1], base_re_ref[0], base_im_ref[0])
    re_out, im_out = row_pass(
        jnp.concatenate([re_mid, im_mid], axis=1), base_re_ref[0], base_im_ref[0]
    )
    out_ref[0, 0] = re_out
    out_ref[1, 0] = -im_out


def params():
    return pltpu.CompilerParams(vmem_limit_bytes=VMEM_LIMIT)


def shape(*dims):
    return jax.ShapeDtypeStruct(dims, F32)


SMEM = pl.BlockSpec(memory_space=pltpu.SMEM)


def per_wave(*block):
    if len(block) == 4:
        return pl.BlockSpec(block, lambda w: (0, w, 0, 0))
    return pl.BlockSpec(block, lambda w: (w, 0, 0))


def whole(*block):
    return pl.BlockSpec(block, lambda *unused: (0,) * len(block))


def neighbours(value, axis, count, step):
    return lax.ppermute(
        value, axis, [(i, i + step) for i in range(count) if 0 <= i + step < count]
    )


def mirrored_spectrum(spectrum):
    def mirror(value, axis, dim):
        size = value.shape[dim]
        rest = lax.ppermute(value, axis, [(i, 7 - i) for i in range(8)])
        edge = lax.ppermute(
            lax.slice_in_dim(value, 0, 1, axis=dim), axis, [(i, (8 - i) % 8) for i in range(8)]
        )
        rest = lax.rev(lax.slice_in_dim(rest, 1, size, axis=dim), (dim,))
        return jnp.concatenate([edge, rest], axis=dim)

    return mirror(mirror(spectrum, "col", 1), "row", 2)


def taps_of(wavelength):
    lane = jnp.arange(256)
    offset = jnp.where(lane < 128, lane, lane - 256).astype(F32)
    spread = jnp.arange(-HALO, HALO + 1).astype(F32)
    norm = 1.0 / jnp.sqrt(jnp.sum(jnp.exp(-2.0 * (spread / HALO) ** 2)))
    amplitude = jnp.where(jnp.abs(offset) <= HALO, jnp.exp(-((offset / HALO) ** 2)) * norm, 0.0)
    phase = offset * offset / (2.0 * wavelength[:, None] * HALO)
    return (amplitude * jnp.cos(phase))[:, None, :], (amplitude * jnp.sin(phase))[:, None, :]


def shards(wavefield, wavelength, weight, spectrum, measured):
    wave_place = lax.axis_index("wave")
    row_place = lax.axis_index("row")[None]

    left_edge, right_edge, known_share = pl.pallas_call(
        pack_kernel,
        in_specs=[SMEM, pl.BlockSpec(), pl.BlockSpec()],
        out_shape=(shape(LW, 64, 128), shape(LW, 64, 128), shape(NROW, 16, 128)),
        compiler_params=params(),
    )(wave_place[None], wavefield, measured)
    from_left = neighbours(right_edge, "col", NCOL, 1)
    from_right = neighbours(left_edge, "col", NCOL, -1)

    base_re, base_im = taps_of(wavelength)
    base_specs = [per_wave(1, 1, 256), per_wave(1, 1, 256)]
    mirror = mirrored_spectrum(spectrum)
    spec_re = 0.5 * (spectrum[0] + mirror[0])
    spec_im = 0.5 * (spectrum[1] - mirror[1])
    spec_re = lax.dynamic_slice_in_dim(spec_re, wave_place * KB, KB, 0)
    spec_im = lax.dynamic_slice_in_dim(spec_im, wave_place * KB, KB, 0)
    known = lax.all_to_all(known_share, "row", split_axis=0, concat_axis=0, tiled=True)

    middle = pl.pallas_call(
        columns_kernel,
        grid=(LW,),
        in_specs=[per_wave(2, 1, 64, 128), per_wave(1, 64, 128), per_wave(1, 64, 128)] + base_specs,
        out_specs=per_wave(2, 1, 64, 128),
        out_shape=shape(2, LW, 64, 128),
        compiler_params=params(),
    )(wavefield, from_left, from_right, base_re, base_im)
    from_up = neighbours(middle, "row", NROW, 1)
    from_down = neighbours(middle, "row", NROW, -1)
    propagated, left_edge, right_edge, shares = pl.pallas_call(
        rows_kernel,
        grid=(LW,),
        in_specs=[SMEM] + [per_wave(2, 1, 64, 128)] * 3 + base_specs,
        out_specs=(
            per_wave(2, 1, 64, 128),
            per_wave(1, 64, 128),
            per_wave(1, 64, 128),
            whole(NW * NROW, 16, 128),
        ),
        out_shape=(
            shape(2, LW, 64, 128),
            shape(LW, 64, 128),
            shape(LW, 64, 128),
            shape(NW * NROW, 16, 128),
        ),
        scratch_shapes=[pltpu.VMEM((64, 128), F32)],
        compiler_params=params(),
    )(weight, from_up, middle, from_down, base_re, base_im)

    prop_left = neighbours(right_edge, "col", NCOL, 1)
    prop_right = neighbours(left_edge, "col", NCOL, -1)
    prop_up = neighbours(propagated, "row", NROW, 1)
    prop_down = neighbours(propagated, "row", NROW, -1)
    sides = jnp.stack([prop_left, prop_right])
    up_sides = neighbours(sides, "row", NROW, 1)
    down_sides = neighbours(sides, "row", NROW, -1)

    image = lax.all_to_all(shares, ("wave", "row"), split_axis=0, concat_axis=0, tiled=True)
    high, low = row_dft_table()
    freq_rows = pl.pallas_call(
        row_dft_kernel,
        out_shape=shape(NCOL * NW, 16, 128),
        compiler_params=params(),
    )(image, known, jnp.asarray(high), jnp.asarray(low))
    freq_rows = lax.all_to_all(freq_rows, ("col", "wave"), split_axis=0, concat_axis=0, tiled=True)

    high, low = col_dft_table()
    table_spec = pl.BlockSpec((1, NC, 256), lambda i, place: (place[0], 0, 0))
    filtered = pl.pallas_call(
        filter_kernel,
        grid_spec=pltpu.PrefetchScalarGridSpec(
            num_scalar_prefetch=1,
            grid=(1,),
            in_specs=[
                whole(NCOL * NW, 16, 128), table_spec, table_spec, whole(KB, 128), whole(KB, 128),
            ],
            out_specs=whole(NROW, 2 * KB, 128),
        ),
        out_shape=shape(NROW, 2 * KB, 128),
        compiler_params=params(),
    )(row_place, freq_rows, jnp.asarray(high), jnp.asarray(low), spec_re, spec_im)
    filtered = lax.all_to_all(filtered, "row", split_axis=0, concat_axis=0, tiled=True)

    high, low = col_inverse_table()
    table_spec = pl.BlockSpec((NC, 256), lambda i: (0, i))
    columns = pl.pallas_call(
        col_inverse_kernel,
        grid=(8,),
        in_specs=[whole(NROW, 2 * KB, 128), table_spec, table_spec],
        out_specs=whole(NCOL * NW, 16, 128),
        out_shape=shape(NCOL * NW, 16, 128),
        compiler_params=params(),
    )(filtered, jnp.asarray(high), jnp.asarray(low))
    columns = lax.all_to_all(columns, ("col", "wave"), split_axis=0, concat_axis=0, tiled=True)

    high, low = row_inverse_table()
    table_spec = pl.BlockSpec((1, 384, NR), lambda i, place: (place[0], 0, 0))
    images = pl.pallas_call(
        row_inverse_kernel,
        grid_spec=pltpu.PrefetchScalarGridSpec(
            num_scalar_prefetch=1,
            grid=(1,),
            in_specs=[whole(NCOL * NW, 16, 128), table_spec, table_spec],
            out_specs=whole(NW, 128, 128),
        ),
        out_shape=shape(NW, 128, 128),
        compiler_params=params(),
    )(row_place, columns, jnp.asarray(high), jnp.asarray(low))
    images = lax.all_to_all(images, "wave", split_axis=0, concat_axis=0, tiled=True)

    field_grad, residual = pl.pallas_call(
        gradient_kernel,
        grid=(LW,),
        in_specs=[
            SMEM,
            per_wave(2, 1, 64, 128),
            per_wave(1, 64, 128),
            per_wave(1, 64, 128),
            per_wave(2, 1, 64, 128),
            per_wave(2, 1, 64, 128),
            per_wave(2, 1, 64, 128),
            per_wave(2, 1, 64, 128),
            whole(NW, 128, 128),
            whole(64, 128),
        ] + base_specs,
        out_specs=(per_wave(2, 1, 64, 128), whole(64, 128)),
        out_shape=(shape(2, LW, 64, 128), shape(64, 128)),
        compiler_params=params(),
    )(
        weight, propagated, prop_left, prop_right, prop_up, up_sides, prop_down, down_sides,
        images, measured, base_re, base_im,
    )
    return field_grad, residual


def solution(mesh):
    placed = (
        P(None, "wave", "row", "col"),
        P("wave"),
        P("wave"),
        P(None, "col", "row"),
        P("row", "col"),
    )
    return jax.shard_map(
        shards,
        mesh=mesh,
        in_specs=placed,
        out_specs=(P(None, "wave", "row", "col"), P("row", "col")),
        check_vma=False,
    )
```

time: 1050 us -> 177 us (0.17)
  the two profiles are of different devices: /device:TPU:193 before, /device:TPU:32 now
where the time goes in v1:
time: 177 us; the launch traced here: 175 us
  starting transfers between devices  83.5 us (47%)
  waiting for transfers between devices  43.1 us (24%)
  Pallas kernels  31.8 us (18%)
  local copies, waits for them, and re-layouts  11.5 us (6%)
  other arithmetic  3.61 us (2%)
    ppermute x10, starting transfers between devices, neighbours(): lax.ppermute(value, axis, [(i, i + step) for i in range(count) if 0 <= i...  23 us
    all_to_all x1, starting transfers between devices, shards(): lax.all_to_all(freq_rows, ('col', 'wave'), split_axis=0, concat_axis=0, t...  18 us
    ppermute x10, waiting for transfers between devices, neighbours(): lax.ppermute(value, axis, [(i, i + step) for i in range(count) if 0 <= i...  13.4 us
    unnamed x32, local copies, waits for them, and re-layouts  11.2 us
    ppermute x2, waiting for transfers between devices, mirror(): rest = lax.ppermute(value, axis, [(i, 7 - i) for i in range(8)])  11.2 us
    all_to_all x1, starting transfers between devices, shards(): lax.all_to_all(columns, ('col', 'wave'), split_axis=0, concat_axis=0, til...  10.5 us
    pallas_call x1, Pallas kernels, shards(): pl.pallas_call(gradient_kernel, grid=(LW,), in_specs=[SMEM, per_wave(2, 1...  9.04 us
    all_to_all x1, starting transfers between devices, shards(): lax.all_to_all(shares, ('wave', 'row'), split_axis=0, concat_axis=0, tile...  7.8 us
  transfers between devices with their start and end apart: 20, of which 9 were waited for; matrix products, arithmetic and copies ran while one was open for 2% of the time, Pallas kernels for 10%

profile of v1, /device:TPU:32, one launch (start us, length us, event | category | flops | bytes accessed | tf_op | source)
XLA Modules:
  0.0 175.0 jit_solution(2606938828119929827)
XLA Ops:
  3.2 3.5 %collective-permute-start = (f32[8,64,128]{2,1,0:T(8,128)S(1)}, f32[8,64,128]{2,1,0:T(8,128)S(1)}, u32[]{:S(2)}, u32[]{:S(2)}) collective-permute-start(f32[8,64,128]{2,1,0:T(8,128)S(1)} %get-tuple-element.9), channel_id=1, source_target_pairs={{0,1},{1,2},{2,3},{3,4},{4,5},{5,6},{6,7},{8,9},{9,10},{10,11},{11... | collective-permute-start | bytes 786440 | tf_op jit(solution)/shard_map/ppermute | solution.py:355
  12.3 4.1 %collective-permute-done.1.right_ref = f32[8,64,128]{2,1,0:T(8,128)S(1)} collective-permute-done((f32[8,64,128]{2,1,0:T(8,128)S(1)}, f32[8,64,128]{2,1,0:T(8,128)S(1)}, u32[]{:S(2)}, u32[]{:S(2)}) %collective-permute-start.1) | collective-permute-done | bytes 262176 | tf_op jit(solution)/shard_map/ppermute | solution.py:355
  17.4 2.9 %shard_map.141.own_ref = f32[2,8,64,128]{3,2,1,0:T(8,128)S(1)} custom-call(f32[2,8,64,128]{3,2,1,0:T(8,128)S(1)} %copy-done.4, f32[8,64,128]{2,1,0:T(8,128)S(1)} %collective-permute-done.left_ref, f32[8,64,128]{2,1,0:T(8,128)S(1)} %collective-permute-done.1.right_ref, f32[8,1,256]{2,1,0:T(1,128)S(1)} %get-tuple-element.19.base_re_ref, ...), custom_call_target="tpu_custom_call" | custom-call | tf_op jit(solution)/shard_map/pallas_call | solution.py:405
  22.3 2.4 %collective-permute-start.2 = (f32[2,8,64,128]{3,2,1,0:T(8,128)S(1)}, f32[2,8,64,128]{3,2,1,0:T(8,128)}, u32[]{:S(2)}, u32[]{:S(2)}) collective-permute-start(f32[2,8,64,128]{3,2,1,0:T(8,128)S(1)} %shard_map.141.own_ref), channel_id=1, source_target_pairs={{0,8},{8,16},{16,24},{24,32},{32,40},{40,48},{48,56},{1,9},{9,17},... | collective-permute-start | bytes 1572872 | tf_op jit(solution)/shard_map/ppermute | solution.py:355
  24.7 6.0 %all-to-all-start.1 = ((f32[8,16,128]{2,1,0:T(8,128)}), f32[8,16,128]{2,1,0:T(8,128)S(1)}, u32[]{:S(2)}, u32[]{:S(2)}) async-start(f32[8,16,128]{2,1,0:T(8,128)} %get-tuple-element.15), calls=%async_computation.1 | async-start | bytes 131072 | tf_op jit(solution)/shard_map/all_to_all | solution.py:403
  30.8 7.3 %collective-permute-done.2.up_ref = f32[2,8,64,128]{3,2,1,0:T(8,128)} collective-permute-done((f32[2,8,64,128]{3,2,1,0:T(8,128)S(1)}, f32[2,8,64,128]{3,2,1,0:T(8,128)}, u32[]{:S(2)}, u32[]{:S(2)}) %collective-permute-start.2) | collective-permute-done | bytes 524320 | tf_op jit(solution)/shard_map/ppermute | solution.py:355
  38.7 6.3 %shard_map.142 = (f32[2,8,64,128]{3,2,1,0:T(8,128)S(1)}, f32[8,64,128]{2,1,0:T(8,128)}, f32[8,64,128]{2,1,0:T(8,128)}, f32[32,16,128]{2,1,0:T(8,128)}) custom-call(f32[8]{0:T(128)S(1)} %copy-done.13, f32[2,8,64,128]{3,2,1,0:T(8,128)} %collective-permute-done.2.up_ref, f32[2,8,64,128]{3,2,1,0:T(8,128)S(1)} %shard_map.141.own_ref, ...), custom_call_target="tpu_custom_call" | custom-call | tf_op jit(solution)/shard_map/pallas_call | solution.py:415
  45.9 7.8 %all-to-all-start = ((f32[32,16,128]{2,1,0:T(8,128)}), f32[32,16,128]{2,1,0:T(8,128)S(1)}, u32[]{:S(2)}, u32[]{:S(2)}) async-start(f32[32,16,128]{2,1,0:T(8,128)} %get-tuple-element.14), calls=%async_computation | async-start | bytes 524288 | tf_op jit(solution)/shard_map/all_to_all | solution.py:443
  55.3 8.8 %collective-permute-done.11 = f32[2,64,128]{2,1,0:T(8,128)S(1)} collective-permute-done((f32[2,64,128]{2,1,0:T(8,128)S(1)}, f32[2,64,128]{2,1,0:T(8,128)S(1)}, u32[]{:S(2)}, u32[]{:S(2)}) %collective-permute-start.11) | collective-permute-done | bytes 65568 | tf_op jit(solution)/shard_map/ppermute | solution.py:363
  66.0 18.0 %all-to-all-start.2 = ((f32[32,16,128]{2,1,0:T(8,128)}), f32[32,16,128]{2,1,0:T(8,128)S(1)}, u32[]{:S(2)}, u32[]{:S(2)}) async-start(f32[32,16,128]{2,1,0:T(8,128)} %shard_map.143), calls=%async_computation.2 | async-start | bytes 524288 | tf_op jit(solution)/shard_map/all_to_all | solution.py:450
  84.0 5.4 %collective-permute-start.12 = (f32[2,64,1]{2,1,0:T(8,128)S(1)}, f32[2,64,1]{2,1,0:T(8,128)S(1)}, u32[]{:S(2)}, u32[]{:S(2)}) collective-permute-start(f32[2,64,1]{2,1,0:T(8,128)S(1)} %fusion), channel_id=1, source_target_pairs={{0,0},{8,56},{16,48},{24,40},{32,32},{40,24},{48,16},{56,8},{1,1},... | collective-permute-start | bytes 1544 | tf_op jit(solution)/shard_map/ppermute | solution.py:364
  89.5 6.2 %collective-permute-done.12 = f32[2,64,1]{2,1,0:T(8,128)S(1)} collective-permute-done((f32[2,64,1]{2,1,0:T(8,128)S(1)}, f32[2,64,1]{2,1,0:T(8,128)S(1)}, u32[]{:S(2)}, u32[]{:S(2)}) %collective-permute-start.12) | collective-permute-done | bytes 544 | tf_op jit(solution)/shard_map/ppermute | solution.py:364
  95.7 2.4 %collective-permute-done.13 = f32[2,64,128]{2,1,0:T(8,128)S(1)} collective-permute-done((f32[2,64,128]{2,1,0:T(8,128)S(1)}, f32[2,64,128]{2,1,0:T(8,128)S(1)}, u32[]{:S(2)}, u32[]{:S(2)}) %collective-permute-start.13) | collective-permute-done | bytes 65568 | tf_op jit(solution)/shard_map/ppermute | solution.py:363
  100.6 2.2 %shard_map.144 = f32[8,32,128]{2,1,0:T(8,128)} custom-call(s32[1]{0:T(128)} %bitcast.3.place_ref, f32[32,16,128]{2,1,0:T(8,128)S(1)} %all-to-all-done.2.rows_ref, bf16[8,1024,256]{2,1,0:T(8,128)(2,1)S(1)} %copy-done.1, bf16[8,1024,256]{2,1,0:T(8,128)(2,1)} %constant.61.clone.low_ref, f32[16,128]{1,0:T(8,128)S(1)} %get-tuple-element.23.spec_re_ref, ...), custom_call_target="tpu_custom_call" | custom-call | tf_op jit(solution)/shard_map/pallas_call | solution.py:454
  102.9 7.7 %all-to-all-start.3 = ((f32[8,32,128]{2,1,0:T(8,128)}), f32[8,32,128]{2,1,0:T(8,128)S(1)}, u32[]{:S(2)}, u32[]{:S(2)}) async-start(f32[8,32,128]{2,1,0:T(8,128)} %shard_map.144), calls=%async_computation.3 | async-start | bytes 262144 | tf_op jit(solution)/shard_map/all_to_all | solution.py:467
  110.6 3.2 %collective-permute-start.4 = (f32[8,64,128]{2,1,0:T(8,128)}, f32[8,64,128]{2,1,0:T(8,128)}, u32[]{:S(2)}, u32[]{:S(2)}) collective-permute-start(f32[8,64,128]{2,1,0:T(8,128)} %get-tuple-element.12), channel_id=1, source_target_pairs={{0,1},{1,2},{2,3},{3,4},{4,5},{5,6},{6,7},{8,9},{9,10},{10,11},{11... | collective-permute-start | bytes 786440 | tf_op jit(solution)/shard_map/ppermute | solution.py:355
  118.4 7.0 %shard_map.145 = f32[32,16,128]{2,1,0:T(8,128)S(1)} custom-call(f32[8,32,128]{2,1,0:T(8,128)S(1)} %all-to-all-done.3.rows_ref, bf16[1024,2048]{1,0:T(8,128)(2,1)S(1)} %copy-done, bf16[1024,2048]{1,0:T(8,128)(2,1)} %constant.63.clone.low_ref), custom_call_target="tpu_custom_call" | custom-call | tf_op jit(solution)/shard_map/pallas_call | solution.py:471
  126.2 10.5 %all-to-all-start.4 = ((f32[32,16,128]{2,1,0:T(8,128)}), f32[32,16,128]{2,1,0:T(8,128)S(1)}, u32[]{:S(2)}, u32[]{:S(2)}) async-start(f32[32,16,128]{2,1,0:T(8,128)} %copy-done.5), calls=%async_computation.4 | async-start | bytes 524288 | tf_op jit(solution)/shard_map/all_to_all | solution.py:479
  138.7 2.4 %collective-permute-start.6 = (f32[2,8,64,128]{3,2,1,0:T(8,128)}, f32[2,8,64,128]{3,2,1,0:T(8,128)}, u32[]{:S(2)}, u32[]{:S(2)}) collective-permute-start(f32[2,8,64,128]{3,2,1,0:T(8,128)} %copy-done.9), channel_id=1, source_target_pairs={{0,8},{8,16},{16,24},{24,32},{32,40},{40,48},{48,56},{1,9},{9,17},... | collective-permute-start | bytes 1572872 | tf_op jit(solution)/shard_map/ppermute | solution.py:355
  143.0 3.1 %collective-permute-start.9 = (f32[2,8,64,128]{3,2,1,0:T(8,128)}, f32[2,8,64,128]{3,2,1,0:T(8,128)}, u32[]{:S(2)}, u32[]{:S(2)}) collective-permute-start(f32[2,8,64,128]{3,2,1,0:T(8,128)} %pad_maximum_fusion), channel_id=1, source_target_pairs={{8,0},{16,8},{24,16},{32,24},{40,32},{48,40},{56,48},{9,1},{17,9},... | collective-permute-start | bytes 1572872 | tf_op jit(solution)/shard_map/ppermute | solution.py:355
  148.1 4.5 %all-to-all-done.4.rows_ref = f32[32,16,128]{2,1,0:T(8,128)S(1)} async-done(((f32[32,16,128]{2,1,0:T(8,128)}), f32[32,16,128]{2,1,0:T(8,128)S(1)}, u32[]{:S(2)}, u32[]{:S(2)}) %all-to-all-start.4) | async-done | bytes 262176 | tf_op jit(solution)/shard_map/all_to_all | solution.py:479
  154.9 3.4 %all-to-all-start.5 = ((f32[4,128,128]{2,1,0:T(8,128)}), f32[4,128,128]{2,1,0:T(8,128)S(1)}, u32[]{:S(2)}, u32[]{:S(2)}) async-start(f32[4,128,128]{2,1,0:T(8,128)} %copy-done.6), calls=%async_computation.5 | async-start | bytes 524288 | tf_op jit(solution)/shard_map/all_to_all | solution.py:494
  158.4 6.6 %all-to-all-done.5.images_ref = f32[4,128,128]{2,1,0:T(8,128)S(1)} async-done(((f32[4,128,128]{2,1,0:T(8,128)}), f32[4,128,128]{2,1,0:T(8,128)S(1)}, u32[]{:S(2)}, u32[]{:S(2)}) %all-to-all-start.5) | async-done | bytes 262176 | tf_op jit(solution)/shard_map/all_to_all | solution.py:494
  166.0 9.0 %shard_map.147 = (f32[2,8,64,128]{3,2,1,0:T(8,128)}, f32[64,128]{1,0:T(8,128)}) custom-call(f32[8]{0:T(128)S(1)} %copy-done.14, f32[2,8,64,128]{3,2,1,0:T(8,128)S(1)} %copy-done.10, f32[8,64,128]{2,1,0:T(8,128)} %collective-permute-done.4.left_ref, f32[8,64,128]{2,1,0:T(8,128)} %collective-permute-done.5.right_ref, ...), custom_call_target="tpu_custom_call" | custom-call | tf_op jit(solution)/shard_map/pallas_call | solution.py:496
  (72 shorter events, 32.4 us)
Async XLA Ops:
  2.4 51.2 %copy-start.15 = (f32[2,64,128]{2,1,0:T(8,128)S(1)}, f32[2,64,128]{2,1,0:T(8,128)}, u32[]{:S(2)}) copy-start(f32[2,64,128]{2,1,0:T(8,128)} %param.16) | copy-start | bytes 196612
  3.2 9.0 %collective-permute-start = (f32[8,64,128]{2,1,0:T(8,128)S(1)}, f32[8,64,128]{2,1,0:T(8,128)S(1)}, u32[]{:S(2)}, u32[]{:S(2)}) collective-permute-start(f32[8,64,128]{2,1,0:T(8,128)S(1)} %get-tuple-element.9), channel_id=1, source_target_pairs={{0,1},{1,2},{2,3},{3,4},{4,5},{5,6},{6,7},{8,9},{9,10},{10,11},{11... | collective-permute-start | bytes 786440 | tf_op jit(solution)/shard_map/ppermute | solution.py:355
  6.7 9.7 %collective-permute-start.1 = (f32[8,64,128]{2,1,0:T(8,128)S(1)}, f32[8,64,128]{2,1,0:T(8,128)S(1)}, u32[]{:S(2)}, u32[]{:S(2)}) collective-permute-start(f32[8,64,128]{2,1,0:T(8,128)S(1)} %get-tuple-element.10), channel_id=1, source_target_pairs={{1,0},{2,1},{3,2},{4,3},{5,4},{6,5},{7,6},{9,8},{10,9},{11,10},{12... | collective-permute-start | bytes 786440 | tf_op jit(solution)/shard_map/ppermute | solution.py:355
  17.4 46.7 %copy-start.7 = (bf16[512,1024]{1,0:T(8,128)(2,1)S(1)}, bf16[512,1024]{1,0:T(8,128)(2,1)}, u32[]{:S(2)}) copy-start(bf16[512,1024]{1,0:T(8,128)(2,1)} %constant.59.clone.low_ref) | copy-start | bytes 3145732
  17.4 46.7 %copy-start.8 = (bf16[512,1024]{1,0:T(8,128)(2,1)S(1)}, bf16[512,1024]{1,0:T(8,128)(2,1)}, u32[]{:S(2)}) copy-start(bf16[512,1024]{1,0:T(8,128)(2,1)} %constant.58.clone.high_ref) | copy-start | bytes 3145732
  20.4 10.4 %collective-permute-start.3 = (f32[2,8,64,128]{3,2,1,0:T(8,128)S(1)}, f32[2,8,64,128]{3,2,1,0:T(8,128)S(1)}, u32[]{:S(2)}, u32[]{:S(2)}) collective-permute-start(f32[2,8,64,128]{3,2,1,0:T(8,128)S(1)} %shard_map.141.own_ref), channel_id=1, source_target_pairs={{8,0},{16,8},{24,16},{32,24},{40,32},{48,40},{56,48},{9,1},{17,9},... | collective-permute-start | bytes 1572872 | tf_op jit(solution)/shard_map/ppermute | solution.py:355
  22.3 15.8 %collective-permute-start.2 = (f32[2,8,64,128]{3,2,1,0:T(8,128)S(1)}, f32[2,8,64,128]{3,2,1,0:T(8,128)}, u32[]{:S(2)}, u32[]{:S(2)}) collective-permute-start(f32[2,8,64,128]{3,2,1,0:T(8,128)S(1)} %shard_map.141.own_ref), channel_id=1, source_target_pairs={{0,8},{8,16},{16,24},{24,32},{32,40},{40,48},{48,56},{1,9},{9,17},... | collective-permute-start | bytes 1572872 | tf_op jit(solution)/shard_map/ppermute | solution.py:355
  24.7 21.1 %all-to-all-start.1 = ((f32[8,16,128]{2,1,0:T(8,128)}), f32[8,16,128]{2,1,0:T(8,128)S(1)}, u32[]{:S(2)}, u32[]{:S(2)}) async-start(f32[8,16,128]{2,1,0:T(8,128)} %get-tuple-element.15), calls=%async_computation.1 | async-start | bytes 131072 | tf_op jit(solution)/shard_map/all_to_all | solution.py:403
  45.9 18.2 %all-to-all-start = ((f32[32,16,128]{2,1,0:T(8,128)}), f32[32,16,128]{2,1,0:T(8,128)S(1)}, u32[]{:S(2)}, u32[]{:S(2)}) async-start(f32[32,16,128]{2,1,0:T(8,128)} %get-tuple-element.14), calls=%async_computation | async-start | bytes 524288 | tf_op jit(solution)/shard_map/all_to_all | solution.py:443
  53.7 10.4 %collective-permute-start.11 = (f32[2,64,128]{2,1,0:T(8,128)S(1)}, f32[2,64,128]{2,1,0:T(8,128)S(1)}, u32[]{:S(2)}, u32[]{:S(2)}) collective-permute-start(f32[2,64,128]{2,1,0:T(8,128)S(1)} %copy-done.15), channel_id=1, source_target_pairs={{0,7},{1,6},{2,5},{3,4},{4,3},{5,2},{6,1},{7,0},{8,15},{9,14},{10,... | collective-permute-start | bytes 196616 | tf_op jit(solution)/shard_map/ppermute | solution.py:363
  54.6 29.4 %collective-permute-start.10 = (f32[2,1,128]{2,1,0:T(1,128)S(1)}, f32[2,1,128]{2,1,0:T(1,128)S(1)}, u32[]{:S(2)}, u32[]{:S(2)}) collective-permute-start(f32[2,1,128]{2,1,0:T(1,128)S(1)} %slice.25), channel_id=1, source_target_pairs={{0,0},{1,7},{2,6},{3,5},{4,4},{5,3},{6,2},{7,1},{8,8},{9,15},{10,1... | collective-permute-start | bytes 3080 | tf_op jit(solution)/shard_map/ppermute | solution.py:364
  66.0 32.5 %all-to-all-start.2 = ((f32[32,16,128]{2,1,0:T(8,128)}), f32[32,16,128]{2,1,0:T(8,128)S(1)}, u32[]{:S(2)}, u32[]{:S(2)}) async-start(f32[32,16,128]{2,1,0:T(8,128)} %shard_map.143), calls=%async_computation.2 | async-start | bytes 524288 | tf_op jit(solution)/shard_map/all_to_all | solution.py:450
  84.0 11.7 %collective-permute-start.12 = (f32[2,64,1]{2,1,0:T(8,128)S(1)}, f32[2,64,1]{2,1,0:T(8,128)S(1)}, u32[]{:S(2)}, u32[]{:S(2)}) collective-permute-start(f32[2,64,1]{2,1,0:T(8,128)S(1)} %fusion), channel_id=1, source_target_pairs={{0,0},{8,56},{16,48},{24,40},{32,32},{40,24},{48,16},{56,8},{1,1},... | collective-permute-start | bytes 1544 | tf_op jit(solution)/shard_map/ppermute | solution.py:364
  89.4 8.7 %collective-permute-start.13 = (f32[2,64,128]{2,1,0:T(8,128)S(1)}, f32[2,64,128]{2,1,0:T(8,128)S(1)}, u32[]{:S(2)}, u32[]{:S(2)}) collective-permute-start(f32[2,64,128]{2,1,0:T(8,128)S(1)} %pad_maximum_fusion.1), channel_id=1, source_target_pairs={{0,56},{8,48},{16,40},{24,32},{32,24},{40,16},{48,8},{56,0},{1,57}... | collective-permute-start | bytes 196616 | tf_op jit(solution)/shard_map/ppermute | solution.py:363
  102.9 13.4 %all-to-all-start.3 = ((f32[8,32,128]{2,1,0:T(8,128)}), f32[8,32,128]{2,1,0:T(8,128)S(1)}, u32[]{:S(2)}, u32[]{:S(2)}) async-start(f32[8,32,128]{2,1,0:T(8,128)} %shard_map.144), calls=%async_computation.3 | async-start | bytes 262144 | tf_op jit(solution)/shard_map/all_to_all | solution.py:467
  110.6 30.5 %collective-permute-start.4 = (f32[8,64,128]{2,1,0:T(8,128)}, f32[8,64,128]{2,1,0:T(8,128)}, u32[]{:S(2)}, u32[]{:S(2)}) collective-permute-start(f32[8,64,128]{2,1,0:T(8,128)} %get-tuple-element.12), channel_id=1, source_target_pairs={{0,1},{1,2},{2,3},{3,4},{4,5},{5,6},{6,7},{8,9},{9,10},{10,11},{11... | collective-permute-start | bytes 786440 | tf_op jit(solution)/shard_map/ppermute | solution.py:355
  113.8 27.3 %collective-permute-start.5 = (f32[8,64,128]{2,1,0:T(8,128)}, f32[8,64,128]{2,1,0:T(8,128)}, u32[]{:S(2)}, u32[]{:S(2)}) collective-permute-start(f32[8,64,128]{2,1,0:T(8,128)} %get-tuple-element.13), channel_id=1, source_target_pairs={{1,0},{2,1},{3,2},{4,3},{5,4},{6,5},{7,6},{9,8},{10,9},{11,10},{12... | collective-permute-start | bytes 786440 | tf_op jit(solution)/shard_map/ppermute | solution.py:355
  118.4 34.1 %copy-start.2 = (bf16[8,384,512]{2,1,0:T(8,128)(2,1)S(1)}, bf16[8,384,512]{2,1,0:T(8,128)(2,1)}, u32[]{:S(2)}) copy-start(bf16[8,384,512]{2,1,0:T(8,128)(2,1)} %constant.64.clone.high_ref) | copy-start | bytes 9437188
  126.2 26.4 %all-to-all-start.4 = ((f32[32,16,128]{2,1,0:T(8,128)}), f32[32,16,128]{2,1,0:T(8,128)S(1)}, u32[]{:S(2)}, u32[]{:S(2)}) async-start(f32[32,16,128]{2,1,0:T(8,128)} %copy-done.5), calls=%async_computation.4 | async-start | bytes 524288 | tf_op jit(solution)/shard_map/all_to_all | solution.py:479
  136.7 21.6 %collective-permute-start.8 = (f32[2,8,64,128]{3,2,1,0:T(8,128)}, f32[2,8,64,128]{3,2,1,0:T(8,128)}, u32[]{:S(2)}, u32[]{:S(2)}) collective-permute-start(f32[2,8,64,128]{3,2,1,0:T(8,128)} %copy-done.9), channel_id=1, source_target_pairs={{8,0},{16,8},{24,16},{32,24},{40,32},{48,40},{56,48},{9,1},{17,9},... | collective-permute-start | bytes 1572872 | tf_op jit(solution)/shard_map/ppermute | solution.py:355
  138.7 19.6 %collective-permute-start.6 = (f32[2,8,64,128]{3,2,1,0:T(8,128)}, f32[2,8,64,128]{3,2,1,0:T(8,128)}, u32[]{:S(2)}, u32[]{:S(2)}) collective-permute-start(f32[2,8,64,128]{3,2,1,0:T(8,128)} %copy-done.9), channel_id=1, source_target_pairs={{0,8},{8,16},{16,24},{24,32},{32,40},{40,48},{48,56},{1,9},{9,17},... | collective-permute-start | bytes 1572872 | tf_op jit(solution)/shard_map/ppermute | solution.py:355
  143.0 15.3 %collective-permute-start.9 = (f32[2,8,64,128]{3,2,1,0:T(8,128)}, f32[2,8,64,128]{3,2,1,0:T(8,128)}, u32[]{:S(2)}, u32[]{:S(2)}) collective-permute-start(f32[2,8,64,128]{3,2,1,0:T(8,128)} %pad_maximum_fusion), channel_id=1, source_target_pairs={{8,0},{16,8},{24,16},{32,24},{40,32},{48,40},{56,48},{9,1},{17,9},... | collective-permute-start | bytes 1572872 | tf_op jit(solution)/shard_map/ppermute | solution.py:355
  146.2 12.2 %collective-permute-start.7 = (f32[2,8,64,128]{3,2,1,0:T(8,128)}, f32[2,8,64,128]{3,2,1,0:T(8,128)}, u32[]{:S(2)}, u32[]{:S(2)}) collective-permute-start(f32[2,8,64,128]{3,2,1,0:T(8,128)} %pad_maximum_fusion), channel_id=1, source_target_pairs={{0,8},{8,16},{16,24},{24,32},{32,40},{40,48},{48,56},{1,9},{9,17},... | collective-permute-start | bytes 1572872 | tf_op jit(solution)/shard_map/ppermute | solution.py:355
  154.9 10.1 %all-to-all-start.5 = ((f32[4,128,128]{2,1,0:T(8,128)}), f32[4,128,128]{2,1,0:T(8,128)S(1)}, u32[]{:S(2)}, u32[]{:S(2)}) async-start(f32[4,128,128]{2,1,0:T(8,128)} %copy-done.6), calls=%async_computation.5 | async-start | bytes 524288 | tf_op jit(solution)/shard_map/all_to_all | solution.py:494
  (12 other events, 58.9 us)

commit v2 on v1

v2 whole, which is shorter than its diff:
```python
import functools

import jax
import jax.numpy as jnp
import ml_dtypes
import numpy as np
from jax import lax
from jax.experimental import pallas as pl
from jax.experimental.pallas import tpu as pltpu
from jax.sharding import PartitionSpec as P

WAVES = 32
HALO = 64
TR = 64
TC = 128
NR = 512
NC = 1024
NW = 4
NROW = 8
NCOL = 8
LW = WAVES // NW
QC = TC // NW
KB = NR // (NCOL * NW)
STEP = 2
HALO_BYTES = 1 << 27
ROOT = float(np.sqrt(0.5))
F32 = jnp.float32
BF16 = jnp.bfloat16
VMEM_LIMIT = 20 * 1024 * 1024


def halves_of(table):
    high = table.astype(ml_dtypes.bfloat16)
    low = (table - high.astype(np.float64)).astype(ml_dtypes.bfloat16)
    return high, low


@functools.lru_cache(None)
def row_dft_table():
    group, block, inner = np.meshgrid(np.arange(4), np.arange(NROW), np.arange(16), indexing="ij")
    rows = (TR * block + 16 * group + inner).reshape(-1)
    angle = 2 * np.pi * (np.arange(NR)[:, None] * rows[None, :] % NR) / NR
    return halves_of(np.concatenate([np.cos(angle), -np.sin(angle)], axis=1))


@functools.lru_cache(None)
def col_dft_table():
    freq = (8 * np.arange(128)[None, :] + np.arange(8)[:, None])[:, None, :]
    angle = 2 * np.pi * (np.arange(128)[None, :, None] * freq % NC) / NC
    return halves_of(np.concatenate([np.cos(angle), np.sin(angle)], axis=2))


@functools.lru_cache(None)
def col_inverse_table():
    freq = (8 * np.arange(128)[None, :] + np.arange(8)[:, None])[:, :, None]
    angle = 2 * np.pi * (np.arange(128)[None, None, :] * freq % NC) / NC
    return halves_of(np.concatenate([np.cos(angle), np.sin(angle)], axis=2))


@functools.lru_cache(None)
def column_order():
    table = np.zeros((128, 128))
    for m in range(16):
        for n in range(8):
            table[8 * m + n, 16 * n + m] = 1.0
    return table.astype(ml_dtypes.bfloat16)


@functools.lru_cache(None)
def row_inverse_table():
    rows = TR * np.arange(NROW)[:, None] + np.arange(TR)[None, :]
    angle = 2 * np.pi * (rows[:, :, None] * np.arange(NR)[None, None, :] % NR) / NR
    return halves_of(np.concatenate([np.cos(angle), np.sin(angle)], axis=1))


def split(values):
    high = values.astype(BF16)
    return high, (values - high.astype(F32)).astype(BF16)


def mm(left, right):
    return jnp.dot(left, right, preferred_element_type=F32)


def mm3(left, right):
    rows = left[0].shape[0]
    most = mm(jnp.concatenate(left, axis=0), right[0])
    return most[:rows] + (most[rows:] + mm(left[0], right[1]))


def three(values):
    high = values.astype(BF16)
    middle, low = split(values - high.astype(F32))
    return high, middle, low


def lane_ids(rows, lanes=128):
    return lax.broadcasted_iota(jnp.int32, (rows, lanes), 1)


def swapped(values):
    return pltpu.roll(values, 64, 1)


def column_taps(base):
    wide = jnp.broadcast_to(base, (128, 256))
    own = pltpu.roll(wide, 0, 1, stride=1, stride_axis=0)[:, :128]
    left = pltpu.roll(wide[:64], 256 - 64, 1, stride=1, stride_axis=0)[:, :128]
    right = pltpu.roll(wide[:64], 128, 1, stride=1, stride_axis=0)[:, :128]
    return jnp.concatenate([own, left, right], axis=0)


def row_taps(base):
    wide = jnp.broadcast_to(base, (64, 256))
    return pltpu.roll(wide, 64, 1, stride=1, stride_axis=0)[:, :192]


def column_pass(parts_re, parts_im, table):
    rows = parts_re[0].shape[0]
    field = jnp.concatenate(
        [jnp.concatenate(parts_re, axis=1), jnp.concatenate(parts_im, axis=1)], axis=0
    )
    mix = mm3(split(field), table)
    return (
        mix[:rows, :128] - mix[rows:, 128:],
        mix[:rows, 128:] + mix[rows:, :128],
    )


def row_pass(stacked, table):
    mix = mm3(table, split(stacked))
    return mix[:64, :128] - mix[64:, 128:], mix[:64, 128:] + mix[64:, :128]


def over_waves(step):
    def body(start, carry):
        for wave in range(STEP):
            step(start * STEP + wave)
        return carry

    lax.fori_loop(0, LW // STEP, body, 0)


def edges(re_part, im_part):
    lane = lane_ids(re_part.shape[0])
    return (
        jnp.where(lane < 64, re_part, swapped(im_part)),
        jnp.where(lane < 64, swapped(re_part), im_part),
    )


def halo_parts(from_left, from_right):
    lane = lane_ids(from_left.shape[0])
    return (
        jnp.where(lane < 64, from_left, swapped(from_right)),
        jnp.where(lane < 64, swapped(from_left), from_right),
    )


def quarter(block, which):
    lane = lane_ids(16)
    out = jnp.zeros((16, 128), F32)
    for group in range(4):
        amount = lax.rem(32 * group - 32 * which + 128, 128)
        moved = pltpu.roll(block[16 * group : 16 * group + 16], amount, 1)
        out = jnp.where(lane // 32 == group, moved, out)
    return out


def fetch(pairs, sems):
    copies = [
        pltpu.make_async_copy(source, target, sems.at[i])
        for i, (source, target) in enumerate(pairs)
    ]
    for copy in copies:
        copy.start()
    return copies


def load_kernel(place_ref, table_ref, out_ref, sems):
    for copy in fetch([(table_ref.at[place_ref[0]], out_ref)], sems):
        copy.wait()


def pack_kernel(field_ref, held_ref, left_ref, right_ref, sems):
    copies = fetch([(field_ref.at[:, wave], held_ref.at[:, wave]) for wave in range(LW)], sems)
    for wave in range(LW):
        copies[wave].wait()
        left, right = edges(held_ref[0, wave], held_ref[1, wave])
        left_ref[wave] = left
        right_ref[wave] = right


def mirror_kernel(
    place_ref, measured_ref, spec_ref, after_ref, share_ref, mirror_ref, first_ref,
    measured_in, spec_in, sems,
):
    copies = fetch([(spec_ref, spec_in), (measured_ref, measured_in)], sems)
    place = place_ref[0]
    row = lax.broadcasted_iota(jnp.int32, (16, 64), 0)
    pick = (lane_ids(16, 64) == 64 - KB * place - row).astype(BF16)
    copies[0].wait()
    start = pl.multiple_of(place * KB, KB)
    for part in range(2):
        mirror_ref[part] = sum(mm(pick, piece) for piece in three(spec_in[part]))
        first_ref[part] = spec_in[part, 0:8]
        share_ref[16 + 16 * part : 32 + 16 * part] = spec_in[part, pl.ds(start, KB)]
    copies[1].wait()
    share_ref[0:16] = quarter(measured_in[...], place)


def share_kernel(place_ref, share_ref, mirror_ref, first_ref, out_ref):
    place = place_ref[0]
    top = lax.broadcasted_iota(jnp.int32, (16, 128), 0) == 0
    rows = [share_ref[...]]
    for part in range(2):
        other = jnp.broadcast_to(first_ref[part, 0:1], (16, 128))
        rows.append(jnp.where(jnp.logical_and(top, place == 0), other, mirror_ref[part]))
    out_ref[...] = jnp.broadcast_to(jnp.concatenate(rows, axis=0)[None], out_ref.shape)


def order_kernel(rows_ref, order_ref, reverse_ref, out_ref):
    order, reverse = order_ref[...], reverse_ref[...]
    lane = lane_ids(64) // 16
    parts = []
    for row in range(NROW):
        parts.append(sum(mm(piece, order) for piece in three(rows_ref[row, 16:80])))
    ordered = []
    for n in range(8):
        out = jnp.zeros((64, 128), F32)
        for row in range(NROW):
            moved = pltpu.roll(parts[row], (16 * (row - n)) % 128, 1)
            out = jnp.where(lane == row, moved, out)
        ordered.append(out)
    for n in range(8):
        back = sum(mm(piece, reverse) for piece in three(ordered[(8 - n) % 8][32:]))
        if n == 0:
            back = pltpu.roll(back, 1, 1)
        out_ref[n, 0:16] = 0.5 * (ordered[n][0:16] + back[0:16])
        out_ref[n, 16:32] = 0.5 * (ordered[n][16:32] - back[16:32])


def column_tables(base_re_ref, base_im_ref, high_ref, low_ref):
    for wave in range(LW):
        high_ref[wave], low_ref[wave] = split(
            jnp.concatenate(
                [column_taps(base_re_ref[wave]), column_taps(base_im_ref[wave])], axis=1
            )
        )


def row_tables(base_re_ref, base_im_ref, high_ref, low_ref):
    for wave in range(LW):
        high_ref[wave], low_ref[wave] = split(
            jnp.concatenate([row_taps(base_re_ref[wave]), row_taps(base_im_ref[wave])], axis=0)
        )


def columns_kernel(
    field_ref, left_ref, right_ref, base_re_ref, base_im_ref, after_ref, out_ref, high_ref, low_ref
):
    column_tables(base_re_ref, base_im_ref, high_ref, low_ref)

    def step(wave):
        halo_re, halo_im = halo_parts(left_ref[wave], right_ref[wave])
        out_ref[0, wave], out_ref[1, wave] = column_pass(
            (field_ref[0, wave], halo_re),
            (field_ref[1, wave], halo_im),
            (high_ref[wave], low_ref[wave]),
        )

    over_waves(step)


def stacked_rows(refs, wave):
    return jnp.concatenate(
        [jnp.concatenate([ref[0, wave], ref[1, wave]], axis=1) for ref in refs], axis=0
    )


def rows_kernel(
    weight_ref, up_ref, own_ref, down_ref, base_re_ref, base_im_ref,
    out_ref, left_ref, right_ref, share_ref, total_ref, high_ref, low_ref,
):
    row_tables(base_re_ref, base_im_ref, high_ref, low_ref)
    total_ref[...] = jnp.zeros_like(total_ref)

    def step(wave):
        re_out, im_out = row_pass(
            stacked_rows((up_ref, own_ref, down_ref), wave), (high_ref[wave], low_ref[wave])
        )
        out_ref[0, wave] = re_out
        out_ref[1, wave] = im_out
        left, right = edges(re_out, im_out)
        left_ref[wave] = left
        right_ref[wave] = right
        total_ref[...] += weight_ref[wave] * (re_out * re_out + im_out * im_out)

    over_waves(step)
    block = total_ref[...] * (1.0 / WAVES)
    for target in range(NW):
        piece = quarter(block, target)
        share_ref[target * NROW : (target + 1) * NROW] = jnp.broadcast_to(
            piece[None], (NROW, 16, 128)
        )


def row_dft_kernel(image_ref, measured_ref, table_ref, out_ref):
    summed = image_ref[0:NROW] + image_ref[NROW : 2 * NROW]
    summed = summed + image_ref[2 * NROW : 3 * NROW]
    summed = (summed + image_ref[3 * NROW : 4 * NROW]).reshape(128, 128)
    known = measured_ref[:, 0:16].reshape(128, 128)
    lane = lane_ids(128) // 32
    top = []
    low = []
    for group in range(4):
        first = pltpu.roll(summed, (128 - 32 * group) % 128, 1)
        third = pltpu.roll(known, (192 - 32 * group) % 128, 1)
        both = jnp.where(lane == 0, first, jnp.where(lane == 2, third, 0.0))
        top.append(both)
        low.append(pltpu.roll(both, 32, 1))
    operand = split(jnp.concatenate(top + low, axis=0))
    out_ref[...] = mm3((table_ref[0], table_ref[1]), operand).reshape(out_ref.shape)


def eight_point(terms, sign):
    if len(terms) == 1:
        return terms
    count = len(terms)
    even = eight_point(terms[0::2], sign)
    odd = eight_point(terms[1::2], sign)
    first, second = [], []
    for n in range(count // 2):
        re_part, im_part = odd[n]
        im_part = im_part if sign > 0 else -im_part
        turn = 8 * n // count
        if turn == 1:
            re_part, im_part = (re_part - im_part) * ROOT, (re_part + im_part) * ROOT
        elif turn == 2:
            re_part, im_part = -im_part, re_part
        elif turn == 3:
            re_part, im_part = -(re_part + im_part) * ROOT, (re_part - im_part) * ROOT
        im_part = im_part if sign > 0 else -im_part
        first.append((even[n][0] + re_part, even[n][1] + im_part))
        second.append((even[n][0] - re_part, even[n][1] - im_part))
    return first + second


def filter_kernel(rows_ref, spec_ref, table_ref, out_ref):
    lane = lane_ids(16) // 32
    blocks = []
    for col in range(NCOL):
        channels = []
        for channel in range(4):
            piece = jnp.zeros((16, 128), F32)
            for wave in range(NW):
                moved = pltpu.roll(rows_ref[col * NW + wave], (32 * (wave - channel)) % 128, 1)
                piece = jnp.where(lane == wave, moved, piece)
            channels.append(piece)
        blocks.append(
            (
                jnp.concatenate([channels[0], channels[2]], axis=0),
                jnp.concatenate([channels[1], channels[3]], axis=0),
            )
        )
    sums = eight_point(blocks, -1)
    scale = 1.0 / (NR * NC)
    back = []
    for n in range(8):
        operand = split(jnp.concatenate(sums[n], axis=0))
        mix = mm3(operand, (table_ref[0, n], table_ref[1, n]))
        freq_re = mix[:32, :128] + mix[32:, 128:]
        freq_im = mix[32:, :128] - mix[:32, 128:]
        image_re, known_re = freq_re[:16], freq_re[16:]
        image_im, known_im = freq_im[:16], freq_im[16:]
        spec_re, spec_im = spec_ref[n, 0:16], spec_ref[n, 16:32]
        blur_re = image_re * spec_re - image_im * spec_im
        blur_im = image_re * spec_im + image_im * spec_re
        rest_re = blur_re - known_re
        rest_im = blur_im - known_im
        pull_re = rest_re * spec_re + rest_im * spec_im
        pull_im = rest_im * spec_re - rest_re * spec_im
        both = jnp.concatenate([blur_re - pull_im, blur_im + pull_re], axis=0) * scale
        mix = mm3(split(both), (table_ref[2, n], table_ref[3, n]))
        back.append((mix[:16, :128] - mix[16:, 128:], mix[:16, 128:] + mix[16:, :128]))
    columns = eight_point(back, 1)
    for col in range(NCOL):
        left, right = edges(*columns[col])
        out_ref[col * NW + 1] = left
        out_ref[(col + 7) % 8 * NW + 3] = left
        out_ref[(col + 1) % 8 * NW] = right
        out_ref[col * NW + 2] = right


def halo_kernel(left_ref, right_ref, out_ref):
    for wave in range(LW):
        out_ref[0, wave], out_ref[1, wave] = halo_parts(left_ref[wave], right_ref[wave])


def row_inverse_kernel(rows_ref, table_ref, after_ref, out_ref):
    operand = split(rows_ref[...].reshape(NR, 128))
    mix = mm3((table_ref[0], table_ref[1]), operand)
    cos_part, sin_part = mix[:64], mix[64:]
    pulled = sin_part + swapped(cos_part)
    blurred = cos_part - swapped(sin_part)
    both = jnp.where(lane_ids(64) < 64, pulled, swapped(blurred))
    out_ref[...] = jnp.broadcast_to(both[None], out_ref.shape)


def back_columns_kernel(
    images_ref, measured_ref, field_ref, halo_ref, base_re_ref, base_im_ref,
    out_ref, residual_ref, centre_ref, border_ref, high_ref, low_ref,
):
    column_tables(base_re_ref, base_im_ref, high_ref, low_ref)
    low = lane_ids(64) < 64
    first, second = images_ref[1], images_ref[2]
    centre_ref[...] = jnp.where(low, first, swapped(second))
    residual_ref[...] = jnp.where(low, swapped(first), second) - measured_ref[...]
    border_ref[...] = jnp.where(low, images_ref[0], swapped(images_ref[3]))

    def step(wave):
        centre, border = centre_ref[...], border_ref[...]
        out_ref[0, wave], out_ref[1, wave] = column_pass(
            (field_ref[0, wave] * centre, halo_ref[0, wave] * border),
            (-field_ref[1, wave] * centre, -halo_ref[1, wave] * border),
            (high_ref[wave], low_ref[wave]),
        )

    over_waves(step)


def back_rows_kernel(
    weight_ref, up_ref, own_ref, down_ref, base_re_ref, base_im_ref, out_ref, high_ref, low_ref
):
    row_tables(base_re_ref, base_im_ref, high_ref, low_ref)

    def step(wave):
        re_out, im_out = row_pass(
            stacked_rows((up_ref, own_ref, down_ref), wave), (high_ref[wave], low_ref[wave])
        )
        factor = 2.0 * weight_ref[wave]
        out_ref[0, wave] = factor * re_out
        out_ref[1, wave] = -factor * im_out

    over_waves(step)


def params():
    return pltpu.CompilerParams(vmem_limit_bytes=VMEM_LIMIT)


def near(*dims, dtype=F32):
    return pltpu.VMEM(dims, dtype)


def far(*dims, dtype=F32):
    return pltpu.HBM(dims, dtype)


SMEM = pl.BlockSpec(memory_space=pltpu.SMEM)
ANY = pl.BlockSpec(memory_space=pl.ANY)
VM = pl.BlockSpec()


def kept(value):
    return pltpu.with_memory_space_constraint(value, pltpu.HBM)


def loaded(place, table):
    return pl.pallas_call(
        load_kernel,
        in_specs=[SMEM, ANY],
        out_shape=near(*table.shape[1:], dtype=BF16),
        scratch_shapes=[pltpu.SemaphoreType.DMA((1,))],
        compiler_params=params(),
    )(place, kept(jnp.asarray(table)))


def neighbours(value, axis, count, step):
    return lax.ppermute(
        value, axis, [(i, i + step) for i in range(count) if 0 <= i + step < count]
    )


def taps_of(wavelength):
    lane = jnp.arange(256)
    offset = jnp.where(lane < 128, lane, lane - 256).astype(F32)
    spread = jnp.arange(-HALO, HALO + 1).astype(F32)
    norm = 1.0 / jnp.sqrt(jnp.sum(jnp.exp(-2.0 * (spread / HALO) ** 2)))
    amplitude = jnp.where(jnp.abs(offset) <= HALO, jnp.exp(-((offset / HALO) ** 2)) * norm, 0.0)
    phase = offset * offset / (2.0 * wavelength[:, None] * HALO)
    return (amplitude * jnp.cos(phase))[:, None, :], (amplitude * jnp.sin(phase))[:, None, :]


def shards(wavefield, wavelength, weight, spectrum, measured):
    wave_place = lax.axis_index("wave")[None]
    row_place = lax.axis_index("row")[None]
    call = functools.partial(pl.pallas_call, compiler_params=params())
    field, edge, slots = (2, LW, 64, 128), (LW, 64, 128), (NCOL * NW, 16, 128)

    field_held, left_edge, right_edge = call(
        pack_kernel,
        in_specs=[ANY],
        out_shape=(near(*field), far(*edge), far(*edge)),
        scratch_shapes=[pltpu.SemaphoreType.DMA((LW,))],
    )(kept(wavefield))
    from_left = neighbours(right_edge, "col", NCOL, 1)
    from_right = neighbours(left_edge, "col", NCOL, -1)

    base = taps_of(wavelength)
    known_share, mirror, first = call(
        mirror_kernel,
        in_specs=[SMEM, ANY, ANY, ANY],
        out_shape=(near(48, 128), far(2, KB, 128), far(2, 8, 128)),
        scratch_shapes=[
            pltpu.VMEM((64, 128), F32), pltpu.VMEM((2, 64, 128), F32), pltpu.SemaphoreType.DMA((2,)),
        ],
    )(wave_place, kept(measured), kept(spectrum), kept(left_edge))
    mirror = lax.ppermute(mirror, "col", [(i, 7 - i) for i in range(NCOL)])
    first = lax.ppermute(first, "col", [(i, (8 - i) % 8) for i in range(NCOL)])
    known_share = call(share_kernel, in_specs=[SMEM, VM, VM, VM], out_shape=far(NROW, 80, 128))(
        wave_place, known_share, mirror, first
    )
    known = known_share
    known = lax.all_to_all(known, "row", split_axis=0, concat_axis=0, tiled=True)
    spec = call(order_kernel, out_shape=near(8, 32, 128))(
        known, jnp.asarray(column_order()), jnp.asarray(np.eye(128)[::-1].astype(ml_dtypes.bfloat16))
    )

    col_scratch = [pltpu.VMEM((LW, 256, 256), BF16)] * 2
    row_scratch = [pltpu.VMEM((LW, 128, 192), BF16)] * 2
    middle = call(
        columns_kernel,
        in_specs=[VM] * 5 + [ANY],
        out_shape=near(*field),
        scratch_shapes=col_scratch,
    )(field_held, from_left, from_right, *base, kept(known_share))
    from_up = neighbours(middle, "row", NROW, 1)
    from_down = neighbours(middle, "row", NROW, -1)
    propagated, left_edge, right_edge, shares = call(
        rows_kernel,
        in_specs=[SMEM] + [VM] * 5,
        out_shape=(near(*field), far(*edge), far(*edge), far(*slots)),
        scratch_shapes=[pltpu.VMEM((64, 128), F32)] + row_scratch,
    )(weight, from_up, middle, from_down, *base)

    prop_left = neighbours(right_edge, "col", NCOL, 1)
    prop_right = neighbours(left_edge, "col", NCOL, -1)
    prop_halo = call(
        halo_kernel,
        out_shape=near(*field),
        cost_estimate=pl.CostEstimate(flops=0, bytes_accessed=HALO_BYTES, transcendentals=0),
    )(prop_left, prop_right)

    image = lax.all_to_all(shares, ("wave", "row"), split_axis=0, concat_axis=0, tiled=True)
    first_place = jnp.zeros((1,), jnp.int32)
    row_dft = loaded(first_place, np.stack(row_dft_table())[None])
    freq_rows = call(row_dft_kernel, out_shape=far(*slots))(image, known, row_dft)
    freq_rows = lax.all_to_all(freq_rows, ("col", "wave"), split_axis=0, concat_axis=0, tiled=True)

    col_dft = loaded(first_place, np.stack(col_dft_table() + col_inverse_table())[None])
    columns = call(filter_kernel, out_shape=far(*slots))(freq_rows, spec, col_dft)
    columns = lax.all_to_all(columns, ("col", "wave"), split_axis=0, concat_axis=0, tiled=True)

    row_back = loaded(row_place, np.stack(row_inverse_table(), axis=1))
    images = call(row_inverse_kernel, in_specs=[VM, VM, ANY], out_shape=far(NW, 64, 128))(
        columns, row_back, prop_halo
    )
    images = lax.all_to_all(images, "wave", split_axis=0, concat_axis=0, tiled=True)

    middle, residual = call(
        back_columns_kernel,
        out_shape=(near(*field), far(64, 128)),
        scratch_shapes=[pltpu.VMEM((64, 128), F32)] * 2 + col_scratch,
    )(images, measured, propagated, prop_halo, *base)
    from_up = neighbours(middle, "row", NROW, 1)
    from_down = neighbours(middle, "row", NROW, -1)
    field_grad = call(
        back_rows_kernel,
        in_specs=[SMEM] + [VM] * 5,
        out_shape=far(*field),
        scratch_shapes=row_scratch,
    )(weight, from_up, middle, from_down, *base)
    return field_grad, residual


def solution(mesh):
    placed = (
        P(None, "wave", "row", "col"),
        P("wave"),
        P("wave"),
        P(None, "col", "row"),
        P("row", "col"),
    )
    return jax.shard_map(
        shards,
        mesh=mesh,
        in_specs=placed,
        out_specs=(P(None, "wave", "row", "col"), P("row", "col")),
        check_vma=False,
    )
```

time: 177 us -> 158 us (0.89)
  the two profiles are of different devices: /device:TPU:32 before, /device:TPU:25 now
where the time goes in v2:
time: 158 us; the launch traced here: 157 us
  starting transfers between devices  67.7 us (43%)
  waiting for transfers between devices  51.8 us (33%)
  Pallas kernels  25.5 us (16%)
  blocking collectives  8.78 us (6%)
  other arithmetic  1.63 us (1%)
    ppermute x8, starting transfers between devices, neighbours(): lax.ppermute(value, axis, [(i, i + step) for i in range(count) if 0 <= i...  33.1 us
    ppermute x8, waiting for transfers between devices, neighbours(): lax.ppermute(value, axis, [(i, i + step) for i in range(count) if 0 <= i...  28.2 us
    all_to_all x1, waiting for transfers between devices, shards(): lax.all_to_all(shares, ('wave', 'row'), split_axis=0, concat_axis=0, tile...  9.67 us
    all_to_all x1, waiting for transfers between devices, shards(): lax.all_to_all(freq_rows, ('col', 'wave'), split_axis=0, concat_axis=0, t...  9.21 us
    all_to_all x1, blocking collectives, shards(): lax.all_to_all(images, 'wave', split_axis=0, concat_axis=0, tiled=True)  8.78 us
    all_to_all x1, starting transfers between devices, shards(): lax.all_to_all(known, 'row', split_axis=0, concat_axis=0, tiled=True)  8.28 us
    ppermute x1, starting transfers between devices, shards(): mirror = lax.ppermute(mirror, 'col', [(i, 7 - i) for i in range(NCOL)])  7.11 us
    all_to_all x1, starting transfers between devices, shards(): lax.all_to_all(shares, ('wave', 'row'), split_axis=0, concat_axis=0, tile...  6.37 us
  transfers between devices with their start and end apart: 14, of which 9 were waited for; matrix products, arithmetic and copies ran while one was open for 1% of the time, Pallas kernels for 8%

profile of v2, /device:TPU:25, one launch (start us, length us, event | category | flops | bytes accessed | tf_op | source)
XLA Modules:
  0.0 157.1 jit_solution(13046775299227385428)
XLA Ops:
  0.6 2.4 %shard_map.113 = (f32[2,8,64,128]{3,2,1,0:T(8,128)S(1)}, f32[8,64,128]{2,1,0:T(8,128)}, f32[8,64,128]{2,1,0:T(8,128)}) custom-call(f32[2,8,64,128]{3,2,1,0:T(8,128)} %field_ref.1), custom_call_target="tpu_custom_call" | custom-call | tf_op jit(solution)/shard_map/pallas_call | solution.py:501
  3.0 2.4 %collective-permute-start.1 = (f32[8,64,128]{2,1,0:T(8,128)}, f32[8,64,128]{2,1,0:T(8,128)S(1)}, u32[]{:S(2)}, u32[]{:S(2)}) collective-permute-start(f32[8,64,128]{2,1,0:T(8,128)} %get-tuple-element.16.after_ref), channel_id=1, source_target_pairs={{1,0},{2,1},{3,2},{4,3},{5,4},{6,5},{7,6},{9,8},{10,9},{11,10},{12... | collective-permute-start | bytes 786440 | tf_op jit(solution)/shard_map/ppermute | solution.py:480
  7.1 7.1 %collective-permute-start.2 = (f32[2,16,128]{2,1,0:T(8,128)}, f32[2,16,128]{2,1,0:T(8,128)S(1)}, u32[]{:S(2)}, u32[]{:S(2)}) collective-permute-start(f32[2,16,128]{2,1,0:T(8,128)} %get-tuple-element.18), channel_id=1, source_target_pairs={{0,7},{1,6},{2,5},{3,4},{4,3},{5,2},{6,1},{7,0},{8,15},{9,14},{10,... | collective-permute-start | bytes 49160 | tf_op jit(solution)/shard_map/ppermute | solution.py:519
  14.2 2.2 %collective-permute-start.3 = (f32[2,8,128]{2,1,0:T(8,128)}, f32[2,8,128]{2,1,0:T(8,128)S(1)}, u32[]{:S(2)}, u32[]{:S(2)}) collective-permute-start(f32[2,8,128]{2,1,0:T(8,128)} %get-tuple-element.19), channel_id=1, source_target_pairs={{0,0},{1,7},{2,6},{3,5},{4,4},{5,3},{6,2},{7,1},{8,8},{9,15},{10,1... | collective-permute-start | bytes 24584 | tf_op jit(solution)/shard_map/ppermute | solution.py:520
  20.3 4.8 %collective-permute-done.3.first_ref = f32[2,8,128]{2,1,0:T(8,128)S(1)} collective-permute-done((f32[2,8,128]{2,1,0:T(8,128)}, f32[2,8,128]{2,1,0:T(8,128)S(1)}, u32[]{:S(2)}, u32[]{:S(2)}) %collective-permute-start.3) | collective-permute-done | bytes 8224 | tf_op jit(solution)/shard_map/ppermute | solution.py:520
  25.8 8.3 %all-to-all-start.1 = ((f32[8,80,128]{2,1,0:T(8,128)}), f32[8,80,128]{2,1,0:T(8,128)S(1)}, u32[]{:S(2)}, u32[]{:S(2)}) async-start(f32[8,80,128]{2,1,0:T(8,128)} %shard_map.115.after_ref), calls=%async_computation.1 | async-start | bytes 655360 | tf_op jit(solution)/shard_map/all_to_all | solution.py:525
  36.3 3.5 %collective-permute-start.4 = (f32[2,8,64,128]{3,2,1,0:T(8,128)S(1)}, f32[2,8,64,128]{3,2,1,0:T(8,128)S(1)}, u32[]{:S(2)}, u32[]{:S(2)}) collective-permute-start(f32[2,8,64,128]{3,2,1,0:T(8,128)S(1)} %shard_map.116.own_ref), channel_id=1, source_target_pairs={{0,8},{8,16},{16,24},{24,32},{32,40},{40,48},{48,56},{1,9},{9,17},... | collective-permute-start | bytes 1572872 | tf_op jit(solution)/shard_map/ppermute | solution.py:480
  41.8 4.2 %collective-permute-done.4.up_ref = f32[2,8,64,128]{3,2,1,0:T(8,128)S(1)} collective-permute-done((f32[2,8,64,128]{3,2,1,0:T(8,128)S(1)}, f32[2,8,64,128]{3,2,1,0:T(8,128)S(1)}, u32[]{:S(2)}, u32[]{:S(2)}) %collective-permute-start.4) | collective-permute-done | bytes 524320 | tf_op jit(solution)/shard_map/ppermute | solution.py:480
  46.0 4.4 %collective-permute-done.5.down_ref = f32[2,8,64,128]{3,2,1,0:T(8,128)S(1)} collective-permute-done((f32[2,8,64,128]{3,2,1,0:T(8,128)S(1)}, f32[2,8,64,128]{3,2,1,0:T(8,128)S(1)}, u32[]{:S(2)}, u32[]{:S(2)}) %collective-permute-start.5) | collective-permute-done | bytes 524320 | tf_op jit(solution)/shard_map/ppermute | solution.py:480
  50.4 3.2 %shard_map.117 = (f32[2,8,64,128]{3,2,1,0:T(8,128)S(1)}, f32[8,64,128]{2,1,0:T(8,128)}, f32[8,64,128]{2,1,0:T(8,128)}, f32[32,16,128]{2,1,0:T(8,128)}) custom-call(f32[8]{0:T(128)S(1)} %copy-done.3, f32[2,8,64,128]{3,2,1,0:T(8,128)S(1)} %collective-permute-done.4.up_ref, f32[2,8,64,128]{3,2,1,0:T(8,128)S(1)} %shard_map.116.own_ref, ...), custom_call_target="tpu_custom_call" | custom-call | tf_op jit(solution)/shard_map/pallas_call | solution.py:540
  53.5 6.4 %all-to-all-start = ((f32[32,16,128]{2,1,0:T(8,128)}), f32[32,16,128]{2,1,0:T(8,128)S(1)}, u32[]{:S(2)}, u32[]{:S(2)}) async-start(f32[32,16,128]{2,1,0:T(8,128)} %get-tuple-element.20), calls=%async_computation | async-start | bytes 524288 | tf_op jit(solution)/shard_map/all_to_all | solution.py:555
  61.5 9.7 %all-to-all-done.image_ref = f32[32,16,128]{2,1,0:T(8,128)S(1)} async-done(((f32[32,16,128]{2,1,0:T(8,128)}), f32[32,16,128]{2,1,0:T(8,128)S(1)}, u32[]{:S(2)}, u32[]{:S(2)}) %all-to-all-start) | async-done | bytes 262176 | tf_op jit(solution)/shard_map/all_to_all | solution.py:555
  73.1 5.7 %all-to-all-start.2 = ((f32[32,16,128]{2,1,0:T(8,128)}), f32[32,16,128]{2,1,0:T(8,128)S(1)}, u32[]{:S(2)}, u32[]{:S(2)}) async-start(f32[32,16,128]{2,1,0:T(8,128)} %shard_map.119), calls=%async_computation.2 | async-start | bytes 524288 | tf_op jit(solution)/shard_map/all_to_all | solution.py:559
  81.3 9.2 %all-to-all-done.2.rows_ref = f32[32,16,128]{2,1,0:T(8,128)S(1)} async-done(((f32[32,16,128]{2,1,0:T(8,128)}), f32[32,16,128]{2,1,0:T(8,128)S(1)}, u32[]{:S(2)}, u32[]{:S(2)}) %all-to-all-start.2) | async-done | bytes 262176 | tf_op jit(solution)/shard_map/all_to_all | solution.py:559
  90.5 2.8 %shard_map.122 = f32[32,16,128]{2,1,0:T(8,128)} custom-call(f32[32,16,128]{2,1,0:T(8,128)S(1)} %all-to-all-done.2.rows_ref, f32[8,32,128]{2,1,0:T(8,128)S(1)} %shard_map.120.spec_ref, bf16[4,8,128,256]{3,2,1,0:T(8,128)(2,1)S(1)} %shard_map.121.table_ref), custom_call_target="tpu_custom_call" | custom-call | tf_op jit(solution)/shard_map/pallas_call | solution.py:562
  93.3 4.9 %all-to-all-start.3 = ((f32[32,16,128]{2,1,0:T(8,128)}), f32[32,16,128]{2,1,0:T(8,128)S(1)}, u32[]{:S(2)}, u32[]{:S(2)}) async-start(f32[32,16,128]{2,1,0:T(8,128)} %shard_map.122), calls=%async_computation.3 | async-start | bytes 524288 | tf_op jit(solution)/shard_map/all_to_all | solution.py:563
  98.2 7.0 %collective-permute-start.6 = (f32[8,64,128]{2,1,0:T(8,128)}, f32[8,64,128]{2,1,0:T(8,128)S(1)}, u32[]{:S(2)}, u32[]{:S(2)}) collective-permute-start(f32[8,64,128]{2,1,0:T(8,128)} %get-tuple-element.21), channel_id=1, source_target_pairs={{0,1},{1,2},{2,3},{3,4},{4,5},{5,6},{6,7},{8,9},{9,10},{10,11},{11... | collective-permute-start | bytes 786440 | tf_op jit(solution)/shard_map/ppermute | solution.py:480
  108.1 3.9 %collective-permute-done.6.left_ref = f32[8,64,128]{2,1,0:T(8,128)S(1)} collective-permute-done((f32[8,64,128]{2,1,0:T(8,128)}, f32[8,64,128]{2,1,0:T(8,128)S(1)}, u32[]{:S(2)}, u32[]{:S(2)}) %collective-permute-start.6) | collective-permute-done | bytes 262176 | tf_op jit(solution)/shard_map/ppermute | solution.py:480
  112.1 7.1 %collective-permute-done.7.right_ref = f32[8,64,128]{2,1,0:T(8,128)S(1)} collective-permute-done((f32[8,64,128]{2,1,0:T(8,128)}, f32[8,64,128]{2,1,0:T(8,128)S(1)}, u32[]{:S(2)}, u32[]{:S(2)}) %collective-permute-start.7) | collective-permute-done | bytes 262176 | tf_op jit(solution)/shard_map/ppermute | solution.py:480
  120.4 8.8 %all_to_all.25.images_ref = f32[4,64,128]{2,1,0:T(8,128)S(1)} all-to-all(f32[4,64,128]{2,1,0:T(8,128)} %shard_map.125), channel_id=1, replica_groups=mesh['wave'=4,'row'=8,'col'=8] {'wave'}, dimensions={0} | all-to-all | bytes 262144 | tf_op jit(solution)/shard_map/all_to_all | solution.py:569
  131.3 12.5 %collective-permute-start.8 = (f32[2,8,64,128]{3,2,1,0:T(8,128)S(1)}, f32[2,8,64,128]{3,2,1,0:T(8,128)S(1)}, u32[]{:S(2)}, u32[]{:S(2)}) collective-permute-start(f32[2,8,64,128]{3,2,1,0:T(8,128)S(1)} %get-tuple-element.24.own_ref), channel_id=1, source_target_pairs={{0,8},{8,16},{16,24},{24,32},{32,40},{40,48},{48,56},{1,9},{9,17},... | collective-permute-start | bytes 1572872 | tf_op jit(solution)/shard_map/ppermute | solution.py:480
  145.8 4.2 %collective-permute-done.8.up_ref = f32[2,8,64,128]{3,2,1,0:T(8,128)S(1)} collective-permute-done((f32[2,8,64,128]{3,2,1,0:T(8,128)S(1)}, f32[2,8,64,128]{3,2,1,0:T(8,128)S(1)}, u32[]{:S(2)}, u32[]{:S(2)}) %collective-permute-start.8) | collective-permute-done | bytes 524320 | tf_op jit(solution)/shard_map/ppermute | solution.py:480
  150.0 4.4 %collective-permute-done.9.down_ref = f32[2,8,64,128]{3,2,1,0:T(8,128)S(1)} collective-permute-done((f32[2,8,64,128]{3,2,1,0:T(8,128)S(1)}, f32[2,8,64,128]{3,2,1,0:T(8,128)S(1)}, u32[]{:S(2)}, u32[]{:S(2)}) %collective-permute-start.9) | collective-permute-done | bytes 524320 | tf_op jit(solution)/shard_map/ppermute | solution.py:480
  154.4 2.7 %shard_map.127 = f32[2,8,64,128]{3,2,1,0:T(8,128)} custom-call(f32[8]{0:T(128)S(1)} %copy-done.3, f32[2,8,64,128]{3,2,1,0:T(8,128)S(1)} %collective-permute-done.8.up_ref, f32[2,8,64,128]{3,2,1,0:T(8,128)S(1)} %get-tuple-element.24.own_ref, f32[2,8,64,128]{3,2,1,0:T(8,128)S(1)} %collective-permute-done.9.down_ref, ...), custom_call_target="tpu_custom_call" | custom-call | tf_op jit(solution)/shard_map/pallas_call | solution.py:578
  (32 shorter events, 23.7 us)
Async XLA Ops:
  0.6 49.7 %copy-start.3 = (f32[8]{0:T(128)S(1)}, f32[8]{0:T(128)}, u32[]{:S(2)}) copy-start(f32[8]{0:T(128)} %weight_ref.3) | copy-start | bytes 100
  3.0 31.4 %collective-permute-start.1 = (f32[8,64,128]{2,1,0:T(8,128)}, f32[8,64,128]{2,1,0:T(8,128)S(1)}, u32[]{:S(2)}, u32[]{:S(2)}) collective-permute-start(f32[8,64,128]{2,1,0:T(8,128)} %get-tuple-element.16.after_ref), channel_id=1, source_target_pairs={{1,0},{2,1},{3,2},{4,3},{5,4},{6,5},{7,6},{9,8},{10,9},{11,10},{12... | collective-permute-start | bytes 786440 | tf_op jit(solution)/shard_map/ppermute | solution.py:480
  7.1 18.0 %collective-permute-start.2 = (f32[2,16,128]{2,1,0:T(8,128)}, f32[2,16,128]{2,1,0:T(8,128)S(1)}, u32[]{:S(2)}, u32[]{:S(2)}) collective-permute-start(f32[2,16,128]{2,1,0:T(8,128)} %get-tuple-element.18), channel_id=1, source_target_pairs={{0,7},{1,6},{2,5},{3,4},{4,3},{5,2},{6,1},{7,0},{8,15},{9,14},{10,... | collective-permute-start | bytes 49160 | tf_op jit(solution)/shard_map/ppermute | solution.py:519
  14.2 10.9 %collective-permute-start.3 = (f32[2,8,128]{2,1,0:T(8,128)}, f32[2,8,128]{2,1,0:T(8,128)S(1)}, u32[]{:S(2)}, u32[]{:S(2)}) collective-permute-start(f32[2,8,128]{2,1,0:T(8,128)} %get-tuple-element.19), channel_id=1, source_target_pairs={{0,0},{1,7},{2,6},{3,5},{4,4},{5,3},{6,2},{7,1},{8,8},{9,15},{10,1... | collective-permute-start | bytes 24584 | tf_op jit(solution)/shard_map/ppermute | solution.py:520
  16.4 18.1 %collective-permute-start = (f32[8,64,128]{2,1,0:T(8,128)}, f32[8,64,128]{2,1,0:T(8,128)S(1)}, u32[]{:S(2)}, u32[]{:S(2)}) collective-permute-start(f32[8,64,128]{2,1,0:T(8,128)} %get-tuple-element.15), channel_id=1, source_target_pairs={{0,1},{1,2},{2,3},{3,4},{4,5},{5,6},{6,7},{8,9},{9,10},{10,11},{11... | collective-permute-start | bytes 786440 | tf_op jit(solution)/shard_map/ppermute | solution.py:480
  25.8 27.7 %all-to-all-start.1 = ((f32[8,80,128]{2,1,0:T(8,128)}), f32[8,80,128]{2,1,0:T(8,128)S(1)}, u32[]{:S(2)}, u32[]{:S(2)}) async-start(f32[8,80,128]{2,1,0:T(8,128)} %shard_map.115.after_ref), calls=%async_computation.1 | async-start | bytes 655360 | tf_op jit(solution)/shard_map/all_to_all | solution.py:525
  36.3 9.6 %collective-permute-start.4 = (f32[2,8,64,128]{3,2,1,0:T(8,128)S(1)}, f32[2,8,64,128]{3,2,1,0:T(8,128)S(1)}, u32[]{:S(2)}, u32[]{:S(2)}) collective-permute-start(f32[2,8,64,128]{3,2,1,0:T(8,128)S(1)} %shard_map.116.own_ref), channel_id=1, source_target_pairs={{0,8},{8,16},{16,24},{24,32},{32,40},{40,48},{48,56},{1,9},{9,17},... | collective-permute-start | bytes 1572872 | tf_op jit(solution)/shard_map/ppermute | solution.py:480
  39.9 10.5 %collective-permute-start.5 = (f32[2,8,64,128]{3,2,1,0:T(8,128)S(1)}, f32[2,8,64,128]{3,2,1,0:T(8,128)S(1)}, u32[]{:S(2)}, u32[]{:S(2)}) collective-permute-start(f32[2,8,64,128]{3,2,1,0:T(8,128)S(1)} %shard_map.116.own_ref), channel_id=1, source_target_pairs={{8,0},{16,8},{24,16},{32,24},{40,32},{48,40},{56,48},{9,1},{17,9},... | collective-permute-start | bytes 1572872 | tf_op jit(solution)/shard_map/ppermute | solution.py:480
  53.5 17.7 %all-to-all-start = ((f32[32,16,128]{2,1,0:T(8,128)}), f32[32,16,128]{2,1,0:T(8,128)S(1)}, u32[]{:S(2)}, u32[]{:S(2)}) async-start(f32[32,16,128]{2,1,0:T(8,128)} %get-tuple-element.20), calls=%async_computation | async-start | bytes 524288 | tf_op jit(solution)/shard_map/all_to_all | solution.py:555
  73.1 17.4 %all-to-all-start.2 = ((f32[32,16,128]{2,1,0:T(8,128)}), f32[32,16,128]{2,1,0:T(8,128)S(1)}, u32[]{:S(2)}, u32[]{:S(2)}) async-start(f32[32,16,128]{2,1,0:T(8,128)} %shard_map.119), calls=%async_computation.2 | async-start | bytes 524288 | tf_op jit(solution)/shard_map/all_to_all | solution.py:559
  78.8 1.6 %copy-start.1 = (bf16[128,128]{1,0:T(8,128)(2,1)S(1)}, bf16[128,128]{1,0:T(8,128)(2,1)}, u32[]{:S(2)}) copy-start(bf16[128,128]{1,0:T(8,128)(2,1)} %constant.44.clone.order_ref) | copy-start | bytes 98308
  78.8 1.6 %copy-start.2 = (bf16[128,128]{1,0:T(8,128)(2,1)S(1)}, bf16[128,128]{1,0:T(8,128)(2,1)}, u32[]{:S(2)}) copy-start(bf16[128,128]{1,0:T(8,128)(2,1)} %constant.45.clone.reverse_ref) | copy-start | bytes 98308
  93.3 26.1 %all-to-all-start.3 = ((f32[32,16,128]{2,1,0:T(8,128)}), f32[32,16,128]{2,1,0:T(8,128)S(1)}, u32[]{:S(2)}, u32[]{:S(2)}) async-start(f32[32,16,128]{2,1,0:T(8,128)} %shard_map.122), calls=%async_computation.3 | async-start | bytes 524288 | tf_op jit(solution)/shard_map/all_to_all | solution.py:563
  98.2 13.9 %collective-permute-start.6 = (f32[8,64,128]{2,1,0:T(8,128)}, f32[8,64,128]{2,1,0:T(8,128)S(1)}, u32[]{:S(2)}, u32[]{:S(2)}) collective-permute-start(f32[8,64,128]{2,1,0:T(8,128)} %get-tuple-element.21), channel_id=1, source_target_pairs={{0,1},{1,2},{2,3},{3,4},{4,5},{5,6},{6,7},{8,9},{9,10},{10,11},{11... | collective-permute-start | bytes 786440 | tf_op jit(solution)/shard_map/ppermute | solution.py:480
  105.2 13.9 %collective-permute-start.7 = (f32[8,64,128]{2,1,0:T(8,128)}, f32[8,64,128]{2,1,0:T(8,128)S(1)}, u32[]{:S(2)}, u32[]{:S(2)}) collective-permute-start(f32[8,64,128]{2,1,0:T(8,128)} %get-tuple-element.22), channel_id=1, source_target_pairs={{1,0},{2,1},{3,2},{4,3},{5,4},{6,5},{7,6},{9,8},{10,9},{11,10},{12... | collective-permute-start | bytes 786440 | tf_op jit(solution)/shard_map/ppermute | solution.py:480
  107.2 22.1 %copy-start = (f32[64,128]{1,0:T(8,128)S(1)}, f32[64,128]{1,0:T(8,128)}, u32[]{:S(2)}) copy-start(f32[64,128]{1,0:T(8,128)} %measured_ref.3) | copy-start | bytes 98308
  131.3 18.7 %collective-permute-start.8 = (f32[2,8,64,128]{3,2,1,0:T(8,128)S(1)}, f32[2,8,64,128]{3,2,1,0:T(8,128)S(1)}, u32[]{:S(2)}, u32[]{:S(2)}) collective-permute-start(f32[2,8,64,128]{3,2,1,0:T(8,128)S(1)} %get-tuple-element.24.own_ref), channel_id=1, source_target_pairs={{0,8},{8,16},{16,24},{24,32},{32,40},{40,48},{48,56},{1,9},{9,17},... | collective-permute-start | bytes 1572872 | tf_op jit(solution)/shard_map/ppermute | solution.py:480
  143.9 10.5 %collective-permute-start.9 = (f32[2,8,64,128]{3,2,1,0:T(8,128)S(1)}, f32[2,8,64,128]{3,2,1,0:T(8,128)S(1)}, u32[]{:S(2)}, u32[]{:S(2)}) collective-permute-start(f32[2,8,64,128]{3,2,1,0:T(8,128)S(1)} %get-tuple-element.24.own_ref), channel_id=1, source_target_pairs={{8,0},{16,8},{24,16},{32,24},{40,32},{48,40},{56,48},{9,1},{17,9},... | collective-permute-start | bytes 1572872 | tf_op jit(solution)/shard_map/ppermute | solution.py:480

commit v3 on v2

--- a/solution.py
+++ b/solution.py
@@ -22,7 +22,7 @@
 QC = TC // NW
 KB = NR // (NCOL * NW)
 STEP = 2
-HALO_BYTES = 1 << 27
+LONG = pl.CostEstimate(flops=1 << 50, bytes_accessed=1 << 36, transcendentals=1 << 40)
 ROOT = float(np.sqrt(0.5))
 F32 = jnp.float32
 BF16 = jnp.bfloat16
@@ -397,7 +397,7 @@
         out_ref[0, wave], out_ref[1, wave] = halo_parts(left_ref[wave], right_ref[wave])
 
 
-def row_inverse_kernel(rows_ref, table_ref, after_ref, out_ref):
+def row_inverse_kernel(rows_ref, table_ref, out_ref):
     operand = split(rows_ref[...].reshape(NR, 128))
     mix = mm3((table_ref[0], table_ref[1]), operand)
     cos_part, sin_part = mix[:64], mix[64:]
@@ -549,7 +549,7 @@
     prop_halo = call(
         halo_kernel,
         out_shape=near(*field),
-        cost_estimate=pl.CostEstimate(flops=0, bytes_accessed=HALO_BYTES, transcendentals=0),
+        cost_estimate=LONG,
     )(prop_left, prop_right)
 
     image = lax.all_to_all(shares, ("wave", "row"), split_axis=0, concat_axis=0, tiled=True)
@@ -563,9 +563,7 @@
     columns = lax.all_to_all(columns, ("col", "wave"), split_axis=0, concat_axis=0, tiled=True)
 
     row_back = loaded(row_place, np.stack(row_inverse_table(), axis=1))
-    images = call(row_inverse_kernel, in_specs=[VM, VM, ANY], out_shape=far(NW, 64, 128))(
-        columns, row_back, prop_halo
-    )
+    images = call(row_inverse_kernel, out_shape=far(NW, 64, 128))(columns, row_back)
     images = lax.all_to_all(images, "wave", split_axis=0, concat_axis=0, tiled=True)
 
     middle, residual = call(

time: 158 us -> 148 us (0.937)
  blocking collectives: 8.78 us -> 0 us
  waiting for transfers between devices: 51.8 us -> 46.8 us
  starting transfers between devices: 67.7 us -> 70.3 us
    all_to_all x1 -> x0, blocking collectives: 8.78 us -> none  [shards(): lax.all_to_all(images, 'wave', split_axis=0, concat_axis=0, tiled=True)]
    ppermute x8, waiting for transfers between devices: 28.2 us -> 22.5 us  [neighbours(): lax.ppermute(value, axis, [(i, i + step) for i in range(count) if 0 <= i...]
    all_to_all x0 -> x1, starting transfers between devices: none -> 3.95 us  [shards(): lax.all_to_all(images, 'wave', split_axis=0, concat_axis=0, tiled=True)]
  transfers between devices with their start and end apart: 14 -> 15, of which waited for: 9 -> 9; matrix products, arithmetic and copies ran while one was open for 1% -> 1% of each run, Pallas kernels for 8% -> 9%
where the time goes in v3:
time: 148 us; the launch traced here: 147 us
  starting transfers between devices  70.3 us (48%)
  waiting for transfers between devices  46.8 us (32%)
  Pallas kernels  26.4 us (18%)
  other arithmetic  1.63 us (1%)
  between operations  1.59 us (1%)
    ppermute x8, starting transfers between devices, neighbours(): lax.ppermute(value, axis, [(i, i + step) for i in range(count) if 0 <= i...  31.7 us
    ppermute x8, waiting for transfers between devices, neighbours(): lax.ppermute(value, axis, [(i, i + step) for i in range(count) if 0 <= i...  22.5 us
    all_to_all x1, waiting for transfers between devices, shards(): lax.all_to_all(shares, ('wave', 'row'), split_axis=0, concat_axis=0, tile...  9.67 us
    all_to_all x1, waiting for transfers between devices, shards(): lax.all_to_all(freq_rows, ('col', 'wave'), split_axis=0, concat_axis=0, t...  9.21 us
    all_to_all x1, starting transfers between devices, shards(): lax.all_to_all(known, 'row', split_axis=0, concat_axis=0, tiled=True)  8.28 us
    ppermute x1, starting transfers between devices, shards(): mirror = lax.ppermute(mirror, 'col', [(i, 7 - i) for i in range(NCOL)])  7.1 us
    all_to_all x1, starting transfers between devices, shards(): lax.all_to_all(shares, ('wave', 'row'), split_axis=0, concat_axis=0, tile...  6.39 us
    all_to_all x1, starting transfers between devices, shards(): lax.all_to_all(freq_rows, ('col', 'wave'), split_axis=0, concat_axis=0, t...  5.74 us
  transfers between devices with their start and end apart: 15, of which 9 were waited for; matrix products, arithmetic and copies ran while one was open for 1% of the time, Pallas kernels for 9%

profile of v3, /device:TPU:25, one launch (start us, length us, event | category | flops | bytes accessed | tf_op | source)
XLA Modules:
  0.0 147.4 jit_solution(3789781143415611079)
XLA Ops:
  0.6 2.4 %shard_map.113 = (f32[2,8,64,128]{3,2,1,0:T(8,128)S(1)}, f32[8,64,128]{2,1,0:T(8,128)}, f32[8,64,128]{2,1,0:T(8,128)}) custom-call(f32[2,8,64,128]{3,2,1,0:T(8,128)} %field_ref.1), custom_call_target="tpu_custom_call" | custom-call | tf_op jit(solution)/shard_map/pallas_call | solution.py:501
  3.0 2.4 %collective-permute-start.1 = (f32[8,64,128]{2,1,0:T(8,128)}, f32[8,64,128]{2,1,0:T(8,128)S(1)}, u32[]{:S(2)}, u32[]{:S(2)}) collective-permute-start(f32[8,64,128]{2,1,0:T(8,128)} %get-tuple-element.16.after_ref), channel_id=1, source_target_pairs={{1,0},{2,1},{3,2},{4,3},{5,4},{6,5},{7,6},{9,8},{10,9},{11,10},{12... | collective-permute-start | bytes 786440 | tf_op jit(solution)/shard_map/ppermute | solution.py:480
  7.1 7.1 %collective-permute-start.2 = (f32[2,16,128]{2,1,0:T(8,128)}, f32[2,16,128]{2,1,0:T(8,128)S(1)}, u32[]{:S(2)}, u32[]{:S(2)}) collective-permute-start(f32[2,16,128]{2,1,0:T(8,128)} %get-tuple-element.18), channel_id=1, source_target_pairs={{0,7},{1,6},{2,5},{3,4},{4,3},{5,2},{6,1},{7,0},{8,15},{9,14},{10,... | collective-permute-start | bytes 49160 | tf_op jit(solution)/shard_map/ppermute | solution.py:519
  14.2 2.2 %collective-permute-start.3 = (f32[2,8,128]{2,1,0:T(8,128)}, f32[2,8,128]{2,1,0:T(8,128)S(1)}, u32[]{:S(2)}, u32[]{:S(2)}) collective-permute-start(f32[2,8,128]{2,1,0:T(8,128)} %get-tuple-element.19), channel_id=1, source_target_pairs={{0,0},{1,7},{2,6},{3,5},{4,4},{5,3},{6,2},{7,1},{8,8},{9,15},{10,1... | collective-permute-start | bytes 24584 | tf_op jit(solution)/shard_map/ppermute | solution.py:520
  20.3 4.8 %collective-permute-done.3.first_ref = f32[2,8,128]{2,1,0:T(8,128)S(1)} collective-permute-done((f32[2,8,128]{2,1,0:T(8,128)}, f32[2,8,128]{2,1,0:T(8,128)S(1)}, u32[]{:S(2)}, u32[]{:S(2)}) %collective-permute-start.3) | collective-permute-done | bytes 8224 | tf_op jit(solution)/shard_map/ppermute | solution.py:520
  25.8 8.3 %all-to-all-start.1 = ((f32[8,80,128]{2,1,0:T(8,128)}), f32[8,80,128]{2,1,0:T(8,128)S(1)}, u32[]{:S(2)}, u32[]{:S(2)}) async-start(f32[8,80,128]{2,1,0:T(8,128)} %shard_map.115.after_ref), calls=%async_computation.1 | async-start | bytes 655360 | tf_op jit(solution)/shard_map/all_to_all | solution.py:525
  36.4 3.5 %collective-permute-start.4 = (f32[2,8,64,128]{3,2,1,0:T(8,128)S(1)}, f32[2,8,64,128]{3,2,1,0:T(8,128)S(1)}, u32[]{:S(2)}, u32[]{:S(2)}) collective-permute-start(f32[2,8,64,128]{3,2,1,0:T(8,128)S(1)} %shard_map.116.own_ref), channel_id=1, source_target_pairs={{0,8},{8,16},{16,24},{24,32},{32,40},{40,48},{48,56},{1,9},{9,17},... | collective-permute-start | bytes 1572872 | tf_op jit(solution)/shard_map/ppermute | solution.py:480
  41.8 4.2 %collective-permute-done.4.up_ref = f32[2,8,64,128]{3,2,1,0:T(8,128)S(1)} collective-permute-done((f32[2,8,64,128]{3,2,1,0:T(8,128)S(1)}, f32[2,8,64,128]{3,2,1,0:T(8,128)S(1)}, u32[]{:S(2)}, u32[]{:S(2)}) %collective-permute-start.4) | collective-permute-done | bytes 524320 | tf_op jit(solution)/shard_map/ppermute | solution.py:480
  46.0 4.4 %collective-permute-done.5.down_ref = f32[2,8,64,128]{3,2,1,0:T(8,128)S(1)} collective-permute-done((f32[2,8,64,128]{3,2,1,0:T(8,128)S(1)}, f32[2,8,64,128]{3,2,1,0:T(8,128)S(1)}, u32[]{:S(2)}, u32[]{:S(2)}) %collective-permute-start.5) | collective-permute-done | bytes 524320 | tf_op jit(solution)/shard_map/ppermute | solution.py:480
  50.4 3.2 %shard_map.117 = (f32[2,8,64,128]{3,2,1,0:T(8,128)S(1)}, f32[8,64,128]{2,1,0:T(8,128)}, f32[8,64,128]{2,1,0:T(8,128)}, f32[32,16,128]{2,1,0:T(8,128)}) custom-call(f32[8]{0:T(128)S(1)} %copy-done.7, f32[2,8,64,128]{3,2,1,0:T(8,128)S(1)} %collective-permute-done.4.up_ref, f32[2,8,64,128]{3,2,1,0:T(8,128)S(1)} %shard_map.116.own_ref, ...), custom_call_target="tpu_custom_call" | custom-call | tf_op jit(solution)/shard_map/pallas_call | solution.py:540
  53.6 6.4 %all-to-all-start = ((f32[32,16,128]{2,1,0:T(8,128)}), f32[32,16,128]{2,1,0:T(8,128)S(1)}, u32[]{:S(2)}, u32[]{:S(2)}) async-start(f32[32,16,128]{2,1,0:T(8,128)} %get-tuple-element.20), calls=%async_computation | async-start | bytes 524288 | tf_op jit(solution)/shard_map/all_to_all | solution.py:555
  61.6 9.7 %all-to-all-done.image_ref = f32[32,16,128]{2,1,0:T(8,128)S(1)} async-done(((f32[32,16,128]{2,1,0:T(8,128)}), f32[32,16,128]{2,1,0:T(8,128)S(1)}, u32[]{:S(2)}, u32[]{:S(2)}) %all-to-all-start) | async-done | bytes 262176 | tf_op jit(solution)/shard_map/all_to_all | solution.py:555
  73.1 5.7 %all-to-all-start.2 = ((f32[32,16,128]{2,1,0:T(8,128)}), f32[32,16,128]{2,1,0:T(8,128)S(1)}, u32[]{:S(2)}, u32[]{:S(2)}) async-start(f32[32,16,128]{2,1,0:T(8,128)} %shard_map.119), calls=%async_computation.2 | async-start | bytes 524288 | tf_op jit(solution)/shard_map/all_to_all | solution.py:559
  81.3 9.2 %all-to-all-done.2.rows_ref = f32[32,16,128]{2,1,0:T(8,128)S(1)} async-done(((f32[32,16,128]{2,1,0:T(8,128)}), f32[32,16,128]{2,1,0:T(8,128)S(1)}, u32[]{:S(2)}, u32[]{:S(2)}) %all-to-all-start.2) | async-done | bytes 262176 | tf_op jit(solution)/shard_map/all_to_all | solution.py:559
  90.5 2.8 %shard_map.122 = f32[32,16,128]{2,1,0:T(8,128)} custom-call(f32[32,16,128]{2,1,0:T(8,128)S(1)} %all-to-all-done.2.rows_ref, f32[8,32,128]{2,1,0:T(8,128)S(1)} %shard_map.120.spec_ref, bf16[4,8,128,256]{3,2,1,0:T(8,128)(2,1)S(1)} %shard_map.121.table_ref), custom_call_target="tpu_custom_call" | custom-call | tf_op jit(solution)/shard_map/pallas_call | solution.py:562
  93.3 4.9 %all-to-all-start.3 = ((f32[32,16,128]{2,1,0:T(8,128)}), f32[32,16,128]{2,1,0:T(8,128)S(1)}, u32[]{:S(2)}, u32[]{:S(2)}) async-start(f32[32,16,128]{2,1,0:T(8,128)} %shard_map.122), calls=%async_computation.3 | async-start | bytes 524288 | tf_op jit(solution)/shard_map/all_to_all | solution.py:563
  98.2 7.0 %collective-permute-start.6 = (f32[8,64,128]{2,1,0:T(8,128)}, f32[8,64,128]{2,1,0:T(8,128)S(1)}, u32[]{:S(2)}, u32[]{:S(2)}) collective-permute-start(f32[8,64,128]{2,1,0:T(8,128)} %get-tuple-element.22), channel_id=1, source_target_pairs={{0,1},{1,2},{2,3},{3,4},{4,5},{5,6},{6,7},{8,9},{9,10},{10,11},{11... | collective-permute-start | bytes 786440 | tf_op jit(solution)/shard_map/ppermute | solution.py:480
  109.9 4.0 %all-to-all-start.4 = ((f32[4,64,128]{2,1,0:T(8,128)}), f32[4,64,128]{2,1,0:T(8,128)}, u32[]{:S(2)}, u32[]{:S(2)}) async-start(f32[4,64,128]{2,1,0:T(8,128)} %shard_map.124), calls=%async_computation.4 | async-start | bytes 262144 | tf_op jit(solution)/shard_map/all_to_all | solution.py:567
  113.9 5.3 %collective-permute-done.7.right_ref = f32[8,64,128]{2,1,0:T(8,128)S(1)} collective-permute-done((f32[8,64,128]{2,1,0:T(8,128)}, f32[8,64,128]{2,1,0:T(8,128)S(1)}, u32[]{:S(2)}, u32[]{:S(2)}) %collective-permute-start.7) | collective-permute-done | bytes 262176 | tf_op jit(solution)/shard_map/ppermute | solution.py:480
  120.0 3.0 %shard_map.126 = (f32[2,8,64,128]{3,2,1,0:T(8,128)S(1)}, f32[64,128]{1,0:T(8,128)}) custom-call(f32[4,64,128]{2,1,0:T(8,128)} %all-to-all-done.4.images_ref, f32[64,128]{1,0:T(8,128)S(1)} %copy-done.4, f32[2,8,64,128]{3,2,1,0:T(8,128)S(1)} %get-tuple-element.21.field_ref, f32[2,8,64,128]{3,2,1,0:T(8,128)S(1)} %shard_map.125.halo_ref, ...), custom_call_target="tpu_custom_call" | custom-call | tf_op jit(solution)/shard_map/pallas_call | solution.py:569
  123.0 11.1 %collective-permute-start.8 = (f32[2,8,64,128]{3,2,1,0:T(8,128)S(1)}, f32[2,8,64,128]{3,2,1,0:T(8,128)S(1)}, u32[]{:S(2)}, u32[]{:S(2)}) collective-permute-start(f32[2,8,64,128]{3,2,1,0:T(8,128)S(1)} %get-tuple-element.24.own_ref), channel_id=1, source_target_pairs={{0,8},{8,16},{16,24},{24,32},{32,40},{40,48},{48,56},{1,9},{9,17},... | collective-permute-start | bytes 1572872 | tf_op jit(solution)/shard_map/ppermute | solution.py:480
  136.1 4.2 %collective-permute-done.8.up_ref = f32[2,8,64,128]{3,2,1,0:T(8,128)S(1)} collective-permute-done((f32[2,8,64,128]{3,2,1,0:T(8,128)S(1)}, f32[2,8,64,128]{3,2,1,0:T(8,128)S(1)}, u32[]{:S(2)}, u32[]{:S(2)}) %collective-permute-start.8) | collective-permute-done | bytes 524320 | tf_op jit(solution)/shard_map/ppermute | solution.py:480
  140.2 4.4 %collective-permute-done.9.down_ref = f32[2,8,64,128]{3,2,1,0:T(8,128)S(1)} collective-permute-done((f32[2,8,64,128]{3,2,1,0:T(8,128)S(1)}, f32[2,8,64,128]{3,2,1,0:T(8,128)S(1)}, u32[]{:S(2)}, u32[]{:S(2)}) %collective-permute-start.9) | collective-permute-done | bytes 524320 | tf_op jit(solution)/shard_map/ppermute | solution.py:480
  144.6 2.7 %shard_map.127 = f32[2,8,64,128]{3,2,1,0:T(8,128)} custom-call(f32[8]{0:T(128)S(1)} %copy-done.8, f32[2,8,64,128]{3,2,1,0:T(8,128)S(1)} %collective-permute-done.8.up_ref, f32[2,8,64,128]{3,2,1,0:T(8,128)S(1)} %get-tuple-element.24.own_ref, f32[2,8,64,128]{3,2,1,0:T(8,128)S(1)} %collective-permute-done.9.down_ref, f32[8,1,256]{2,1,0:T(1,128)S(1)} %copy-done.3, ...), custom_call_target="tpu_custom_call" | custom-call | tf_op jit(solution)/shard_map/pallas_call | solution.py:576
  (43 shorter events, 22.9 us)
Async XLA Ops:
  0.6 49.8 %copy-start.7 = (f32[8]{0:T(128)S(1)}, f32[8]{0:T(128)}, u32[]{:S(2)}) copy-start(f32[8]{0:T(128)} %weight_ref.3) | copy-start | bytes 100
  3.0 31.4 %collective-permute-start.1 = (f32[8,64,128]{2,1,0:T(8,128)}, f32[8,64,128]{2,1,0:T(8,128)S(1)}, u32[]{:S(2)}, u32[]{:S(2)}) collective-permute-start(f32[8,64,128]{2,1,0:T(8,128)} %get-tuple-element.16.after_ref), channel_id=1, source_target_pairs={{1,0},{2,1},{3,2},{4,3},{5,4},{6,5},{7,6},{9,8},{10,9},{11,10},{12... | collective-permute-start | bytes 786440 | tf_op jit(solution)/shard_map/ppermute | solution.py:480
  7.1 18.0 %collective-permute-start.2 = (f32[2,16,128]{2,1,0:T(8,128)}, f32[2,16,128]{2,1,0:T(8,128)S(1)}, u32[]{:S(2)}, u32[]{:S(2)}) collective-permute-start(f32[2,16,128]{2,1,0:T(8,128)} %get-tuple-element.18), channel_id=1, source_target_pairs={{0,7},{1,6},{2,5},{3,4},{4,3},{5,2},{6,1},{7,0},{8,15},{9,14},{10,... | collective-permute-start | bytes 49160 | tf_op jit(solution)/shard_map/ppermute | solution.py:519
  14.2 10.9 %collective-permute-start.3 = (f32[2,8,128]{2,1,0:T(8,128)}, f32[2,8,128]{2,1,0:T(8,128)S(1)}, u32[]{:S(2)}, u32[]{:S(2)}) collective-permute-start(f32[2,8,128]{2,1,0:T(8,128)} %get-tuple-element.19), channel_id=1, source_target_pairs={{0,0},{1,7},{2,6},{3,5},{4,4},{5,3},{6,2},{7,1},{8,8},{9,15},{10,1... | collective-permute-start | bytes 24584 | tf_op jit(solution)/shard_map/ppermute | solution.py:520
  16.4 18.1 %collective-permute-start = (f32[8,64,128]{2,1,0:T(8,128)}, f32[8,64,128]{2,1,0:T(8,128)S(1)}, u32[]{:S(2)}, u32[]{:S(2)}) collective-permute-start(f32[8,64,128]{2,1,0:T(8,128)} %get-tuple-element.15), channel_id=1, source_target_pairs={{0,1},{1,2},{2,3},{3,4},{4,5},{5,6},{6,7},{8,9},{9,10},{10,11},{11... | collective-permute-start | bytes 786440 | tf_op jit(solution)/shard_map/ppermute | solution.py:480
  25.8 27.8 %all-to-all-start.1 = ((f32[8,80,128]{2,1,0:T(8,128)}), f32[8,80,128]{2,1,0:T(8,128)S(1)}, u32[]{:S(2)}, u32[]{:S(2)}) async-start(f32[8,80,128]{2,1,0:T(8,128)} %shard_map.115.after_ref), calls=%async_computation.1 | async-start | bytes 655360 | tf_op jit(solution)/shard_map/all_to_all | solution.py:525
  34.4 16.0 %copy-start.2 = (f32[8,1,256]{2,1,0:T(1,128)}, f32[8,1,256]{2,1,0:T(1,128)S(1)}, u32[]{:S(2)}) copy-start(f32[8,1,256]{2,1,0:T(1,128)S(1)} %get-tuple-element.27.base_re_ref) | copy-start | bytes 24580
  34.4 19.1 %copy-start = (f32[8,1,256]{2,1,0:T(1,128)}, f32[8,1,256]{2,1,0:T(1,128)S(1)}, u32[]{:S(2)}) copy-start(f32[8,1,256]{2,1,0:T(1,128)S(1)} %get-tuple-element.26.base_im_ref) | copy-start | bytes 24580
  36.4 9.6 %collective-permute-start.4 = (f32[2,8,64,128]{3,2,1,0:T(8,128)S(1)}, f32[2,8,64,128]{3,2,1,0:T(8,128)S(1)}, u32[]{:S(2)}, u32[]{:S(2)}) collective-permute-start(f32[2,8,64,128]{3,2,1,0:T(8,128)S(1)} %shard_map.116.own_ref), channel_id=1, source_target_pairs={{0,8},{8,16},{16,24},{24,32},{32,40},{40,48},{48,56},{1,9},{9,17},... | collective-permute-start | bytes 1572872 | tf_op jit(solution)/shard_map/ppermute | solution.py:480
  39.9 10.5 %collective-permute-start.5 = (f32[2,8,64,128]{3,2,1,0:T(8,128)S(1)}, f32[2,8,64,128]{3,2,1,0:T(8,128)S(1)}, u32[]{:S(2)}, u32[]{:S(2)}) collective-permute-start(f32[2,8,64,128]{3,2,1,0:T(8,128)S(1)} %shard_map.116.own_ref), channel_id=1, source_target_pairs={{8,0},{16,8},{24,16},{32,24},{40,32},{48,40},{56,48},{9,1},{17,9},... | collective-permute-start | bytes 1572872 | tf_op jit(solution)/shard_map/ppermute | solution.py:480
  53.6 17.7 %all-to-all-start = ((f32[32,16,128]{2,1,0:T(8,128)}), f32[32,16,128]{2,1,0:T(8,128)S(1)}, u32[]{:S(2)}, u32[]{:S(2)}) async-start(f32[32,16,128]{2,1,0:T(8,128)} %get-tuple-element.20), calls=%async_computation | async-start | bytes 524288 | tf_op jit(solution)/shard_map/all_to_all | solution.py:555
  73.1 17.4 %all-to-all-start.2 = ((f32[32,16,128]{2,1,0:T(8,128)}), f32[32,16,128]{2,1,0:T(8,128)S(1)}, u32[]{:S(2)}, u32[]{:S(2)}) async-start(f32[32,16,128]{2,1,0:T(8,128)} %shard_map.119), calls=%async_computation.2 | async-start | bytes 524288 | tf_op jit(solution)/shard_map/all_to_all | solution.py:559
  78.9 1.6 %copy-start.5 = (bf16[128,128]{1,0:T(8,128)(2,1)S(1)}, bf16[128,128]{1,0:T(8,128)(2,1)}, u32[]{:S(2)}) copy-start(bf16[128,128]{1,0:T(8,128)(2,1)} %constant.44.clone.order_ref) | copy-start | bytes 98308
  78.9 1.6 %copy-start.6 = (bf16[128,128]{1,0:T(8,128)(2,1)S(1)}, bf16[128,128]{1,0:T(8,128)(2,1)}, u32[]{:S(2)}) copy-start(bf16[128,128]{1,0:T(8,128)(2,1)} %constant.45.clone.reverse_ref) | copy-start | bytes 98308
  93.3 15.5 %all-to-all-start.3 = ((f32[32,16,128]{2,1,0:T(8,128)}), f32[32,16,128]{2,1,0:T(8,128)S(1)}, u32[]{:S(2)}, u32[]{:S(2)}) async-start(f32[32,16,128]{2,1,0:T(8,128)} %shard_map.122), calls=%async_computation.3 | async-start | bytes 524288 | tf_op jit(solution)/shard_map/all_to_all | solution.py:563
  98.2 15.6 %collective-permute-start.6 = (f32[8,64,128]{2,1,0:T(8,128)}, f32[8,64,128]{2,1,0:T(8,128)S(1)}, u32[]{:S(2)}, u32[]{:S(2)}) collective-permute-start(f32[8,64,128]{2,1,0:T(8,128)} %get-tuple-element.22), channel_id=1, source_target_pairs={{0,1},{1,2},{2,3},{3,4},{4,5},{5,6},{6,7},{8,9},{9,10},{10,11},{11... | collective-permute-start | bytes 786440 | tf_op jit(solution)/shard_map/ppermute | solution.py:480
  105.3 13.9 %collective-permute-start.7 = (f32[8,64,128]{2,1,0:T(8,128)}, f32[8,64,128]{2,1,0:T(8,128)S(1)}, u32[]{:S(2)}, u32[]{:S(2)}) collective-permute-start(f32[8,64,128]{2,1,0:T(8,128)} %get-tuple-element.23), channel_id=1, source_target_pairs={{1,0},{2,1},{3,2},{4,3},{5,4},{6,5},{7,6},{9,8},{10,9},{11,10},{12... | collective-permute-start | bytes 786440 | tf_op jit(solution)/shard_map/ppermute | solution.py:480
  109.9 9.5 %all-to-all-start.4 = ((f32[4,64,128]{2,1,0:T(8,128)}), f32[4,64,128]{2,1,0:T(8,128)}, u32[]{:S(2)}, u32[]{:S(2)}) async-start(f32[4,64,128]{2,1,0:T(8,128)} %shard_map.124), calls=%async_computation.4 | async-start | bytes 262144 | tf_op jit(solution)/shard_map/all_to_all | solution.py:567
  119.2 0.7 copy-start.1
  119.2 0.7 copy-start.3
  119.2 0.8 copy-start.4
  119.2 25.4 %copy-start.8 = (f32[8]{0:T(128)S(1)}, f32[8]{0:T(128)}, u32[]{:S(2)}) copy-start(f32[8]{0:T(128)} %weight_ref.3) | copy-start | bytes 100
  123.0 17.2 %collective-permute-start.8 = (f32[2,8,64,128]{3,2,1,0:T(8,128)S(1)}, f32[2,8,64,128]{3,2,1,0:T(8,128)S(1)}, u32[]{:S(2)}, u32[]{:S(2)}) collective-permute-start(f32[2,8,64,128]{3,2,1,0:T(8,128)S(1)} %get-tuple-element.24.own_ref), channel_id=1, source_target_pairs={{0,8},{8,16},{16,24},{24,32},{32,40},{40,48},{48,56},{1,9},{9,17},... | collective-permute-start | bytes 1572872 | tf_op jit(solution)/shard_map/ppermute | solution.py:480
  134.1 10.5 %collective-permute-start.9 = (f32[2,8,64,128]{3,2,1,0:T(8,128)S(1)}, f32[2,8,64,128]{3,2,1,0:T(8,128)S(1)}, u32[]{:S(2)}, u32[]{:S(2)}) collective-permute-start(f32[2,8,64,128]{3,2,1,0:T(8,128)S(1)} %get-tuple-element.24.own_ref), channel_id=1, source_target_pairs={{8,0},{16,8},{24,16},{32,24},{40,32},{48,40},{56,48},{9,1},{17,9},... | collective-permute-start | bytes 1572872 | tf_op jit(solution)/shard_map/ppermute | solution.py:480

commit v4 on v3

--- a/solution.py
+++ b/solution.py
@@ -22,7 +22,7 @@
 QC = TC // NW
 KB = NR // (NCOL * NW)
 STEP = 2
-LONG = pl.CostEstimate(flops=1 << 50, bytes_accessed=1 << 36, transcendentals=1 << 40)
+MEDIUM = pl.CostEstimate(flops=1 << 36, bytes_accessed=0, transcendentals=0)
 ROOT = float(np.sqrt(0.5))
 F32 = jnp.float32
 BF16 = jnp.bfloat16
@@ -549,7 +549,7 @@
     prop_halo = call(
         halo_kernel,
         out_shape=near(*field),
-        cost_estimate=LONG,
+        cost_estimate=MEDIUM,
     )(prop_left, prop_right)
 
     image = lax.all_to_all(shares, ("wave", "row"), split_axis=0, concat_axis=0, tiled=True)

time: 148 us -> 147 us (level)
  no operation moved by 1% of the time
where the time goes in v4:
time: 147 us; the launch traced here: 146 us
  starting transfers between devices  69.6 us (47%)
  waiting for transfers between devices  47.6 us (32%)
  Pallas kernels  25.5 us (17%)
  other arithmetic  1.57 us (1%)
  between operations  1.5 us (1%)
    ppermute x8, starting transfers between devices, neighbours(): lax.ppermute(value, axis, [(i, i + step) for i in range(count) if 0 <= i...  31.7 us
    ppermute x8, waiting for transfers between devices, neighbours(): lax.ppermute(value, axis, [(i, i + step) for i in range(count) if 0 <= i...  23.1 us
    all_to_all x1, waiting for transfers between devices, shards(): lax.all_to_all(shares, ('wave', 'row'), split_axis=0, concat_axis=0, tile...  9.67 us
    all_to_all x1, waiting for transfers between devices, shards(): lax.all_to_all(freq_rows, ('col', 'wave'), split_axis=0, concat_axis=0, t...  9.21 us
    all_to_all x1, starting transfers between devices, shards(): lax.all_to_all(known, 'row', split_axis=0, concat_axis=0, tiled=True)  8.28 us
    ppermute x1, starting transfers between devices, shards(): mirror = lax.ppermute(mirror, 'col', [(i, 7 - i) for i in range(NCOL)])  7.11 us
    all_to_all x1, starting transfers between devices, shards(): lax.all_to_all(shares, ('wave', 'row'), split_axis=0, concat_axis=0, tile...  6.37 us
    all_to_all x1, starting transfers between devices, shards(): lax.all_to_all(freq_rows, ('col', 'wave'), split_axis=0, concat_axis=0, t...  5.75 us
  transfers between devices with their start and end apart: 15, of which 9 were waited for; matrix products, arithmetic and copies ran while one was open for 1% of the time, Pallas kernels for 9%

profile of v4, /device:TPU:25, one launch (start us, length us, event | category | flops | bytes accessed | tf_op | source)
XLA Modules:
  0.0 145.8 jit_solution(3554131439489015767)
XLA Ops:
  0.6 2.4 %shard_map.113 = (f32[2,8,64,128]{3,2,1,0:T(8,128)S(1)}, f32[8,64,128]{2,1,0:T(8,128)}, f32[8,64,128]{2,1,0:T(8,128)}) custom-call(f32[2,8,64,128]{3,2,1,0:T(8,128)} %field_ref.1), custom_call_target="tpu_custom_call" | custom-call | tf_op jit(solution)/shard_map/pallas_call | solution.py:501
  3.0 2.4 %collective-permute-start.1 = (f32[8,64,128]{2,1,0:T(8,128)}, f32[8,64,128]{2,1,0:T(8,128)S(1)}, u32[]{:S(2)}, u32[]{:S(2)}) collective-permute-start(f32[8,64,128]{2,1,0:T(8,128)} %get-tuple-element.16.after_ref), channel_id=1, source_target_pairs={{1,0},{2,1},{3,2},{4,3},{5,4},{6,5},{7,6},{9,8},{10,9},{11,10},{12... | collective-permute-start | bytes 786440 | tf_op jit(solution)/shard_map/ppermute | solution.py:480
  7.1 7.1 %collective-permute-start.2 = (f32[2,16,128]{2,1,0:T(8,128)}, f32[2,16,128]{2,1,0:T(8,128)S(1)}, u32[]{:S(2)}, u32[]{:S(2)}) collective-permute-start(f32[2,16,128]{2,1,0:T(8,128)} %get-tuple-element.18), channel_id=1, source_target_pairs={{0,7},{1,6},{2,5},{3,4},{4,3},{5,2},{6,1},{7,0},{8,15},{9,14},{10,... | collective-permute-start | bytes 49160 | tf_op jit(solution)/shard_map/ppermute | solution.py:519
  14.2 2.2 %collective-permute-start.3 = (f32[2,8,128]{2,1,0:T(8,128)}, f32[2,8,128]{2,1,0:T(8,128)S(1)}, u32[]{:S(2)}, u32[]{:S(2)}) collective-permute-start(f32[2,8,128]{2,1,0:T(8,128)} %get-tuple-element.19), channel_id=1, source_target_pairs={{0,0},{1,7},{2,6},{3,5},{4,4},{5,3},{6,2},{7,1},{8,8},{9,15},{10,1... | collective-permute-start | bytes 24584 | tf_op jit(solution)/shard_map/ppermute | solution.py:520
  20.2 4.9 %collective-permute-done.3.first_ref = f32[2,8,128]{2,1,0:T(8,128)S(1)} collective-permute-done((f32[2,8,128]{2,1,0:T(8,128)}, f32[2,8,128]{2,1,0:T(8,128)S(1)}, u32[]{:S(2)}, u32[]{:S(2)}) %collective-permute-start.3) | collective-permute-done | bytes 8224 | tf_op jit(solution)/shard_map/ppermute | solution.py:520
  25.8 8.3 %all-to-all-start.1 = ((f32[8,80,128]{2,1,0:T(8,128)}), f32[8,80,128]{2,1,0:T(8,128)S(1)}, u32[]{:S(2)}, u32[]{:S(2)}) async-start(f32[8,80,128]{2,1,0:T(8,128)} %shard_map.115.after_ref), calls=%async_computation.1 | async-start | bytes 655360 | tf_op jit(solution)/shard_map/all_to_all | solution.py:525
  36.3 3.5 %collective-permute-start.4 = (f32[2,8,64,128]{3,2,1,0:T(8,128)S(1)}, f32[2,8,64,128]{3,2,1,0:T(8,128)S(1)}, u32[]{:S(2)}, u32[]{:S(2)}) collective-permute-start(f32[2,8,64,128]{3,2,1,0:T(8,128)S(1)} %shard_map.116.own_ref), channel_id=1, source_target_pairs={{0,8},{8,16},{16,24},{24,32},{32,40},{40,48},{48,56},{1,9},{9,17},... | collective-permute-start | bytes 1572872 | tf_op jit(solution)/shard_map/ppermute | solution.py:480
  41.8 4.2 %collective-permute-done.4.up_ref = f32[2,8,64,128]{3,2,1,0:T(8,128)S(1)} collective-permute-done((f32[2,8,64,128]{3,2,1,0:T(8,128)S(1)}, f32[2,8,64,128]{3,2,1,0:T(8,128)S(1)}, u32[]{:S(2)}, u32[]{:S(2)}) %collective-permute-start.4) | collective-permute-done | bytes 524320 | tf_op jit(solution)/shard_map/ppermute | solution.py:480
  46.0 4.4 %collective-permute-done.5.down_ref = f32[2,8,64,128]{3,2,1,0:T(8,128)S(1)} collective-permute-done((f32[2,8,64,128]{3,2,1,0:T(8,128)S(1)}, f32[2,8,64,128]{3,2,1,0:T(8,128)S(1)}, u32[]{:S(2)}, u32[]{:S(2)}) %collective-permute-start.5) | collective-permute-done | bytes 524320 | tf_op jit(solution)/shard_map/ppermute | solution.py:480
  50.4 3.2 %shard_map.117 = (f32[2,8,64,128]{3,2,1,0:T(8,128)S(1)}, f32[8,64,128]{2,1,0:T(8,128)}, f32[8,64,128]{2,1,0:T(8,128)}, f32[32,16,128]{2,1,0:T(8,128)}) custom-call(f32[8]{0:T(128)S(1)} %copy-done.3, f32[2,8,64,128]{3,2,1,0:T(8,128)S(1)} %collective-permute-done.4.up_ref, f32[2,8,64,128]{3,2,1,0:T(8,128)S(1)} %shard_map.116.own_ref, ...), custom_call_target="tpu_custom_call" | custom-call | tf_op jit(solution)/shard_map/pallas_call | solution.py:540
  53.6 6.4 %all-to-all-start = ((f32[32,16,128]{2,1,0:T(8,128)}), f32[32,16,128]{2,1,0:T(8,128)S(1)}, u32[]{:S(2)}, u32[]{:S(2)}) async-start(f32[32,16,128]{2,1,0:T(8,128)} %get-tuple-element.20), calls=%async_computation | async-start | bytes 524288 | tf_op jit(solution)/shard_map/all_to_all | solution.py:555
  61.6 9.7 %all-to-all-done.image_ref = f32[32,16,128]{2,1,0:T(8,128)S(1)} async-done(((f32[32,16,128]{2,1,0:T(8,128)}), f32[32,16,128]{2,1,0:T(8,128)S(1)}, u32[]{:S(2)}, u32[]{:S(2)}) %all-to-all-start) | async-done | bytes 262176 | tf_op jit(solution)/shard_map/all_to_all | solution.py:555
  73.1 5.8 %all-to-all-start.2 = ((f32[32,16,128]{2,1,0:T(8,128)}), f32[32,16,128]{2,1,0:T(8,128)S(1)}, u32[]{:S(2)}, u32[]{:S(2)}) async-start(f32[32,16,128]{2,1,0:T(8,128)} %shard_map.119), calls=%async_computation.2 | async-start | bytes 524288 | tf_op jit(solution)/shard_map/all_to_all | solution.py:559
  81.3 9.2 %all-to-all-done.2.rows_ref = f32[32,16,128]{2,1,0:T(8,128)S(1)} async-done(((f32[32,16,128]{2,1,0:T(8,128)}), f32[32,16,128]{2,1,0:T(8,128)S(1)}, u32[]{:S(2)}, u32[]{:S(2)}) %all-to-all-start.2) | async-done | bytes 262176 | tf_op jit(solution)/shard_map/all_to_all | solution.py:559
  90.5 2.8 %shard_map.122 = f32[32,16,128]{2,1,0:T(8,128)} custom-call(f32[32,16,128]{2,1,0:T(8,128)S(1)} %all-to-all-done.2.rows_ref, f32[8,32,128]{2,1,0:T(8,128)S(1)} %shard_map.120.spec_ref, bf16[4,8,128,256]{3,2,1,0:T(8,128)(2,1)S(1)} %shard_map.121.table_ref), custom_call_target="tpu_custom_call" | custom-call | tf_op jit(solution)/shard_map/pallas_call | solution.py:562
  93.3 4.9 %all-to-all-start.3 = ((f32[32,16,128]{2,1,0:T(8,128)}), f32[32,16,128]{2,1,0:T(8,128)S(1)}, u32[]{:S(2)}, u32[]{:S(2)}) async-start(f32[32,16,128]{2,1,0:T(8,128)} %shard_map.122), calls=%async_computation.3 | async-start | bytes 524288 | tf_op jit(solution)/shard_map/all_to_all | solution.py:563
  98.2 7.0 %collective-permute-start.6 = (f32[8,64,128]{2,1,0:T(8,128)}, f32[8,64,128]{2,1,0:T(8,128)S(1)}, u32[]{:S(2)}, u32[]{:S(2)}) collective-permute-start(f32[8,64,128]{2,1,0:T(8,128)} %get-tuple-element.22), channel_id=1, source_target_pairs={{0,1},{1,2},{2,3},{3,4},{4,5},{5,6},{6,7},{8,9},{9,10},{10,11},{11... | collective-permute-start | bytes 786440 | tf_op jit(solution)/shard_map/ppermute | solution.py:480
  109.9 3.3 %all-to-all-start.4 = ((f32[4,64,128]{2,1,0:T(8,128)}), f32[4,64,128]{2,1,0:T(8,128)S(1)}, u32[]{:S(2)}, u32[]{:S(2)}) async-start(f32[4,64,128]{2,1,0:T(8,128)} %shard_map.124), calls=%async_computation.4 | async-start | bytes 262144 | tf_op jit(solution)/shard_map/all_to_all | solution.py:567
  113.2 5.9 %collective-permute-done.7.right_ref = f32[8,64,128]{2,1,0:T(8,128)S(1)} collective-permute-done((f32[8,64,128]{2,1,0:T(8,128)}, f32[8,64,128]{2,1,0:T(8,128)S(1)}, u32[]{:S(2)}, u32[]{:S(2)}) %collective-permute-start.7) | collective-permute-done | bytes 262176 | tf_op jit(solution)/shard_map/ppermute | solution.py:480
  119.4 2.1 %shard_map.126 = (f32[2,8,64,128]{3,2,1,0:T(8,128)S(1)}, f32[64,128]{1,0:T(8,128)}) custom-call(f32[4,64,128]{2,1,0:T(8,128)S(1)} %all-to-all-done.4.images_ref, f32[64,128]{1,0:T(8,128)S(1)} %copy-done, f32[2,8,64,128]{3,2,1,0:T(8,128)S(1)} %get-tuple-element.21.field_ref, f32[2,8,64,128]{3,2,1,0:T(8,128)S(1)} %shard_map.125.halo_ref, ...), custom_call_target="tpu_custom_call" | custom-call | tf_op jit(solution)/shard_map/pallas_call | solution.py:569
  121.5 11.1 %collective-permute-start.8 = (f32[2,8,64,128]{3,2,1,0:T(8,128)S(1)}, f32[2,8,64,128]{3,2,1,0:T(8,128)S(1)}, u32[]{:S(2)}, u32[]{:S(2)}) collective-permute-start(f32[2,8,64,128]{3,2,1,0:T(8,128)S(1)} %get-tuple-element.24.own_ref), channel_id=1, source_target_pairs={{0,8},{8,16},{16,24},{24,32},{32,40},{40,48},{48,56},{1,9},{9,17},... | collective-permute-start | bytes 1572872 | tf_op jit(solution)/shard_map/ppermute | solution.py:480
  134.5 4.2 %collective-permute-done.8.up_ref = f32[2,8,64,128]{3,2,1,0:T(8,128)S(1)} collective-permute-done((f32[2,8,64,128]{3,2,1,0:T(8,128)S(1)}, f32[2,8,64,128]{3,2,1,0:T(8,128)S(1)}, u32[]{:S(2)}, u32[]{:S(2)}) %collective-permute-start.8) | collective-permute-done | bytes 524320 | tf_op jit(solution)/shard_map/ppermute | solution.py:480
  138.7 4.4 %collective-permute-done.9.down_ref = f32[2,8,64,128]{3,2,1,0:T(8,128)S(1)} collective-permute-done((f32[2,8,64,128]{3,2,1,0:T(8,128)S(1)}, f32[2,8,64,128]{3,2,1,0:T(8,128)S(1)}, u32[]{:S(2)}, u32[]{:S(2)}) %collective-permute-start.9) | collective-permute-done | bytes 524320 | tf_op jit(solution)/shard_map/ppermute | solution.py:480
  143.1 2.7 %shard_map.127 = f32[2,8,64,128]{3,2,1,0:T(8,128)} custom-call(f32[8]{0:T(128)S(1)} %copy-done.3, f32[2,8,64,128]{3,2,1,0:T(8,128)S(1)} %collective-permute-done.8.up_ref, f32[2,8,64,128]{3,2,1,0:T(8,128)S(1)} %get-tuple-element.24.own_ref, f32[2,8,64,128]{3,2,1,0:T(8,128)S(1)} %collective-permute-done.9.down_ref, ...), custom_call_target="tpu_custom_call" | custom-call | tf_op jit(solution)/shard_map/pallas_call | solution.py:576
  (33 shorter events, 22.3 us)
Async XLA Ops:
  0.6 49.7 %copy-start.3 = (f32[8]{0:T(128)S(1)}, f32[8]{0:T(128)}, u32[]{:S(2)}) copy-start(f32[8]{0:T(128)} %weight_ref.3) | copy-start | bytes 100
  3.0 31.4 %collective-permute-start.1 = (f32[8,64,128]{2,1,0:T(8,128)}, f32[8,64,128]{2,1,0:T(8,128)S(1)}, u32[]{:S(2)}, u32[]{:S(2)}) collective-permute-start(f32[8,64,128]{2,1,0:T(8,128)} %get-tuple-element.16.after_ref), channel_id=1, source_target_pairs={{1,0},{2,1},{3,2},{4,3},{5,4},{6,5},{7,6},{9,8},{10,9},{11,10},{12... | collective-permute-start | bytes 786440 | tf_op jit(solution)/shard_map/ppermute | solution.py:480
  7.1 18.0 %collective-permute-start.2 = (f32[2,16,128]{2,1,0:T(8,128)}, f32[2,16,128]{2,1,0:T(8,128)S(1)}, u32[]{:S(2)}, u32[]{:S(2)}) collective-permute-start(f32[2,16,128]{2,1,0:T(8,128)} %get-tuple-element.18), channel_id=1, source_target_pairs={{0,7},{1,6},{2,5},{3,4},{4,3},{5,2},{6,1},{7,0},{8,15},{9,14},{10,... | collective-permute-start | bytes 49160 | tf_op jit(solution)/shard_map/ppermute | solution.py:519
  14.2 10.9 %collective-permute-start.3 = (f32[2,8,128]{2,1,0:T(8,128)}, f32[2,8,128]{2,1,0:T(8,128)S(1)}, u32[]{:S(2)}, u32[]{:S(2)}) collective-permute-start(f32[2,8,128]{2,1,0:T(8,128)} %get-tuple-element.19), channel_id=1, source_target_pairs={{0,0},{1,7},{2,6},{3,5},{4,4},{5,3},{6,2},{7,1},{8,8},{9,15},{10,1... | collective-permute-start | bytes 24584 | tf_op jit(solution)/shard_map/ppermute | solution.py:520
  16.4 18.1 %collective-permute-start = (f32[8,64,128]{2,1,0:T(8,128)}, f32[8,64,128]{2,1,0:T(8,128)S(1)}, u32[]{:S(2)}, u32[]{:S(2)}) collective-permute-start(f32[8,64,128]{2,1,0:T(8,128)} %get-tuple-element.15), channel_id=1, source_target_pairs={{0,1},{1,2},{2,3},{3,4},{4,5},{5,6},{6,7},{8,9},{9,10},{10,11},{11... | collective-permute-start | bytes 786440 | tf_op jit(solution)/shard_map/ppermute | solution.py:480
  25.8 27.7 %all-to-all-start.1 = ((f32[8,80,128]{2,1,0:T(8,128)}), f32[8,80,128]{2,1,0:T(8,128)S(1)}, u32[]{:S(2)}, u32[]{:S(2)}) async-start(f32[8,80,128]{2,1,0:T(8,128)} %shard_map.115.after_ref), calls=%async_computation.1 | async-start | bytes 655360 | tf_op jit(solution)/shard_map/all_to_all | solution.py:525
  36.3 9.6 %collective-permute-start.4 = (f32[2,8,64,128]{3,2,1,0:T(8,128)S(1)}, f32[2,8,64,128]{3,2,1,0:T(8,128)S(1)}, u32[]{:S(2)}, u32[]{:S(2)}) collective-permute-start(f32[2,8,64,128]{3,2,1,0:T(8,128)S(1)} %shard_map.116.own_ref), channel_id=1, source_target_pairs={{0,8},{8,16},{16,24},{24,32},{32,40},{40,48},{48,56},{1,9},{9,17},... | collective-permute-start | bytes 1572872 | tf_op jit(solution)/shard_map/ppermute | solution.py:480
  39.9 10.5 %collective-permute-start.5 = (f32[2,8,64,128]{3,2,1,0:T(8,128)S(1)}, f32[2,8,64,128]{3,2,1,0:T(8,128)S(1)}, u32[]{:S(2)}, u32[]{:S(2)}) collective-permute-start(f32[2,8,64,128]{3,2,1,0:T(8,128)S(1)} %shard_map.116.own_ref), channel_id=1, source_target_pairs={{8,0},{16,8},{24,16},{32,24},{40,32},{48,40},{56,48},{9,1},{17,9},... | collective-permute-start | bytes 1572872 | tf_op jit(solution)/shard_map/ppermute | solution.py:480
  53.6 17.7 %all-to-all-start = ((f32[32,16,128]{2,1,0:T(8,128)}), f32[32,16,128]{2,1,0:T(8,128)S(1)}, u32[]{:S(2)}, u32[]{:S(2)}) async-start(f32[32,16,128]{2,1,0:T(8,128)} %get-tuple-element.20), calls=%async_computation | async-start | bytes 524288 | tf_op jit(solution)/shard_map/all_to_all | solution.py:555
  73.1 17.4 %all-to-all-start.2 = ((f32[32,16,128]{2,1,0:T(8,128)}), f32[32,16,128]{2,1,0:T(8,128)S(1)}, u32[]{:S(2)}, u32[]{:S(2)}) async-start(f32[32,16,128]{2,1,0:T(8,128)} %shard_map.119), calls=%async_computation.2 | async-start | bytes 524288 | tf_op jit(solution)/shard_map/all_to_all | solution.py:559
  78.9 1.6 %copy-start.1 = (bf16[128,128]{1,0:T(8,128)(2,1)S(1)}, bf16[128,128]{1,0:T(8,128)(2,1)}, u32[]{:S(2)}) copy-start(bf16[128,128]{1,0:T(8,128)(2,1)} %constant.44.clone.order_ref) | copy-start | bytes 98308
  78.9 1.6 %copy-start.2 = (bf16[128,128]{1,0:T(8,128)(2,1)S(1)}, bf16[128,128]{1,0:T(8,128)(2,1)}, u32[]{:S(2)}) copy-start(bf16[128,128]{1,0:T(8,128)(2,1)} %constant.45.clone.reverse_ref) | copy-start | bytes 98308
  93.3 15.5 %all-to-all-start.3 = ((f32[32,16,128]{2,1,0:T(8,128)}), f32[32,16,128]{2,1,0:T(8,128)S(1)}, u32[]{:S(2)}, u32[]{:S(2)}) async-start(f32[32,16,128]{2,1,0:T(8,128)} %shard_map.122), calls=%async_computation.3 | async-start | bytes 524288 | tf_op jit(solution)/shard_map/all_to_all | solution.py:563
  98.2 15.0 %collective-permute-start.6 = (f32[8,64,128]{2,1,0:T(8,128)}, f32[8,64,128]{2,1,0:T(8,128)S(1)}, u32[]{:S(2)}, u32[]{:S(2)}) collective-permute-start(f32[8,64,128]{2,1,0:T(8,128)} %get-tuple-element.22), channel_id=1, source_target_pairs={{0,1},{1,2},{2,3},{3,4},{4,5},{5,6},{6,7},{8,9},{9,10},{10,11},{11... | collective-permute-start | bytes 786440 | tf_op jit(solution)/shard_map/ppermute | solution.py:480
  105.2 13.9 %collective-permute-start.7 = (f32[8,64,128]{2,1,0:T(8,128)}, f32[8,64,128]{2,1,0:T(8,128)S(1)}, u32[]{:S(2)}, u32[]{:S(2)}) collective-permute-start(f32[8,64,128]{2,1,0:T(8,128)} %get-tuple-element.23), channel_id=1, source_target_pairs={{1,0},{2,1},{3,2},{4,3},{5,4},{6,5},{7,6},{9,8},{10,9},{11,10},{12... | collective-permute-start | bytes 786440 | tf_op jit(solution)/shard_map/ppermute | solution.py:480
  109.9 9.5 %all-to-all-start.4 = ((f32[4,64,128]{2,1,0:T(8,128)}), f32[4,64,128]{2,1,0:T(8,128)S(1)}, u32[]{:S(2)}, u32[]{:S(2)}) async-start(f32[4,64,128]{2,1,0:T(8,128)} %shard_map.124), calls=%async_computation.4 | async-start | bytes 262144 | tf_op jit(solution)/shard_map/all_to_all | solution.py:567
  113.2 6.2 %copy-start = (f32[64,128]{1,0:T(8,128)S(1)}, f32[64,128]{1,0:T(8,128)}, u32[]{:S(2)}) copy-start(f32[64,128]{1,0:T(8,128)} %measured_ref.3) | copy-start | bytes 98308
  121.5 17.2 %collective-permute-start.8 = (f32[2,8,64,128]{3,2,1,0:T(8,128)S(1)}, f32[2,8,64,128]{3,2,1,0:T(8,128)S(1)}, u32[]{:S(2)}, u32[]{:S(2)}) collective-permute-start(f32[2,8,64,128]{3,2,1,0:T(8,128)S(1)} %get-tuple-element.24.own_ref), channel_id=1, source_target_pairs={{0,8},{8,16},{16,24},{24,32},{32,40},{40,48},{48,56},{1,9},{9,17},... | collective-permute-start | bytes 1572872 | tf_op jit(solution)/shard_map/ppermute | solution.py:480
  132.6 10.5 %collective-permute-start.9 = (f32[2,8,64,128]{3,2,1,0:T(8,128)S(1)}, f32[2,8,64,128]{3,2,1,0:T(8,128)S(1)}, u32[]{:S(2)}, u32[]{:S(2)}) collective-permute-start(f32[2,8,64,128]{3,2,1,0:T(8,128)S(1)} %get-tuple-element.24.own_ref), channel_id=1, source_target_pairs={{8,0},{16,8},{24,16},{32,24},{40,32},{48,40},{56,48},{9,1},{17,9},... | collective-permute-start | bytes 1572872 | tf_op jit(solution)/shard_map/ppermute | solution.py:480

commit v5 on v4

--- a/solution.py
+++ b/solution.py
@@ -21,7 +21,7 @@
 LW = WAVES // NW
 QC = TC // NW
 KB = NR // (NCOL * NW)
-STEP = 2
+STEP = 8
 MEDIUM = pl.CostEstimate(flops=1 << 36, bytes_accessed=0, transcendentals=0)
 ROOT = float(np.sqrt(0.5))
 F32 = jnp.float32

time: 147 us -> 144 us (0.980)
  Pallas kernels: 25.5 us -> 22.5 us
  transfers between devices with their start and end apart: 15 -> 15, of which waited for: 9 -> 9; matrix products, arithmetic and copies ran while one was open for 1% -> 1% of each run, Pallas kernels for 9% -> 8%
where the time goes in v5:
time: 144 us; the launch traced here: 143 us
  starting transfers between devices  69 us (48%)
  waiting for transfers between devices  48.2 us (33%)
  Pallas kernels  22.5 us (16%)
  other arithmetic  1.57 us (1%)
  between operations  1.5 us (1%)
    ppermute x8, starting transfers between devices, neighbours(): lax.ppermute(value, axis, [(i, i + step) for i in range(count) if 0 <= i...  31.7 us
    ppermute x8, waiting for transfers between devices, neighbours(): lax.ppermute(value, axis, [(i, i + step) for i in range(count) if 0 <= i...  23.7 us
    all_to_all x1, waiting for transfers between devices, shards(): lax.all_to_all(shares, ('wave', 'row'), split_axis=0, concat_axis=0, tile...  9.67 us
    all_to_all x1, waiting for transfers between devices, shards(): lax.all_to_all(freq_rows, ('col', 'wave'), split_axis=0, concat_axis=0, t...  9.21 us
    all_to_all x1, starting transfers between devices, shards(): lax.all_to_all(known, 'row', split_axis=0, concat_axis=0, tiled=True)  8.28 us
    ppermute x1, starting transfers between devices, shards(): mirror = lax.ppermute(mirror, 'col', [(i, 7 - i) for i in range(NCOL)])  7.11 us
    all_to_all x1, starting transfers between devices, shards(): lax.all_to_all(freq_rows, ('col', 'wave'), split_axis=0, concat_axis=0, t...  5.76 us
    all_to_all x1, starting transfers between devices, shards(): lax.all_to_all(shares, ('wave', 'row'), split_axis=0, concat_axis=0, tile...  5.75 us
  transfers between devices with their start and end apart: 15, of which 9 were waited for; matrix products, arithmetic and copies ran while one was open for 1% of the time, Pallas kernels for 8%

profile of v5, /device:TPU:25, one launch (start us, length us, event | category | flops | bytes accessed | tf_op | source)
XLA Modules:
  0.0 142.9 jit_solution(9673207883748798223)
XLA Ops:
  0.6 2.4 %shard_map.113 = (f32[2,8,64,128]{3,2,1,0:T(8,128)S(1)}, f32[8,64,128]{2,1,0:T(8,128)}, f32[8,64,128]{2,1,0:T(8,128)}) custom-call(f32[2,8,64,128]{3,2,1,0:T(8,128)} %field_ref.1), custom_call_target="tpu_custom_call" | custom-call | tf_op jit(solution)/shard_map/pallas_call | solution.py:501
  3.0 2.4 %collective-permute-start.1 = (f32[8,64,128]{2,1,0:T(8,128)}, f32[8,64,128]{2,1,0:T(8,128)S(1)}, u32[]{:S(2)}, u32[]{:S(2)}) collective-permute-start(f32[8,64,128]{2,1,0:T(8,128)} %get-tuple-element.16.after_ref), channel_id=1, source_target_pairs={{1,0},{2,1},{3,2},{4,3},{5,4},{6,5},{7,6},{9,8},{10,9},{11,10},{12... | collective-permute-start | bytes 786440 | tf_op jit(solution)/shard_map/ppermute | solution.py:480
  7.1 7.1 %collective-permute-start.2 = (f32[2,16,128]{2,1,0:T(8,128)}, f32[2,16,128]{2,1,0:T(8,128)S(1)}, u32[]{:S(2)}, u32[]{:S(2)}) collective-permute-start(f32[2,16,128]{2,1,0:T(8,128)} %get-tuple-element.18), channel_id=1, source_target_pairs={{0,7},{1,6},{2,5},{3,4},{4,3},{5,2},{6,1},{7,0},{8,15},{9,14},{10,... | collective-permute-start | bytes 49160 | tf_op jit(solution)/shard_map/ppermute | solution.py:519
  14.2 2.2 %collective-permute-start.3 = (f32[2,8,128]{2,1,0:T(8,128)}, f32[2,8,128]{2,1,0:T(8,128)S(1)}, u32[]{:S(2)}, u32[]{:S(2)}) collective-permute-start(f32[2,8,128]{2,1,0:T(8,128)} %get-tuple-element.19), channel_id=1, source_target_pairs={{0,0},{1,7},{2,6},{3,5},{4,4},{5,3},{6,2},{7,1},{8,8},{9,15},{10,1... | collective-permute-start | bytes 24584 | tf_op jit(solution)/shard_map/ppermute | solution.py:520
  20.2 4.9 %collective-permute-done.3.first_ref = f32[2,8,128]{2,1,0:T(8,128)S(1)} collective-permute-done((f32[2,8,128]{2,1,0:T(8,128)}, f32[2,8,128]{2,1,0:T(8,128)S(1)}, u32[]{:S(2)}, u32[]{:S(2)}) %collective-permute-start.3) | collective-permute-done | bytes 8224 | tf_op jit(solution)/shard_map/ppermute | solution.py:520
  25.8 8.3 %all-to-all-start.1 = ((f32[8,80,128]{2,1,0:T(8,128)}), f32[8,80,128]{2,1,0:T(8,128)S(1)}, u32[]{:S(2)}, u32[]{:S(2)}) async-start(f32[8,80,128]{2,1,0:T(8,128)} %shard_map.115.after_ref), calls=%async_computation.1 | async-start | bytes 655360 | tf_op jit(solution)/shard_map/all_to_all | solution.py:525
  35.5 3.5 %collective-permute-start.4 = (f32[2,8,64,128]{3,2,1,0:T(8,128)S(1)}, f32[2,8,64,128]{3,2,1,0:T(8,128)S(1)}, u32[]{:S(2)}, u32[]{:S(2)}) collective-permute-start(f32[2,8,64,128]{3,2,1,0:T(8,128)S(1)} %shard_map.116.own_ref), channel_id=1, source_target_pairs={{0,8},{8,16},{16,24},{24,32},{32,40},{40,48},{48,56},{1,9},{9,17},... | collective-permute-start | bytes 1572872 | tf_op jit(solution)/shard_map/ppermute | solution.py:480
  39.1 1.9 %collective-permute-start.5 = (f32[2,8,64,128]{3,2,1,0:T(8,128)S(1)}, f32[2,8,64,128]{3,2,1,0:T(8,128)S(1)}, u32[]{:S(2)}, u32[]{:S(2)}) collective-permute-start(f32[2,8,64,128]{3,2,1,0:T(8,128)S(1)} %shard_map.116.own_ref), channel_id=1, source_target_pairs={{8,0},{16,8},{24,16},{32,24},{40,32},{48,40},{56,48},{9,1},{17,9},... | collective-permute-start | bytes 1572872 | tf_op jit(solution)/shard_map/ppermute | solution.py:480
  41.0 4.7 %collective-permute-done.4.up_ref = f32[2,8,64,128]{3,2,1,0:T(8,128)S(1)} collective-permute-done((f32[2,8,64,128]{3,2,1,0:T(8,128)S(1)}, f32[2,8,64,128]{3,2,1,0:T(8,128)S(1)}, u32[]{:S(2)}, u32[]{:S(2)}) %collective-permute-start.4) | collective-permute-done | bytes 524320 | tf_op jit(solution)/shard_map/ppermute | solution.py:480
  45.7 4.5 %collective-permute-done.5.down_ref = f32[2,8,64,128]{3,2,1,0:T(8,128)S(1)} collective-permute-done((f32[2,8,64,128]{3,2,1,0:T(8,128)S(1)}, f32[2,8,64,128]{3,2,1,0:T(8,128)S(1)}, u32[]{:S(2)}, u32[]{:S(2)}) %collective-permute-start.5) | collective-permute-done | bytes 524320 | tf_op jit(solution)/shard_map/ppermute | solution.py:480
  50.2 2.3 %shard_map.117 = (f32[2,8,64,128]{3,2,1,0:T(8,128)S(1)}, f32[8,64,128]{2,1,0:T(8,128)}, f32[8,64,128]{2,1,0:T(8,128)}, f32[32,16,128]{2,1,0:T(8,128)}) custom-call(f32[8]{0:T(128)S(1)} %copy-done.3, f32[2,8,64,128]{3,2,1,0:T(8,128)S(1)} %collective-permute-done.4.up_ref, f32[2,8,64,128]{3,2,1,0:T(8,128)S(1)} %shard_map.116.own_ref, ...), custom_call_target="tpu_custom_call" | custom-call | tf_op jit(solution)/shard_map/pallas_call | solution.py:540
  52.5 5.7 %all-to-all-start = ((f32[32,16,128]{2,1,0:T(8,128)}), f32[32,16,128]{2,1,0:T(8,128)S(1)}, u32[]{:S(2)}, u32[]{:S(2)}) async-start(f32[32,16,128]{2,1,0:T(8,128)} %get-tuple-element.20), calls=%async_computation | async-start | bytes 524288 | tf_op jit(solution)/shard_map/all_to_all | solution.py:555
  59.8 9.7 %all-to-all-done.image_ref = f32[32,16,128]{2,1,0:T(8,128)S(1)} async-done(((f32[32,16,128]{2,1,0:T(8,128)}), f32[32,16,128]{2,1,0:T(8,128)S(1)}, u32[]{:S(2)}, u32[]{:S(2)}) %all-to-all-start) | async-done | bytes 262176 | tf_op jit(solution)/shard_map/all_to_all | solution.py:555
  71.4 5.8 %all-to-all-start.2 = ((f32[32,16,128]{2,1,0:T(8,128)}), f32[32,16,128]{2,1,0:T(8,128)S(1)}, u32[]{:S(2)}, u32[]{:S(2)}) async-start(f32[32,16,128]{2,1,0:T(8,128)} %shard_map.119), calls=%async_computation.2 | async-start | bytes 524288 | tf_op jit(solution)/shard_map/all_to_all | solution.py:559
  79.5 9.2 %all-to-all-done.2.rows_ref = f32[32,16,128]{2,1,0:T(8,128)S(1)} async-done(((f32[32,16,128]{2,1,0:T(8,128)}), f32[32,16,128]{2,1,0:T(8,128)S(1)}, u32[]{:S(2)}, u32[]{:S(2)}) %all-to-all-start.2) | async-done | bytes 262176 | tf_op jit(solution)/shard_map/all_to_all | solution.py:559
  88.7 2.8 %shard_map.122 = f32[32,16,128]{2,1,0:T(8,128)} custom-call(f32[32,16,128]{2,1,0:T(8,128)S(1)} %all-to-all-done.2.rows_ref, f32[8,32,128]{2,1,0:T(8,128)S(1)} %shard_map.120.spec_ref, bf16[4,8,128,256]{3,2,1,0:T(8,128)(2,1)S(1)} %shard_map.121.table_ref), custom_call_target="tpu_custom_call" | custom-call | tf_op jit(solution)/shard_map/pallas_call | solution.py:562
  91.6 4.9 %all-to-all-start.3 = ((f32[32,16,128]{2,1,0:T(8,128)}), f32[32,16,128]{2,1,0:T(8,128)S(1)}, u32[]{:S(2)}, u32[]{:S(2)}) async-start(f32[32,16,128]{2,1,0:T(8,128)} %shard_map.122), calls=%async_computation.3 | async-start | bytes 524288 | tf_op jit(solution)/shard_map/all_to_all | solution.py:563
  96.5 7.0 %collective-permute-start.6 = (f32[8,64,128]{2,1,0:T(8,128)}, f32[8,64,128]{2,1,0:T(8,128)S(1)}, u32[]{:S(2)}, u32[]{:S(2)}) collective-permute-start(f32[8,64,128]{2,1,0:T(8,128)} %get-tuple-element.22), channel_id=1, source_target_pairs={{0,1},{1,2},{2,3},{3,4},{4,5},{5,6},{6,7},{8,9},{9,10},{10,11},{11... | collective-permute-start | bytes 786440 | tf_op jit(solution)/shard_map/ppermute | solution.py:480
  108.1 3.3 %all-to-all-start.4 = ((f32[4,64,128]{2,1,0:T(8,128)}), f32[4,64,128]{2,1,0:T(8,128)S(1)}, u32[]{:S(2)}, u32[]{:S(2)}) async-start(f32[4,64,128]{2,1,0:T(8,128)} %shard_map.124), calls=%async_computation.4 | async-start | bytes 262144 | tf_op jit(solution)/shard_map/all_to_all | solution.py:567
  111.5 5.9 %collective-permute-done.7.right_ref = f32[8,64,128]{2,1,0:T(8,128)S(1)} collective-permute-done((f32[8,64,128]{2,1,0:T(8,128)}, f32[8,64,128]{2,1,0:T(8,128)S(1)}, u32[]{:S(2)}, u32[]{:S(2)}) %collective-permute-start.7) | collective-permute-done | bytes 262176 | tf_op jit(solution)/shard_map/ppermute | solution.py:480
  119.2 11.1 %collective-permute-start.8 = (f32[2,8,64,128]{3,2,1,0:T(8,128)S(1)}, f32[2,8,64,128]{3,2,1,0:T(8,128)S(1)}, u32[]{:S(2)}, u32[]{:S(2)}) collective-permute-start(f32[2,8,64,128]{3,2,1,0:T(8,128)S(1)} %get-tuple-element.24.own_ref), channel_id=1, source_target_pairs={{0,8},{8,16},{16,24},{24,32},{32,40},{40,48},{48,56},{1,9},{9,17},... | collective-permute-start | bytes 1572872 | tf_op jit(solution)/shard_map/ppermute | solution.py:480
  132.2 4.2 %collective-permute-done.8.up_ref = f32[2,8,64,128]{3,2,1,0:T(8,128)S(1)} collective-permute-done((f32[2,8,64,128]{3,2,1,0:T(8,128)S(1)}, f32[2,8,64,128]{3,2,1,0:T(8,128)S(1)}, u32[]{:S(2)}, u32[]{:S(2)}) %collective-permute-start.8) | collective-permute-done | bytes 524320 | tf_op jit(solution)/shard_map/ppermute | solution.py:480
  136.4 4.4 %collective-permute-done.9.down_ref = f32[2,8,64,128]{3,2,1,0:T(8,128)S(1)} collective-permute-done((f32[2,8,64,128]{3,2,1,0:T(8,128)S(1)}, f32[2,8,64,128]{3,2,1,0:T(8,128)S(1)}, u32[]{:S(2)}, u32[]{:S(2)}) %collective-permute-start.9) | collective-permute-done | bytes 524320 | tf_op jit(solution)/shard_map/ppermute | solution.py:480
  140.8 2.1 %shard_map.127 = f32[2,8,64,128]{3,2,1,0:T(8,128)} custom-call(f32[8]{0:T(128)S(1)} %copy-done.3, f32[2,8,64,128]{3,2,1,0:T(8,128)S(1)} %collective-permute-done.8.up_ref, f32[2,8,64,128]{3,2,1,0:T(8,128)S(1)} %get-tuple-element.24.own_ref, f32[2,8,64,128]{3,2,1,0:T(8,128)S(1)} %collective-permute-done.9.down_ref, ...), custom_call_target="tpu_custom_call" | custom-call | tf_op jit(solution)/shard_map/pallas_call | solution.py:576
  (33 shorter events, 21.1 us)
Async XLA Ops:
  0.6 49.6 %copy-start.3 = (f32[8]{0:T(128)S(1)}, f32[8]{0:T(128)}, u32[]{:S(2)}) copy-start(f32[8]{0:T(128)} %weight_ref.3) | copy-start | bytes 100
  3.0 31.4 %collective-permute-start.1 = (f32[8,64,128]{2,1,0:T(8,128)}, f32[8,64,128]{2,1,0:T(8,128)S(1)}, u32[]{:S(2)}, u32[]{:S(2)}) collective-permute-start(f32[8,64,128]{2,1,0:T(8,128)} %get-tuple-element.16.after_ref), channel_id=1, source_target_pairs={{1,0},{2,1},{3,2},{4,3},{5,4},{6,5},{7,6},{9,8},{10,9},{11,10},{12... | collective-permute-start | bytes 786440 | tf_op jit(solution)/shard_map/ppermute | solution.py:480
  7.1 18.0 %collective-permute-start.2 = (f32[2,16,128]{2,1,0:T(8,128)}, f32[2,16,128]{2,1,0:T(8,128)S(1)}, u32[]{:S(2)}, u32[]{:S(2)}) collective-permute-start(f32[2,16,128]{2,1,0:T(8,128)} %get-tuple-element.18), channel_id=1, source_target_pairs={{0,7},{1,6},{2,5},{3,4},{4,3},{5,2},{6,1},{7,0},{8,15},{9,14},{10,... | collective-permute-start | bytes 49160 | tf_op jit(solution)/shard_map/ppermute | solution.py:519
  14.2 10.9 %collective-permute-start.3 = (f32[2,8,128]{2,1,0:T(8,128)}, f32[2,8,128]{2,1,0:T(8,128)S(1)}, u32[]{:S(2)}, u32[]{:S(2)}) collective-permute-start(f32[2,8,128]{2,1,0:T(8,128)} %get-tuple-element.19), channel_id=1, source_target_pairs={{0,0},{1,7},{2,6},{3,5},{4,4},{5,3},{6,2},{7,1},{8,8},{9,15},{10,1... | collective-permute-start | bytes 24584 | tf_op jit(solution)/shard_map/ppermute | solution.py:520
  16.4 18.1 %collective-permute-start = (f32[8,64,128]{2,1,0:T(8,128)}, f32[8,64,128]{2,1,0:T(8,128)S(1)}, u32[]{:S(2)}, u32[]{:S(2)}) collective-permute-start(f32[8,64,128]{2,1,0:T(8,128)} %get-tuple-element.15), channel_id=1, source_target_pairs={{0,1},{1,2},{2,3},{3,4},{4,5},{5,6},{6,7},{8,9},{9,10},{10,11},{11... | collective-permute-start | bytes 786440 | tf_op jit(solution)/shard_map/ppermute | solution.py:480
  25.8 26.6 %all-to-all-start.1 = ((f32[8,80,128]{2,1,0:T(8,128)}), f32[8,80,128]{2,1,0:T(8,128)S(1)}, u32[]{:S(2)}, u32[]{:S(2)}) async-start(f32[8,80,128]{2,1,0:T(8,128)} %shard_map.115.after_ref), calls=%async_computation.1 | async-start | bytes 655360 | tf_op jit(solution)/shard_map/all_to_all | solution.py:525
  35.5 10.2 %collective-permute-start.4 = (f32[2,8,64,128]{3,2,1,0:T(8,128)S(1)}, f32[2,8,64,128]{3,2,1,0:T(8,128)S(1)}, u32[]{:S(2)}, u32[]{:S(2)}) collective-permute-start(f32[2,8,64,128]{3,2,1,0:T(8,128)S(1)} %shard_map.116.own_ref), channel_id=1, source_target_pairs={{0,8},{8,16},{16,24},{24,32},{32,40},{40,48},{48,56},{1,9},{9,17},... | collective-permute-start | bytes 1572872 | tf_op jit(solution)/shard_map/ppermute | solution.py:480
  39.1 11.1 %collective-permute-start.5 = (f32[2,8,64,128]{3,2,1,0:T(8,128)S(1)}, f32[2,8,64,128]{3,2,1,0:T(8,128)S(1)}, u32[]{:S(2)}, u32[]{:S(2)}) collective-permute-start(f32[2,8,64,128]{3,2,1,0:T(8,128)S(1)} %shard_map.116.own_ref), channel_id=1, source_target_pairs={{8,0},{16,8},{24,16},{32,24},{40,32},{48,40},{56,48},{9,1},{17,9},... | collective-permute-start | bytes 1572872 | tf_op jit(solution)/shard_map/ppermute | solution.py:480
  52.5 17.0 %all-to-all-start = ((f32[32,16,128]{2,1,0:T(8,128)}), f32[32,16,128]{2,1,0:T(8,128)S(1)}, u32[]{:S(2)}, u32[]{:S(2)}) async-start(f32[32,16,128]{2,1,0:T(8,128)} %get-tuple-element.20), calls=%async_computation | async-start | bytes 524288 | tf_op jit(solution)/shard_map/all_to_all | solution.py:555
  71.4 17.4 %all-to-all-start.2 = ((f32[32,16,128]{2,1,0:T(8,128)}), f32[32,16,128]{2,1,0:T(8,128)S(1)}, u32[]{:S(2)}, u32[]{:S(2)}) async-start(f32[32,16,128]{2,1,0:T(8,128)} %shard_map.119), calls=%async_computation.2 | async-start | bytes 524288 | tf_op jit(solution)/shard_map/all_to_all | solution.py:559
  77.1 1.6 %copy-start.1 = (bf16[128,128]{1,0:T(8,128)(2,1)S(1)}, bf16[128,128]{1,0:T(8,128)(2,1)}, u32[]{:S(2)}) copy-start(bf16[128,128]{1,0:T(8,128)(2,1)} %constant.44.clone.order_ref) | copy-start | bytes 98308
  77.1 1.6 %copy-start.2 = (bf16[128,128]{1,0:T(8,128)(2,1)S(1)}, bf16[128,128]{1,0:T(8,128)(2,1)}, u32[]{:S(2)}) copy-start(bf16[128,128]{1,0:T(8,128)(2,1)} %constant.45.clone.reverse_ref) | copy-start | bytes 98308
  91.6 15.5 %all-to-all-start.3 = ((f32[32,16,128]{2,1,0:T(8,128)}), f32[32,16,128]{2,1,0:T(8,128)S(1)}, u32[]{:S(2)}, u32[]{:S(2)}) async-start(f32[32,16,128]{2,1,0:T(8,128)} %shard_map.122), calls=%async_computation.3 | async-start | bytes 524288 | tf_op jit(solution)/shard_map/all_to_all | solution.py:563
  96.5 15.0 %collective-permute-start.6 = (f32[8,64,128]{2,1,0:T(8,128)}, f32[8,64,128]{2,1,0:T(8,128)S(1)}, u32[]{:S(2)}, u32[]{:S(2)}) collective-permute-start(f32[8,64,128]{2,1,0:T(8,128)} %get-tuple-element.22), channel_id=1, source_target_pairs={{0,1},{1,2},{2,3},{3,4},{4,5},{5,6},{6,7},{8,9},{9,10},{10,11},{11... | collective-permute-start | bytes 786440 | tf_op jit(solution)/shard_map/ppermute | solution.py:480
  103.5 13.9 %collective-permute-start.7 = (f32[8,64,128]{2,1,0:T(8,128)}, f32[8,64,128]{2,1,0:T(8,128)S(1)}, u32[]{:S(2)}, u32[]{:S(2)}) collective-permute-start(f32[8,64,128]{2,1,0:T(8,128)} %get-tuple-element.23), channel_id=1, source_target_pairs={{1,0},{2,1},{3,2},{4,3},{5,4},{6,5},{7,6},{9,8},{10,9},{11,10},{12... | collective-permute-start | bytes 786440 | tf_op jit(solution)/shard_map/ppermute | solution.py:480
  108.1 9.5 %all-to-all-start.4 = ((f32[4,64,128]{2,1,0:T(8,128)}), f32[4,64,128]{2,1,0:T(8,128)S(1)}, u32[]{:S(2)}, u32[]{:S(2)}) async-start(f32[4,64,128]{2,1,0:T(8,128)} %shard_map.124), calls=%async_computation.4 | async-start | bytes 262144 | tf_op jit(solution)/shard_map/all_to_all | solution.py:567
  111.5 6.2 %copy-start = (f32[64,128]{1,0:T(8,128)S(1)}, f32[64,128]{1,0:T(8,128)}, u32[]{:S(2)}) copy-start(f32[64,128]{1,0:T(8,128)} %measured_ref.3) | copy-start | bytes 98308
  119.2 17.2 %collective-permute-start.8 = (f32[2,8,64,128]{3,2,1,0:T(8,128)S(1)}, f32[2,8,64,128]{3,2,1,0:T(8,128)S(1)}, u32[]{:S(2)}, u32[]{:S(2)}) collective-permute-start(f32[2,8,64,128]{3,2,1,0:T(8,128)S(1)} %get-tuple-element.24.own_ref), channel_id=1, source_target_pairs={{0,8},{8,16},{16,24},{24,32},{32,40},{40,48},{48,56},{1,9},{9,17},... | collective-permute-start | bytes 1572872 | tf_op jit(solution)/shard_map/ppermute | solution.py:480
  130.3 10.5 %collective-permute-start.9 = (f32[2,8,64,128]{3,2,1,0:T(8,128)S(1)}, f32[2,8,64,128]{3,2,1,0:T(8,128)S(1)}, u32[]{:S(2)}, u32[]{:S(2)}) collective-permute-start(f32[2,8,64,128]{3,2,1,0:T(8,128)S(1)} %get-tuple-element.24.own_ref), channel_id=1, source_target_pairs={{8,0},{16,8},{24,16},{32,24},{40,32},{48,40},{56,48},{9,1},{17,9},... | collective-permute-start | bytes 1572872 | tf_op jit(solution)/shard_map/ppermute | solution.py:480

commit v6 on v5

--- a/solution.py
+++ b/solution.py
@@ -483,11 +483,12 @@
 
 
 def taps_of(wavelength):
-    lane = jnp.arange(256)
-    offset = jnp.where(lane < 128, lane, lane - 256).astype(F32)
-    spread = jnp.arange(-HALO, HALO + 1).astype(F32)
-    norm = 1.0 / jnp.sqrt(jnp.sum(jnp.exp(-2.0 * (spread / HALO) ** 2)))
-    amplitude = jnp.where(jnp.abs(offset) <= HALO, jnp.exp(-((offset / HALO) ** 2)) * norm, 0.0)
+    lane = np.arange(256)
+    offset = np.where(lane < 128, lane, lane - 256).astype(np.float64)
+    spread = np.arange(-HALO, HALO + 1)
+    norm = 1.0 / np.sqrt(np.sum(np.exp(-2.0 * (spread / HALO) ** 2)))
+    amplitude = np.where(np.abs(offset) <= HALO, np.exp(-((offset / HALO) ** 2)) * norm, 0.0)
+    offset, amplitude = jnp.asarray(offset, F32), jnp.asarray(amplitude, F32)
     phase = offset * offset / (2.0 * wavelength[:, None] * HALO)
     return (amplitude * jnp.cos(phase))[:, None, :], (amplitude * jnp.sin(phase))[:, None, :]
 

time: 144 us -> 144 us (level)
  no operation moved by 1% of the time
where the time goes in v6:
time: 144 us; the launch traced here: 143 us
  starting transfers between devices  69 us (48%)
  waiting for transfers between devices  48.8 us (34%)
  Pallas kernels  22.5 us (16%)
  other arithmetic  1.67 us (1%)
    ppermute x8, starting transfers between devices, neighbours(): lax.ppermute(value, axis, [(i, i + step) for i in range(count) if 0 <= i...  31.7 us
    ppermute x8, waiting for transfers between devices, neighbours(): lax.ppermute(value, axis, [(i, i + step) for i in range(count) if 0 <= i...  23.1 us
    all_to_all x1, waiting for transfers between devices, shards(): lax.all_to_all(shares, ('wave', 'row'), split_axis=0, concat_axis=0, tile...  9.67 us
    all_to_all x1, waiting for transfers between devices, shards(): lax.all_to_all(freq_rows, ('col', 'wave'), split_axis=0, concat_axis=0, t...  9.21 us
    all_to_all x1, starting transfers between devices, shards(): lax.all_to_all(known, 'row', split_axis=0, concat_axis=0, tiled=True)  8.28 us
    ppermute x1, starting transfers between devices, shards(): mirror = lax.ppermute(mirror, 'col', [(i, 7 - i) for i in range(NCOL)])  7.11 us
    all_to_all x1, starting transfers between devices, shards(): lax.all_to_all(shares, ('wave', 'row'), split_axis=0, concat_axis=0, tile...  6.36 us
    ppermute x1, waiting for transfers between devices, shards(): first = lax.ppermute(first, 'col', [(i, (8 - i) % 8) for i in range(NCOL)])  6.12 us
  transfers between devices with their start and end apart: 15, of which 9 were waited for; matrix products, arithmetic and copies ran while one was open for 1% of the time, Pallas kernels for 8%

profile of v6, /device:TPU:25, one launch (start us, length us, event | category | flops | bytes accessed | tf_op | source)
XLA Modules:
  0.0 142.9 jit_solution(11512678297910122934)
XLA Ops:
  0.6 2.4 %shard_map.131 = (f32[2,8,64,128]{3,2,1,0:T(8,128)S(1)}, f32[8,64,128]{2,1,0:T(8,128)}, f32[8,64,128]{2,1,0:T(8,128)}) custom-call(f32[2,8,64,128]{3,2,1,0:T(8,128)} %field_ref.1), custom_call_target="tpu_custom_call" | custom-call | tf_op jit(solution)/shard_map/pallas_call | solution.py:502
  3.0 2.4 %collective-permute-start.1 = (f32[8,64,128]{2,1,0:T(8,128)}, f32[8,64,128]{2,1,0:T(8,128)S(1)}, u32[]{:S(2)}, u32[]{:S(2)}) collective-permute-start(f32[8,64,128]{2,1,0:T(8,128)} %get-tuple-element.16.after_ref), channel_id=1, source_target_pairs={{1,0},{2,1},{3,2},{4,3},{5,4},{6,5},{7,6},{9,8},{10,9},{11,10},{12... | collective-permute-start | bytes 786440 | tf_op jit(solution)/shard_map/ppermute | solution.py:480
  7.1 7.1 %collective-permute-start.2 = (f32[2,16,128]{2,1,0:T(8,128)}, f32[2,16,128]{2,1,0:T(8,128)S(1)}, u32[]{:S(2)}, u32[]{:S(2)}) collective-permute-start(f32[2,16,128]{2,1,0:T(8,128)} %get-tuple-element.18), channel_id=1, source_target_pairs={{0,7},{1,6},{2,5},{3,4},{4,3},{5,2},{6,1},{7,0},{8,15},{9,14},{10,... | collective-permute-start | bytes 49160 | tf_op jit(solution)/shard_map/ppermute | solution.py:520
  14.2 2.2 %collective-permute-start.3 = (f32[2,8,128]{2,1,0:T(8,128)}, f32[2,8,128]{2,1,0:T(8,128)S(1)}, u32[]{:S(2)}, u32[]{:S(2)}) collective-permute-start(f32[2,8,128]{2,1,0:T(8,128)} %get-tuple-element.19), channel_id=1, source_target_pairs={{0,0},{1,7},{2,6},{3,5},{4,4},{5,3},{6,2},{7,1},{8,8},{9,15},{10,1... | collective-permute-start | bytes 24584 | tf_op jit(solution)/shard_map/ppermute | solution.py:521
  19.0 6.1 %collective-permute-done.3.first_ref = f32[2,8,128]{2,1,0:T(8,128)S(1)} collective-permute-done((f32[2,8,128]{2,1,0:T(8,128)}, f32[2,8,128]{2,1,0:T(8,128)S(1)}, u32[]{:S(2)}, u32[]{:S(2)}) %collective-permute-start.3) | collective-permute-done | bytes 8224 | tf_op jit(solution)/shard_map/ppermute | solution.py:521
  25.8 8.3 %all-to-all-start.1 = ((f32[8,80,128]{2,1,0:T(8,128)}), f32[8,80,128]{2,1,0:T(8,128)S(1)}, u32[]{:S(2)}, u32[]{:S(2)}) async-start(f32[8,80,128]{2,1,0:T(8,128)} %shard_map.133.after_ref), calls=%async_computation.1 | async-start | bytes 655360 | tf_op jit(solution)/shard_map/all_to_all | solution.py:526
  36.2 3.5 %collective-permute-start.4 = (f32[2,8,64,128]{3,2,1,0:T(8,128)S(1)}, f32[2,8,64,128]{3,2,1,0:T(8,128)S(1)}, u32[]{:S(2)}, u32[]{:S(2)}) collective-permute-start(f32[2,8,64,128]{3,2,1,0:T(8,128)S(1)} %shard_map.134.own_ref), channel_id=1, source_target_pairs={{0,8},{8,16},{16,24},{24,32},{32,40},{40,48},{48,56},{1,9},{9,17},... | collective-permute-start | bytes 1572872 | tf_op jit(solution)/shard_map/ppermute | solution.py:480
  39.8 1.9 %collective-permute-start.5 = (f32[2,8,64,128]{3,2,1,0:T(8,128)S(1)}, f32[2,8,64,128]{3,2,1,0:T(8,128)S(1)}, u32[]{:S(2)}, u32[]{:S(2)}) collective-permute-start(f32[2,8,64,128]{3,2,1,0:T(8,128)S(1)} %shard_map.134.own_ref), channel_id=1, source_target_pairs={{8,0},{16,8},{24,16},{32,24},{40,32},{48,40},{56,48},{9,1},{17,9},... | collective-permute-start | bytes 1572872 | tf_op jit(solution)/shard_map/ppermute | solution.py:480
  41.7 4.2 %collective-permute-done.4.up_ref = f32[2,8,64,128]{3,2,1,0:T(8,128)S(1)} collective-permute-done((f32[2,8,64,128]{3,2,1,0:T(8,128)S(1)}, f32[2,8,64,128]{3,2,1,0:T(8,128)S(1)}, u32[]{:S(2)}, u32[]{:S(2)}) %collective-permute-start.4) | collective-permute-done | bytes 524320 | tf_op jit(solution)/shard_map/ppermute | solution.py:480
  45.9 4.4 %collective-permute-done.5.down_ref = f32[2,8,64,128]{3,2,1,0:T(8,128)S(1)} collective-permute-done((f32[2,8,64,128]{3,2,1,0:T(8,128)S(1)}, f32[2,8,64,128]{3,2,1,0:T(8,128)S(1)}, u32[]{:S(2)}, u32[]{:S(2)}) %collective-permute-start.5) | collective-permute-done | bytes 524320 | tf_op jit(solution)/shard_map/ppermute | solution.py:480
  50.3 2.3 %shard_map.135 = (f32[2,8,64,128]{3,2,1,0:T(8,128)S(1)}, f32[8,64,128]{2,1,0:T(8,128)}, f32[8,64,128]{2,1,0:T(8,128)}, f32[32,16,128]{2,1,0:T(8,128)}) custom-call(f32[8]{0:T(128)S(1)} %copy-done.3, f32[2,8,64,128]{3,2,1,0:T(8,128)S(1)} %collective-permute-done.4.up_ref, f32[2,8,64,128]{3,2,1,0:T(8,128)S(1)} %shard_map.134.own_ref, ...), custom_call_target="tpu_custom_call" | custom-call | tf_op jit(solution)/shard_map/pallas_call | solution.py:541
  52.5 6.4 %all-to-all-start = ((f32[32,16,128]{2,1,0:T(8,128)}), f32[32,16,128]{2,1,0:T(8,128)S(1)}, u32[]{:S(2)}, u32[]{:S(2)}) async-start(f32[32,16,128]{2,1,0:T(8,128)} %get-tuple-element.20), calls=%async_computation | async-start | bytes 524288 | tf_op jit(solution)/shard_map/all_to_all | solution.py:556
  60.5 9.7 %all-to-all-done.image_ref = f32[32,16,128]{2,1,0:T(8,128)S(1)} async-done(((f32[32,16,128]{2,1,0:T(8,128)}), f32[32,16,128]{2,1,0:T(8,128)S(1)}, u32[]{:S(2)}, u32[]{:S(2)}) %all-to-all-start) | async-done | bytes 262176 | tf_op jit(solution)/shard_map/all_to_all | solution.py:556
  72.0 5.1 %all-to-all-start.2 = ((f32[32,16,128]{2,1,0:T(8,128)}), f32[32,16,128]{2,1,0:T(8,128)S(1)}, u32[]{:S(2)}, u32[]{:S(2)}) async-start(f32[32,16,128]{2,1,0:T(8,128)} %shard_map.137), calls=%async_computation.2 | async-start | bytes 524288 | tf_op jit(solution)/shard_map/all_to_all | solution.py:560
  79.5 9.2 %all-to-all-done.2.rows_ref = f32[32,16,128]{2,1,0:T(8,128)S(1)} async-done(((f32[32,16,128]{2,1,0:T(8,128)}), f32[32,16,128]{2,1,0:T(8,128)S(1)}, u32[]{:S(2)}, u32[]{:S(2)}) %all-to-all-start.2) | async-done | bytes 262176 | tf_op jit(solution)/shard_map/all_to_all | solution.py:560
  88.7 2.8 %shard_map.140 = f32[32,16,128]{2,1,0:T(8,128)} custom-call(f32[32,16,128]{2,1,0:T(8,128)S(1)} %all-to-all-done.2.rows_ref, f32[8,32,128]{2,1,0:T(8,128)S(1)} %shard_map.138.spec_ref, bf16[4,8,128,256]{3,2,1,0:T(8,128)(2,1)S(1)} %shard_map.139.table_ref), custom_call_target="tpu_custom_call" | custom-call | tf_op jit(solution)/shard_map/pallas_call | solution.py:563
  91.6 4.9 %all-to-all-start.3 = ((f32[32,16,128]{2,1,0:T(8,128)}), f32[32,16,128]{2,1,0:T(8,128)S(1)}, u32[]{:S(2)}, u32[]{:S(2)}) async-start(f32[32,16,128]{2,1,0:T(8,128)} %shard_map.140), calls=%async_computation.3 | async-start | bytes 524288 | tf_op jit(solution)/shard_map/all_to_all | solution.py:564
  96.5 7.0 %collective-permute-start.6 = (f32[8,64,128]{2,1,0:T(8,128)}, f32[8,64,128]{2,1,0:T(8,128)S(1)}, u32[]{:S(2)}, u32[]{:S(2)}) collective-permute-start(f32[8,64,128]{2,1,0:T(8,128)} %get-tuple-element.22), channel_id=1, source_target_pairs={{0,1},{1,2},{2,3},{3,4},{4,5},{5,6},{6,7},{8,9},{9,10},{10,11},{11... | collective-permute-start | bytes 786440 | tf_op jit(solution)/shard_map/ppermute | solution.py:480
  108.1 3.3 %all-to-all-start.4 = ((f32[4,64,128]{2,1,0:T(8,128)}), f32[4,64,128]{2,1,0:T(8,128)S(1)}, u32[]{:S(2)}, u32[]{:S(2)}) async-start(f32[4,64,128]{2,1,0:T(8,128)} %shard_map.142), calls=%async_computation.4 | async-start | bytes 262144 | tf_op jit(solution)/shard_map/all_to_all | solution.py:568
  111.5 5.9 %collective-permute-done.7.right_ref = f32[8,64,128]{2,1,0:T(8,128)S(1)} collective-permute-done((f32[8,64,128]{2,1,0:T(8,128)}, f32[8,64,128]{2,1,0:T(8,128)S(1)}, u32[]{:S(2)}, u32[]{:S(2)}) %collective-permute-start.7) | collective-permute-done | bytes 262176 | tf_op jit(solution)/shard_map/ppermute | solution.py:480
  119.2 11.1 %collective-permute-start.8 = (f32[2,8,64,128]{3,2,1,0:T(8,128)S(1)}, f32[2,8,64,128]{3,2,1,0:T(8,128)S(1)}, u32[]{:S(2)}, u32[]{:S(2)}) collective-permute-start(f32[2,8,64,128]{3,2,1,0:T(8,128)S(1)} %get-tuple-element.24.own_ref), channel_id=1, source_target_pairs={{0,8},{8,16},{16,24},{24,32},{32,40},{40,48},{48,56},{1,9},{9,17},... | collective-permute-start | bytes 1572872 | tf_op jit(solution)/shard_map/ppermute | solution.py:480
  132.2 4.2 %collective-permute-done.8.up_ref = f32[2,8,64,128]{3,2,1,0:T(8,128)S(1)} collective-permute-done((f32[2,8,64,128]{3,2,1,0:T(8,128)S(1)}, f32[2,8,64,128]{3,2,1,0:T(8,128)S(1)}, u32[]{:S(2)}, u32[]{:S(2)}) %collective-permute-start.8) | collective-permute-done | bytes 524320 | tf_op jit(solution)/shard_map/ppermute | solution.py:480
  136.4 4.4 %collective-permute-done.9.down_ref = f32[2,8,64,128]{3,2,1,0:T(8,128)S(1)} collective-permute-done((f32[2,8,64,128]{3,2,1,0:T(8,128)S(1)}, f32[2,8,64,128]{3,2,1,0:T(8,128)S(1)}, u32[]{:S(2)}, u32[]{:S(2)}) %collective-permute-start.9) | collective-permute-done | bytes 524320 | tf_op jit(solution)/shard_map/ppermute | solution.py:480
  140.8 2.1 %shard_map.145 = f32[2,8,64,128]{3,2,1,0:T(8,128)} custom-call(f32[8]{0:T(128)S(1)} %copy-done.3, f32[2,8,64,128]{3,2,1,0:T(8,128)S(1)} %collective-permute-done.8.up_ref, f32[2,8,64,128]{3,2,1,0:T(8,128)S(1)} %get-tuple-element.24.own_ref, f32[2,8,64,128]{3,2,1,0:T(8,128)S(1)} %collective-permute-done.9.down_ref, ...), custom_call_target="tpu_custom_call" | custom-call | tf_op jit(solution)/shard_map/pallas_call | solution.py:577
  (31 shorter events, 21.2 us)
Async XLA Ops:
  0.6 49.6 %copy-start.3 = (f32[8]{0:T(128)S(1)}, f32[8]{0:T(128)}, u32[]{:S(2)}) copy-start(f32[8]{0:T(128)} %weight_ref.3) | copy-start | bytes 100
  3.0 32.1 %collective-permute-start.1 = (f32[8,64,128]{2,1,0:T(8,128)}, f32[8,64,128]{2,1,0:T(8,128)S(1)}, u32[]{:S(2)}, u32[]{:S(2)}) collective-permute-start(f32[8,64,128]{2,1,0:T(8,128)} %get-tuple-element.16.after_ref), channel_id=1, source_target_pairs={{1,0},{2,1},{3,2},{4,3},{5,4},{6,5},{7,6},{9,8},{10,9},{11,10},{12... | collective-permute-start | bytes 786440 | tf_op jit(solution)/shard_map/ppermute | solution.py:480
  7.1 18.0 %collective-permute-start.2 = (f32[2,16,128]{2,1,0:T(8,128)}, f32[2,16,128]{2,1,0:T(8,128)S(1)}, u32[]{:S(2)}, u32[]{:S(2)}) collective-permute-start(f32[2,16,128]{2,1,0:T(8,128)} %get-tuple-element.18), channel_id=1, source_target_pairs={{0,7},{1,6},{2,5},{3,4},{4,3},{5,2},{6,1},{7,0},{8,15},{9,14},{10,... | collective-permute-start | bytes 49160 | tf_op jit(solution)/shard_map/ppermute | solution.py:520
  14.2 10.9 %collective-permute-start.3 = (f32[2,8,128]{2,1,0:T(8,128)}, f32[2,8,128]{2,1,0:T(8,128)S(1)}, u32[]{:S(2)}, u32[]{:S(2)}) collective-permute-start(f32[2,8,128]{2,1,0:T(8,128)} %get-tuple-element.19), channel_id=1, source_target_pairs={{0,0},{1,7},{2,6},{3,5},{4,4},{5,3},{6,2},{7,1},{8,8},{9,15},{10,1... | collective-permute-start | bytes 24584 | tf_op jit(solution)/shard_map/ppermute | solution.py:521
  16.4 18.8 %collective-permute-start = (f32[8,64,128]{2,1,0:T(8,128)}, f32[8,64,128]{2,1,0:T(8,128)S(1)}, u32[]{:S(2)}, u32[]{:S(2)}) collective-permute-start(f32[8,64,128]{2,1,0:T(8,128)} %get-tuple-element.15), channel_id=1, source_target_pairs={{0,1},{1,2},{2,3},{3,4},{4,5},{5,6},{6,7},{8,9},{9,10},{10,11},{11... | collective-permute-start | bytes 786440 | tf_op jit(solution)/shard_map/ppermute | solution.py:480
  25.8 26.7 %all-to-all-start.1 = ((f32[8,80,128]{2,1,0:T(8,128)}), f32[8,80,128]{2,1,0:T(8,128)S(1)}, u32[]{:S(2)}, u32[]{:S(2)}) async-start(f32[8,80,128]{2,1,0:T(8,128)} %shard_map.133.after_ref), calls=%async_computation.1 | async-start | bytes 655360 | tf_op jit(solution)/shard_map/all_to_all | solution.py:526
  36.2 9.7 %collective-permute-start.4 = (f32[2,8,64,128]{3,2,1,0:T(8,128)S(1)}, f32[2,8,64,128]{3,2,1,0:T(8,128)S(1)}, u32[]{:S(2)}, u32[]{:S(2)}) collective-permute-start(f32[2,8,64,128]{3,2,1,0:T(8,128)S(1)} %shard_map.134.own_ref), channel_id=1, source_target_pairs={{0,8},{8,16},{16,24},{24,32},{32,40},{40,48},{48,56},{1,9},{9,17},... | collective-permute-start | bytes 1572872 | tf_op jit(solution)/shard_map/ppermute | solution.py:480
  39.8 10.5 %collective-permute-start.5 = (f32[2,8,64,128]{3,2,1,0:T(8,128)S(1)}, f32[2,8,64,128]{3,2,1,0:T(8,128)S(1)}, u32[]{:S(2)}, u32[]{:S(2)}) collective-permute-start(f32[2,8,64,128]{3,2,1,0:T(8,128)S(1)} %shard_map.134.own_ref), channel_id=1, source_target_pairs={{8,0},{16,8},{24,16},{32,24},{40,32},{48,40},{56,48},{9,1},{17,9},... | collective-permute-start | bytes 1572872 | tf_op jit(solution)/shard_map/ppermute | solution.py:480
  52.5 17.7 %all-to-all-start = ((f32[32,16,128]{2,1,0:T(8,128)}), f32[32,16,128]{2,1,0:T(8,128)S(1)}, u32[]{:S(2)}, u32[]{:S(2)}) async-start(f32[32,16,128]{2,1,0:T(8,128)} %get-tuple-element.20), calls=%async_computation | async-start | bytes 524288 | tf_op jit(solution)/shard_map/all_to_all | solution.py:556
  72.0 16.7 %all-to-all-start.2 = ((f32[32,16,128]{2,1,0:T(8,128)}), f32[32,16,128]{2,1,0:T(8,128)S(1)}, u32[]{:S(2)}, u32[]{:S(2)}) async-start(f32[32,16,128]{2,1,0:T(8,128)} %shard_map.137), calls=%async_computation.2 | async-start | bytes 524288 | tf_op jit(solution)/shard_map/all_to_all | solution.py:560
  77.1 1.6 %copy-start.1 = (bf16[128,128]{1,0:T(8,128)(2,1)S(1)}, bf16[128,128]{1,0:T(8,128)(2,1)}, u32[]{:S(2)}) copy-start(bf16[128,128]{1,0:T(8,128)(2,1)} %constant.32.clone.order_ref) | copy-start | bytes 98308
  77.1 1.6 %copy-start.2 = (bf16[128,128]{1,0:T(8,128)(2,1)S(1)}, bf16[128,128]{1,0:T(8,128)(2,1)}, u32[]{:S(2)}) copy-start(bf16[128,128]{1,0:T(8,128)(2,1)} %constant.33.clone.reverse_ref) | copy-start | bytes 98308
  91.6 15.5 %all-to-all-start.3 = ((f32[32,16,128]{2,1,0:T(8,128)}), f32[32,16,128]{2,1,0:T(8,128)S(1)}, u32[]{:S(2)}, u32[]{:S(2)}) async-start(f32[32,16,128]{2,1,0:T(8,128)} %shard_map.140), calls=%async_computation.3 | async-start | bytes 524288 | tf_op jit(solution)/shard_map/all_to_all | solution.py:564
  96.5 15.0 %collective-permute-start.6 = (f32[8,64,128]{2,1,0:T(8,128)}, f32[8,64,128]{2,1,0:T(8,128)S(1)}, u32[]{:S(2)}, u32[]{:S(2)}) collective-permute-start(f32[8,64,128]{2,1,0:T(8,128)} %get-tuple-element.22), channel_id=1, source_target_pairs={{0,1},{1,2},{2,3},{3,4},{4,5},{5,6},{6,7},{8,9},{9,10},{10,11},{11... | collective-permute-start | bytes 786440 | tf_op jit(solution)/shard_map/ppermute | solution.py:480
  103.5 13.9 %collective-permute-start.7 = (f32[8,64,128]{2,1,0:T(8,128)}, f32[8,64,128]{2,1,0:T(8,128)S(1)}, u32[]{:S(2)}, u32[]{:S(2)}) collective-permute-start(f32[8,64,128]{2,1,0:T(8,128)} %get-tuple-element.23), channel_id=1, source_target_pairs={{1,0},{2,1},{3,2},{4,3},{5,4},{6,5},{7,6},{9,8},{10,9},{11,10},{12... | collective-permute-start | bytes 786440 | tf_op jit(solution)/shard_map/ppermute | solution.py:480
  108.1 9.5 %all-to-all-start.4 = ((f32[4,64,128]{2,1,0:T(8,128)}), f32[4,64,128]{2,1,0:T(8,128)S(1)}, u32[]{:S(2)}, u32[]{:S(2)}) async-start(f32[4,64,128]{2,1,0:T(8,128)} %shard_map.142), calls=%async_computation.4 | async-start | bytes 262144 | tf_op jit(solution)/shard_map/all_to_all | solution.py:568
  111.5 6.2 %copy-start = (f32[64,128]{1,0:T(8,128)S(1)}, f32[64,128]{1,0:T(8,128)}, u32[]{:S(2)}) copy-start(f32[64,128]{1,0:T(8,128)} %measured_ref.3) | copy-start | bytes 98308
  119.2 17.2 %collective-permute-start.8 = (f32[2,8,64,128]{3,2,1,0:T(8,128)S(1)}, f32[2,8,64,128]{3,2,1,0:T(8,128)S(1)}, u32[]{:S(2)}, u32[]{:S(2)}) collective-permute-start(f32[2,8,64,128]{3,2,1,0:T(8,128)S(1)} %get-tuple-element.24.own_ref), channel_id=1, source_target_pairs={{0,8},{8,16},{16,24},{24,32},{32,40},{40,48},{48,56},{1,9},{9,17},... | collective-permute-start | bytes 1572872 | tf_op jit(solution)/shard_map/ppermute | solution.py:480
  130.3 10.5 %collective-permute-start.9 = (f32[2,8,64,128]{3,2,1,0:T(8,128)S(1)}, f32[2,8,64,128]{3,2,1,0:T(8,128)S(1)}, u32[]{:S(2)}, u32[]{:S(2)}) collective-permute-start(f32[2,8,64,128]{3,2,1,0:T(8,128)S(1)} %get-tuple-element.24.own_ref), channel_id=1, source_target_pairs={{8,0},{16,8},{24,16},{32,24},{40,32},{48,40},{56,48},{9,1},{17,9},... | collective-permute-start | bytes 1572872 | tf_op jit(solution)/shard_map/ppermute | solution.py:480
